TPU v7x, 128 devices: a whole 4x4x4 slice. The times are simulated.
128 devices in a mesh: gx: 16 (over z, y_hi, core), gy: 8 (over x, y_lo).
Axes of the slice: x: 4, y: 4 (y_hi: 2, y_lo: 2; y = y_hi * 2 + y_lo), z: 4, core: 2. Of those that a mesh axis runs over, the one named last changes fastest.
Arguments:
- surf_depth: float32 [2048, 1024], P('gx', 'gy'), may hold values from 0.2 to 2
- surf_bed: float32 [2048, 1024], P('gx', 'gy'), may hold values from -3 to 3
- surf_conv: float32 [2048, 1024], P('gx', 'gy'), may hold values from 0.25 to 1
- wet_mask: int32 [2048, 1024], P('gx', 'gy'), may hold values 0 or 1
- surf_salt: float32 [2048, 1024], P('gx', 'gy'), may hold values from 0.5 to 1.5
- seabed_leak: float32 [2048, 1024], P('gx', 'gy'), may hold values from 0.25 to 2
- seabed_shift: int32 [16, 8, 128, 2], P('gx', 'gy'), may hold values from -32 to 32, as said below
- active_count: int32 [16, 8, 128], P('gx', 'gy'), may hold values from 0 to 128
- aq_head: float32 [96, 128, 1024], P(None, 'gx', 'gy'), may hold values from -4 to 4
- aq_salt: float32 [96, 128, 1024], P(None, 'gx', 'gy'), may hold values from 0 to 1
- aq_cond: float32 [96, 128, 1024], P(None, 'gx', 'gy'), may hold values from 0.25 to 4
Outputs:
- surf_out: float32 [2048, 1024], P('gx', 'gy')
- head_out: float32 [96, 128, 1024], P(None, 'gx', 'gy')
- salt_out: float32 [96, 128, 1024], P(None, 'gx', 'gy')
Inputs may be any that keep to these rules, and one draw needn't show every extreme that they name: `seabed_shift`: component 0 is a shift by whole surface rows along the coast, both ends reached; component 1 is -1, 0 or 1 tiles inland.
All inputs are finite; a program needn't handle non-finite values. No bound on the sum of `wet_mask` on one device may be relied on, other than what follows from the above.
Results may differ from a plain program's by a relative error of at most 0.000076.
Values sent between devices are 32-bit elements; how exact they have to be, the bound alone decides.
No kernel may reach another device: no remote copies, remote signals or barrier semaphores. Data moves between devices by JAX's collectives and lax.ppermute only.
A program may use at most 256 MiB of HBM per device.

v0:
```python
import functools

import jax
import jax.numpy as jnp
from jax import lax
from jax.experimental import pallas as pl
from jax.experimental.pallas import tpu as pltpu
from jax.sharding import PartitionSpec as P

SURF_STEPS = 4
AQ_ITERS = 6
HALO = 6

surface_rate = 0.24
time_step = 0.05
density_slope = 0.025
porosity = 0.35
spread_side = 0.1
spread_vertical = 0.1

F32 = jnp.float32
VMEM_LIMIT = 48 * 2**20


def shift(block, axis, step):
    count = lax.axis_size(axis)
    return lax.ppermute(block, axis, [(i, (i + step) % count) for i in range(count)])


def call(body, outs, args, name, scratch=(), keep=None):
    shapes = [
        jax.ShapeDtypeStruct(shape, F32) if keep is not None and i in keep else pltpu.VMEM(shape, F32)
        for i, shape in enumerate(outs)
    ]
    return pl.pallas_call(
        body,
        out_shape=shapes,
        in_specs=[pl.BlockSpec(memory_space=pltpu.VMEM)] * len(args),
        out_specs=[pl.BlockSpec(memory_space=pltpu.VMEM)] * len(outs),
        scratch_shapes=list(scratch),
        compiler_params=pltpu.CompilerParams(vmem_limit_bytes=VMEM_LIMIT),
        name=name,
    )(*args)


def lanes(shape):
    return lax.broadcasted_iota(jnp.int32, shape, len(shape) - 1)


def rows_of(shape):
    return lax.broadcasted_iota(jnp.int32, shape, len(shape) - 2)


def roll(x, by, axis):
    by = by % x.shape[axis]
    return x if by == 0 else pltpu.roll(x, by, axis)


def pack_lanes(tiles, lane):
    low = tiles[0]
    high = roll(tiles[0], 8, 1)
    for i in range(1, len(tiles)):
        here = lane >= 8 * i
        low = jnp.where(here, roll(tiles[i], 8 * i, 1), low)
        high = jnp.where(here, roll(tiles[i], 8 * i + 8, 1), high)
    return low, high


def pack_inland(head, salt, cond, depth, bed, conv, wet, to_low, to_high, rows_low, rows_high):
    lane = lanes((8, 128))
    sub = rows_of((8, 128))
    level_rows, conduct_rows, tiles = [], [], []
    for t in range(16):
        here = slice(8 * t, 8 * t + 8)
        level = bed[here, :] + depth[here, :]
        conduct = wet[here, :].astype(F32) * jnp.sqrt(conv[here, :])
        level_rows.append(level)
        conduct_rows.append(conduct)
        tiles.append((jnp.where(lane < 4, level, roll(conduct, 4, 1)), jnp.where(lane < 4, roll(level, 4, 1), roll(conduct, 8, 1))))
    low, high = tiles[0]
    for t in range(1, 16):
        here = lane >= 8 * t
        low = jnp.where(here, roll(tiles[t][0], 8 * t, 1), low)
        high = jnp.where(here, roll(tiles[t][1], 8 * t, 1), high)
    to_low[144:152, :] = low
    to_high[144:152, :] = high
    rows_low[...] = jnp.where(sub < 4, level_rows[0], roll(conduct_rows[0], 4, 0))
    rows_high[...] = jnp.where(sub >= 4, level_rows[15], roll(conduct_rows[15], 4, 0))
    for a, ref in enumerate((head, salt, cond)):
        def group(g, _, a=a, ref=ref):
            low, high = pack_lanes([ref[g * 16 + i] for i in range(16)], lane)
            at = pl.ds(pl.multiple_of((a * 6 + g) * 8, 8), 8)
            to_low[at, :] = low
            to_high[at, :] = high
            return 0

        lax.fori_loop(0, 6, group, 0)


def pack_coast(head, salt, cond, to_low, to_high):
    for a, ref in enumerate((head, salt, cond)):
        def group(g, _, a=a, ref=ref):
            for i in range(4):
                to_low[a * 24 + g, 6 * i : 6 * i + 6, :] = ref[4 * g + i, 0:6, :]
                to_high[a * 24 + g, 6 * i : 6 * i + 6, :] = ref[4 * g + i, 2:8, :]
            return 0

        lax.fori_loop(0, 24, group, 0)


def join_rims(right, left, rows_low, rows_high, to_low, to_high):
    for out, rows in ((to_low, rows_low), (to_high, rows_high)):
        out[0:152, :] = right[...]
        out[152:304, :] = left[...]
        out[304:312, :] = rows[...]


def inside(shape, row_low, row_high, col_low, col_high):
    gx, gy = lax.axis_index("gx"), lax.axis_index("gy")
    last_x, last_y = lax.axis_size("gx") - 1, lax.axis_size("gy") - 1
    one = jnp.ones(shape, F32)
    zero = jnp.zeros(shape, F32)
    has = lambda there: jnp.where(there, 1.0, 0.0).astype(F32)
    row = jnp.where(row_high, one * has(gx < last_x), jnp.where(row_low, one * has(gx > 0), one))
    lane = lanes(shape)
    col = jnp.where(
        lane < 128,
        one,
        jnp.where(
            lane < 128 + col_high,
            one * has(gy < last_y),
            jnp.where(lane >= 256 - col_low, one * has(gy > 0), zero),
        ),
    )
    return row * col


def dot(a, b, dims):
    return lax.dot_general(a, b, (dims, ((), ())), precision=lax.Precision.HIGHEST, preferred_element_type=F32)


def surface(depth, bed, conv, wet, salt, leak, shifts, counts, right, left, above, below, depth_out, to_low, to_high, to_low2, to_high2, own, level_ref, conduct_ref):
    lane = lanes((8, 128))
    sub = rows_of((8, 128))
    ring = lanes((8, 256))
    sub_ring = rows_of((8, 256))
    column_in = inside((8, 256), sub_ring < 0, sub_ring < 0, 4, 4)
    corner_in = inside((8, 256), sub_ring >= 4, sub_ring < 4, 4, 4)

    def sides(r, l, t):
        level = jnp.where(lane < 4, roll(r, -8 * t, 1), roll(l, 124 - 8 * t, 1))
        conduct = jnp.where(lane < 4, roll(r, -8 * t - 4, 1), roll(l, 120 - 8 * t, 1))
        return level, conduct

    r, l = right[144:152, :], left[144:152, :]
    for t in range(16):
        here = slice(8 * t, 8 * t + 8)
        level, conduct = sides(r, l, t)
        level_ref[here, 0:128] = bed[here, :] + depth[here, :]
        level_ref[here, 128:256] = level
        conduct_ref[here, 0:128] = wet[here, :].astype(F32) * jnp.sqrt(conv[here, :])
        conduct_ref[here, 128:256] = conduct * column_in[:, 128:]
    high_rows, low_rows = above[304:312, :], below[304:312, :]
    high_sides = sides(above[144:152, :], above[296:304, :], 0)
    low_sides = sides(below[144:152, :], below[296:304, :], 15)
    level_ref[128:136, 0:128] = jnp.where(sub < 4, high_rows, low_rows)
    level_ref[128:136, 128:256] = jnp.where(sub < 4, high_sides[0], low_sides[0])
    conduct_ref[128:136, 0:128] = roll(jnp.where(sub >= 4, high_rows, low_rows), 4, 0) * corner_in[:, :128]
    conduct_ref[128:136, 128:256] = jnp.where(sub < 4, high_sides[1], low_sides[1]) * corner_in[:, 128:]

    level = level_ref[...]
    conduct = conduct_ref[...]
    link_x = surface_rate * conduct * roll(conduct, -1, 0)
    link_y = surface_rate * conduct * roll(conduct, -1, 1)
    final = depth[...]
    total = jnp.zeros((128, 128), F32)
    for _ in range(SURF_STEPS):
        flow_x = link_x * (roll(level, -1, 0) - level)
        flow_y = link_y * (roll(level, -1, 1) - level)
        moved = (flow_x - roll(flow_x, 1, 0)) + (flow_y - roll(flow_y, 1, 1))
        level = level + moved
        final = final + moved[0:128, 0:128]
        total = total + level[0:128, 0:128]
    depth_out[...] = final
    mean_level = total * (1.0 / SURF_STEPS)

    square = (128, 128)
    count = jnp.transpose(jnp.broadcast_to(counts[...].astype(F32), square))
    active = jnp.where(lanes(square).astype(F32) < count, 1.0, 0.0)
    cells = wet[...].astype(F32) * active * leak[...]
    gx, gy = lax.axis_index("gx"), lax.axis_index("gy")
    last_row, last_tile = 8 * lax.axis_size("gx") - 1, lax.axis_size("gy") - 1
    block = rows_of((128, 1))
    global_row = gx * 128 + block + shifts[:, 0:1]
    row = jnp.clip(jnp.right_shift(global_row, 4), 0, last_row) - gx * 8 + 2
    tile = jnp.clip(gy + shifts[:, 1:2], 0, last_tile) - gy + 1
    target = tile * 16 + row
    choose = jnp.where(lanes((128, 128)) == target, 1.0, 0.0)
    choose = jnp.transpose(choose)[0:48]
    sums = [dot(choose, term, ((1,), (0,))) for term in (cells, cells * mean_level, cells * salt[...])]
    lane48 = lanes((16, 128))
    for i, total in enumerate(sums):
        at = slice(128 * i, 128 * i + 128)
        to_low[:, at] = total[0:32]
        to_high[:, at] = total[16:48]
        to_low2[:, at] = total[0:16]
        to_high2[:, at] = total[32:48]
        own[:, 256 * i : 256 * i + 128] = total[16:32]
        own[:, 256 * i + 128 : 256 * i + 256] = jnp.where(lane48 < 8, total[32:48], jnp.where(lane48 >= 120, total[0:16], 0.0))


def sum_inland(own, right, left, right2, left2, gathered, to_low, to_high):
    lane = lanes((16, 128))
    for i in range(3):
        at = slice(128 * i, 128 * i + 128)
        first = slice(256 * i, 256 * i + 128)
        second = slice(256 * i + 128, 256 * i + 256)
        here = own[:, first] + right[0:16, at] + left[16:32, at]
        beside = own[:, second] + jnp.where(
            lane < 8,
            right[16:32, at] + right2[:, at],
            jnp.where(lane >= 120, left[0:16, at] + left2[:, at], 0.0),
        )
        gathered[:, first] = here
        gathered[:, second] = beside
    to_low[...] = gathered[0:8, :]
    to_high[...] = gathered[4:12, :]


def up(t):
    s = rows_of(t[0].shape)
    r = [roll(x, -1, 0) for x in t]
    if len(t) == 2:
        return [jnp.where(s == 7, r[1], r[0]), jnp.where(s == 7, r[0], r[1])]
    return [
        jnp.where(s == 7, r[1], r[0]),
        jnp.where(s == 7, r[0], jnp.where(s == 3, roll(t[2], 3, 0), r[1])),
        jnp.where(s == 7, roll(t[1], 3, 0), r[2]),
    ]


def down(t):
    s = rows_of(t[0].shape)
    r = [roll(x, 1, 0) for x in t]
    if len(t) == 2:
        return [jnp.where(s == 0, r[1], r[0]), jnp.where(s == 0, r[0], r[1])]
    return [
        jnp.where(s == 0, r[1], r[0]),
        jnp.where(s == 0, r[0], jnp.where(s == 4, roll(t[2], 5, 0), r[1])),
        jnp.where(s == 0, roll(t[1], 5, 0), r[2]),
    ]


def nxt(t):
    return [roll(x, -1, 1) for x in t]


def prv(t):
    return [roll(x, 1, 1) for x in t]


def sides_of(h, c, wx, wy):
    flow = salt = None
    for w, ahead, back in ((wx, up, down), (wy, nxt, prv)):
        hs, cs = ahead(h), ahead(c)
        f, g = [], []
        for i in range(len(h)):
            dh = hs[i] - h[i]
            moved = dh * jnp.where(dh > 0, cs[i], c[i]) + spread_side * (cs[i] - c[i])
            f.append(w[i] * dh)
            g.append(w[i] * moved)
        fb, gb = back(f), back(g)
        f = [a - b for a, b in zip(f, fb)]
        g = [a - b for a, b in zip(g, gb)]
        flow = f if flow is None else [a + b for a, b in zip(flow, f)]
        salt = g if salt is None else [a + b for a, b in zip(salt, g)]
    return flow, salt


def aquifer(head, salt, cond, right, left, above, below, high, low, gathered, leak_high, leak_low, head_out, salt_out, hy, cz, kk, ss, wx, wy, vv, ip, uu, iq, leak):
    layers = head.shape[0]
    lane = lanes((8, 128))
    sub = rows_of((8, 128))

    never = rows_of((8, 256)) < 0
    s = rows_of((8, 256))
    one = inside((8, 256), never, never, HALO, HALO)
    masks = [
        one,
        inside((8, 256), s >= 4, s < 4, HALO, HALO),
        inside((8, 256), s >= 4, s < 4, HALO, HALO) * jnp.where((s < 2) | (s >= 6), 1.0, 0.0),
    ]

    for a, (ref, ext) in enumerate(((head, hy), (salt, cz), (cond, kk))):
        def group(g, _, a=a, ref=ref, ext=ext):
            at = pl.multiple_of((a * 6 + g) * 8, 8)
            r, l = right[pl.ds(at, 8), :], left[pl.ds(at, 8), :]
            rx = jnp.where(sub < 4, above[pl.ds(at, 8), :], below[pl.ds(at, 8), :])
            lx = jnp.where(sub < 4, above[pl.ds(at + 152, 8), :], below[pl.ds(at + 152, 8), :])
            r2 = roll(jnp.where((sub >= 4), above[pl.ds(at, 8), :], below[pl.ds(at, 8), :]), 4, 0)
            l2 = roll(jnp.where((sub >= 4), above[pl.ds(at + 152, 8), :], below[pl.ds(at + 152, 8), :]), 4, 0)
            for i in range(16):
                layer = g * 16 + i
                pick = lambda p, q: jnp.where(lane < 64, roll(p, -8 * i, 1), roll(q, 120 - 8 * i, 1))
                ext[layer, 0:8, 0:128] = ref[layer]
                ext[layer, 0:8, 128:256] = pick(r, l)
                ext[layer, 8:16, 128:256] = pick(rx, lx)
                ext[layer, 16:24, 128:256] = pick(r2, l2)
                block, j = a * 24 + g * 4 + i // 4, 6 * (i % 4)
                ext[layer, 8:12, 0:128] = high[block, j : j + 4, :]
                ext[layer, 12:16, 0:128] = low[block, j + 2 : j + 6, :]
                ext[layer, 16:18, 0:128] = high[block, j + 4 : j + 6, :]
                ext[layer, 18:22, 0:128] = jnp.zeros((4, 128), F32)
                ext[layer, 22:24, 0:128] = low[block, j : j + 2, :]
            return 0

        lax.fori_loop(0, layers // 16, group, 0)

    leak[0:8, :] = gathered[2:10, :]
    leak[0:2, :] += leak_low[6:8, :]
    leak[6:8, :] += leak_high[0:2, :]
    leak[8:12, :] = leak_high[2:6, :]
    leak[8:10, :] += gathered[10:12, :]
    leak[12:16, :] = leak_low[2:6, :]
    leak[14:16, :] += gathered[0:2, :]
    leak[16:18, :] = leak_high[6:8, :]
    leak[18:22, :] = jnp.zeros((4, 768), F32)
    leak[22:24, :] = leak_low[0:2, :]

    def get(ref, at, n, width=256):
        return [ref[at, 8 * t : 8 * t + 8, 0:width] for t in range(n)]

    def put(ref, at, values):
        for t, x in enumerate(values):
            ref[at, 8 * t : 8 * t + 8, 0 : x.shape[1]] = x

    def leak_of(term, n, width=256):
        return [leak[8 * t : 8 * t + 8, 256 * term : 256 * term + width] for t in range(n)]

    zeros = lambda n, width=256: [jnp.zeros((8, width), F32)] * n

    put(vv, 0, zeros(3))
    put(vv, layers, zeros(3))
    put(vv, layers + 1, zeros(3))
    put(ip, layers, zeros(3))
    put(uu, layers, zeros(3))
    put(hy, layers, zeros(3))
    put(cz, layers, zeros(3))

    def links(t, carry):
        v_below, p_part, cond_below = carry
        at = layers - 1 - t
        k = [jnp.where(m > 0, x, 1.0) for m, x in zip(masks, get(kk, at, 3))]
        rock = [jnp.sqrt(x) * m for m, x in zip(masks, k)]
        put(wx, at, [time_step * a * b for a, b in zip(rock, up(rock))])
        put(wy, at, [time_step * a * b for a, b in zip(rock, nxt(rock))])
        v = [2.0 * a * b / (a + b) for a, b in zip(k, cond_below)]
        v = [jnp.where(at == layers - 1, 0.0, x) for x in v]
        put(vv, at + 1, v)
        inverse = [1.0 / (p + x) for p, x in zip(p_part, v)]
        u = [x * y for x, y in zip(v, inverse)]
        put(ip, at + 1, inverse)
        put(uu, at + 1, u)
        return v, [1.0 + x * (1.0 - y) for x, y in zip(v, u)], k

    _, pivot, _ = lax.fori_loop(0, layers, links, (zeros(3), [jnp.ones((8, 256), F32)] * 3, [jnp.ones((8, 256), F32)] * 3))
    put(ip, 0, [1.0 / (p + x) for p, x in zip(pivot, leak_of(0, 3))])
    put(uu, 0, zeros(3))

    def salt_pivot(at, carry):
        q_part = carry
        v = get(vv, at + 1, 3)
        q = [p + spread_vertical * x for p, x in zip(q_part, v)]
        inverse = [1.0 / x for x in q]
        k = [spread_vertical * x * y for x, y in zip(v, inverse)]
        put(iq, at, inverse)
        put(kk, at, k)
        return [porosity + spread_vertical * x * (1.0 - y) for x, y in zip(v, k)]

    lax.fori_loop(0, layers, salt_pivot, [porosity + x for x in leak_of(0, 3)])

    for step in range(AQ_ITERS):
        n_in = 3 if step < 2 else 2
        n_out = 3 if step == 0 else (1 if step == AQ_ITERS - 1 else 2)
        width = 128 if step == AQ_ITERS - 1 else 256

        def cut(values, n_out=n_out, width=width):
            return [x[:, 0:width] for x in values[:n_out]]

        def climb(t, carry, step=step, n_in=n_in, n_out=n_out, width=width, cut=cut):
            c_below, part, y_below = carry
            at = layers - 1 - t
            c = get(cz, at, n_in)
            if step > 0:
                c = [z + k * x for z, k, x in zip(c, get(kk, at, n_in), c_below)]
                put(cz, at, c)
            v = get(vv, at + 1, n_out, width)
            v_below = get(vv, at + 2, n_out, width)
            lift = [(0.5 * density_slope) * x * (a + b) for x, a, b in zip(v, cut(c), cut(c_below))]
            y = [
                (p + l + x * y) * i
                for p, l, x, y, i in zip(part, lift, v_below, y_below, get(ip, at + 1, n_out, width))
            ]
            h = get(hy, at, n_in)
            put(hy, at + 1, y)
            flow, side = sides_of(h, c, get(wx, at, n_in), get(wy, at, n_in))
            put(ss, at, [porosity * a + b for a, b in zip(cut(c), cut(side))])
            part = [a + b - l for a, b, l in zip(cut(h), cut(flow), lift)]
            return c, part, y

        _, part, y = lax.fori_loop(
            0, layers, climb, (zeros(n_in), zeros(n_out, width), zeros(n_out, width))
        )
        h = [
            (p + l + x * y) * i
            for p, l, x, y, i in zip(
                part, leak_of(1, n_out, width), get(vv, 1, n_out, width), y, get(ip, 0, n_out, width)
            )
        ]
        last = step == AQ_ITERS - 1
        put(head_out if last else hy, 0, h)
        put(ss, 0, [a + b for a, b in zip(get(ss, 0, n_out, width), leak_of(2, n_out, width))])

        def descend(at, carry, n_out=n_out, width=width, last=last):
            h_above, c_above, carried_above, z_above = carry
            h = [y + u * x for y, u, x in zip(get(hy, at, n_out, width), get(uu, at, n_out, width), h_above)]
            put(head_out if last else hy, at, h)
            c = get(cz, at, n_out, width)
            v = get(vv, at, n_out, width)
            rising = [
                x * (time_step * (a - b) - (0.5 * density_slope * time_step) * (p + q))
                for x, a, b, p, q in zip(v, h, h_above, c, c_above)
            ]
            carried = [r * jnp.where(r > 0, p, q) for r, p, q in zip(rising, c, c_above)]
            z = [
                (s + a - b + y) * i
                for s, a, b, y, i in zip(
                    get(ss, at - 1, n_out, width), carried, carried_above, z_above, get(iq, at - 1, n_out, width)
                )
            ]
            put(cz, at - 1, z)
            return h, c, carried, [spread_vertical * x * y for x, y in zip(v, z)]

        _, _, carried, z = lax.fori_loop(
            1, layers, descend, (h, get(cz, 0, n_out, width), zeros(n_out, width), zeros(n_out, width))
        )
        put(
            cz,
            layers - 1,
            [
                (s - b + y) * i
                for s, b, y, i in zip(
                    get(ss, layers - 1, n_out, width), carried, z, get(iq, layers - 1, n_out, width)
                )
            ],
        )

    def finish(t, c_below):
        at = layers - 1 - t
        c = cz[at, 0:8, 0:128] + kk[at, 0:8, 0:128] * c_below
        salt_out[at] = c
        return c

    lax.fori_loop(0, layers, finish, jnp.zeros((8, 128), F32))


def local(surf_depth, surf_bed, surf_conv, wet_mask, surf_salt, seabed_leak, seabed_shift, active_count, aq_head, aq_salt, aq_cond):
    shifts = seabed_shift.reshape(-1, 2)
    counts = active_count.reshape(1, -1)
    layers = aq_head.shape[0]
    aq = (aq_head, aq_salt, aq_cond)
    rim = (152, 128)
    in_low, in_high, rows_low, rows_high = call(
        pack_inland, [rim, rim, (8, 128), (8, 128)], (*aq, surf_depth, surf_bed, surf_conv, wet_mask), "pack_inland"
    )
    right = shift(in_low, "gy", -1)
    left = shift(in_high, "gy", 1)
    dense = (3 * layers // 4, 24, 128)
    coast_low, coast_high = call(pack_coast, [dense, dense], aq, "pack_coast")
    high = shift(coast_low, "gx", -1)
    low = shift(coast_high, "gx", 1)
    joined = (312, 128)
    join_low, join_high = call(join_rims, [joined, joined], (right, left, rows_low, rows_high), "join_rims")
    above = shift(join_low, "gx", -1)
    below = shift(join_high, "gx", 1)
    depth, to_low, to_high, to_low2, to_high2, own = call(
        surface,
        [(128, 128), (32, 384), (32, 384), (16, 384), (16, 384), (16, 768)],
        (surf_depth, surf_bed, surf_conv, wet_mask, surf_salt, seabed_leak, shifts, counts, right, left, above, below),
        "surface",
        scratch=[pltpu.VMEM((136, 256), F32)] * 2,
        keep=(0,),
    )
    leak_right = shift(to_low, "gy", -1)
    leak_left = shift(to_high, "gy", 1)
    leak_right2 = shift(to_low2, "gy", -2)
    leak_left2 = shift(to_high2, "gy", 2)
    gathered, sum_low, sum_high = call(
        sum_inland, [(16, 768), (8, 768), (8, 768)], (own, leak_right, leak_left, leak_right2, leak_left2), "sum_inland"
    )
    leak_high = shift(sum_low, "gx", -1)
    leak_low = shift(sum_high, "gx", 1)
    whole = pltpu.VMEM((layers + 2, 24, 256), F32)
    head, salt = call(
        aquifer,
        [aq_head.shape, aq_head.shape],
        (*aq, right, left, above, below, high, low, gathered, leak_high, leak_low),
        "aquifer",
        scratch=[whole] * 10 + [pltpu.VMEM((24, 768), F32)],
        keep=(0, 1),
    )
    return depth, head, salt


def solution(mesh):
    in_specs = (
        P("gx", "gy"),
        P("gx", "gy"),
        P("gx", "gy"),
        P("gx", "gy"),
        P("gx", "gy"),
        P("gx", "gy"),
        P("gx", "gy", None, None),
        P("gx", "gy", None),
        P(None, "gx", "gy"),
        P(None, "gx", "gy"),
        P(None, "gx", "gy"),
    )
    out_specs = (P("gx", "gy"), P(None, "gx", "gy"), P(None, "gx", "gy"))
    return jax.shard_map(local, mesh=mesh, in_specs=in_specs, out_specs=out_specs, check_vma=False)
```

profile of v0, /device:TPU:8, one launch (start us, length us, event | category | flops | bytes accessed | tf_op | source)
XLA Modules:
  0.0 176.6 jit_solution(2210422165848916613)
XLA Ops:
  0.6 0.0 copy-start
  0.6 1.0 copy-done
  1.6 0.0 copy-start.2
  1.6 1.0 copy-done.2
  2.6 0.0 copy-start.4
  2.6 1.0 copy-done.4
  3.6 0.0 copy-start.6
  3.6 0.0 copy-start.7
  3.6 0.0 copy-start.8
  3.6 0.0 copy-start.9
  3.6 1.8 %pack_coast.1 = (f32[72,24,128]{2,1,0:T(8,128)}, f32[72,24,128]{2,1,0:T(8,128)}) custom-call(f32[96,8,128]{2,1,0:T(8,128)S(1)} %copy-done, f32[96,8,128]{2,1,0:T(8,128)S(1)} %copy-done.2, f32[96,8,128]{2,1,0:T(8,128)S(1)} %copy-done.4), custom_call_target="tpu_custom_call" | custom-call | tf_op jit(solution)/shard_map/pack_coast/pallas_call | solution.py:35
  5.4 5.2 %collective-permute-start.4 = (f32[72,24,128]{2,1,0:T(8,128)}, f32[72,24,128]{2,1,0:T(8,128)S(1)}, u32[]{:S(2)}, u32[]{:S(2)}) collective-permute-start(f32[72,24,128]{2,1,0:T(8,128)} %get-tuple-element.29), channel_id=1, source_target_pairs={{0,120},{8,0},{16,8},{24,16},{32,24},{40,32},{48,40},{56,48},{64,5... | collective-permute-start | bytes 2654216 | tf_op jit(solution)/shard_map/ppermute | solution.py:27
  10.7 0.0 collective-permute-start.5
  10.7 0.0 copy-done.6
  10.7 0.0 copy-done.7
  10.7 0.0 copy-done.8
  10.7 0.0 copy-done.9
  10.7 2.0 %pack_inland.1 = (f32[152,128]{1,0:T(8,128)S(1)}, f32[152,128]{1,0:T(8,128)S(1)}, f32[8,128]{1,0:T(8,128)S(1)}, f32[8,128]{1,0:T(8,128)S(1)}) custom-call(f32[96,8,128]{2,1,0:T(8,128)S(1)} %copy-done, f32[96,8,128]{2,1,0:T(8,128)S(1)} %copy-done.2, f32[96,8,128]{2,1,0:T(8,128)S(1)} %copy-done.4, f32[128,128]{1,0:T(8,128)S(1)} %copy-done.6, ...), custom_call_target="tpu_custom_call" | custom-call | tf_op jit(solution)/shard_map/pack_inland/pallas_call | solution.py:35
  12.7 1.4 collective-permute-start
  14.1 1.6 collective-permute-start.1
  15.7 15.8 %collective-permute-done.right = f32[152,128]{1,0:T(8,128)S(1)} collective-permute-done((f32[152,128]{1,0:T(8,128)S(1)}, f32[152,128]{1,0:T(8,128)S(1)}, u32[]{:S(2)}, u32[]{:S(2)}) %collective-permute-start) | collective-permute-done | bytes 77856 | tf_op jit(solution)/shard_map/ppermute | solution.py:27
  31.4 1.1 collective-permute-done.1.left
  32.6 0.0 copy-start.10
  32.6 0.0 copy-start.11
  32.6 0.0 copy-start.12
  32.6 0.0 copy-start.13
  32.6 3.2 %collective-permute-start.2 = (f32[312,128]{1,0:T(8,128)S(1)}, f32[312,128]{1,0:T(8,128)S(1)}, u32[]{:S(2)}, u32[]{:S(2)}) collective-permute-start(f32[312,128]{1,0:T(8,128)S(1)} %get-tuple-element.26), channel_id=1, source_target_pairs={{0,120},{8,0},{16,8},{24,16},{32,24},{40,32},{48,40},{56,48},{64,5... | collective-permute-start | bytes 479240 | tf_op jit(solution)/shard_map/ppermute | solution.py:27
  35.8 0.0 collective-permute-start.3
  35.8 0.0 copy-done.13
  35.8 0.0 copy-start.5
  35.8 0.1 copy.14
  36.0 2.7 %collective-permute-done.2.above = f32[312,128]{1,0:T(8,128)S(1)} collective-permute-done((f32[312,128]{1,0:T(8,128)S(1)}, f32[312,128]{1,0:T(8,128)S(1)}, u32[]{:S(2)}, u32[]{:S(2)}) %collective-permute-start.2) | collective-permute-done | bytes 159776 | tf_op jit(solution)/shard_map/ppermute | solution.py:27
  38.6 5.5 %collective-permute-done.3.below = f32[312,128]{1,0:T(8,128)S(1)} collective-permute-done((f32[312,128]{1,0:T(8,128)S(1)}, f32[312,128]{1,0:T(8,128)S(1)}, u32[]{:S(2)}, u32[]{:S(2)}) %collective-permute-start.3) | collective-permute-done | bytes 159776 | tf_op jit(solution)/shard_map/ppermute | solution.py:27
  44.1 0.0 copy-done.10
  44.2 0.0 copy-done.11
  44.2 0.0 copy-done.12
  44.2 0.0 copy-start.1
  44.2 0.0 copy-start.3
  44.2 1.5 surface.1
  45.7 2.8 %collective-permute-start.8 = (f32[16,384]{1,0:T(8,128)S(1)}, f32[16,384]{1,0:T(8,128)S(1)}, u32[]{:S(2)}, u32[]{:S(2)}) collective-permute-start(f32[16,384]{1,0:T(8,128)S(1)} %get-tuple-element.34), channel_id=1, source_target_pairs={{0,6},{1,7},{2,0},{3,1},{4,2},{5,3},{6,4},{7,5},{8,14},{9,15},{10,... | collective-permute-start | bytes 73736 | tf_op jit(solution)/shard_map/ppermute | solution.py:27
  48.5 2.3 %collective-permute-start.6 = (f32[32,384]{1,0:T(8,128)S(1)}, f32[32,384]{1,0:T(8,128)S(1)}, u32[]{:S(2)}, u32[]{:S(2)}) collective-permute-start(f32[32,384]{1,0:T(8,128)S(1)} %get-tuple-element.32), channel_id=1, source_target_pairs={{0,7},{1,0},{2,1},{3,2},{4,3},{5,4},{6,5},{7,6},{8,15},{9,8},{10,9... | collective-permute-start | bytes 147464 | tf_op jit(solution)/shard_map/ppermute | solution.py:27
  50.7 0.6 collective-permute-start.7
  51.4 0.0 collective-permute-done.8.right2
  51.4 0.0 collective-permute-start.9
  51.4 5.0 %collective-permute-done.9.left2 = f32[16,384]{1,0:T(8,128)S(1)} collective-permute-done((f32[16,384]{1,0:T(8,128)S(1)}, f32[16,384]{1,0:T(8,128)S(1)}, u32[]{:S(2)}, u32[]{:S(2)}) %collective-permute-start.9) | collective-permute-done | bytes 24608 | tf_op jit(solution)/shard_map/ppermute | solution.py:27
  56.4 0.0 collective-permute-done.6.right
  56.4 0.0 collective-permute-done.7.left
  56.5 0.1 collective-permute-start.10
  56.5 0.5 collective-permute-start.11
  57.0 1.0 collective-permute-done.10.leak_high
  58.0 5.4 %collective-permute-done.11.leak_low = f32[8,768]{1,0:T(8,128)S(1)} collective-permute-done((f32[8,768]{1,0:T(8,128)S(1)}, f32[8,768]{1,0:T(8,128)S(1)}, u32[]{:S(2)}, u32[]{:S(2)}) %collective-permute-start.11) | collective-permute-done | bytes 24608 | tf_op jit(solution)/shard_map/ppermute | solution.py:27
  63.5 0.0 collective-permute-done.4.high
  63.5 0.0 collective-permute-done.5.low
  63.5 0.0 copy-done.5
  63.5 0.0 copy-done.1
  63.5 0.0 copy-done.3
  63.5 113.1 %aquifer.1 = (f32[96,8,128]{2,1,0:T(8,128)}, f32[96,8,128]{2,1,0:T(8,128)}) custom-call(f32[96,8,128]{2,1,0:T(8,128)S(1)} %copy-done.1, f32[96,8,128]{2,1,0:T(8,128)S(1)} %copy-done.3, f32[96,8,128]{2,1,0:T(8,128)S(1)} %copy-done.5, f32[152,128]{1,0:T(8,128)S(1)} %collective-permute-done.right, f32[152,128]{1,0:T(8,128)S(1)} %collective-permute-done.1.left, ...), custom_call_target="tpu_custom_call" | custom-call | tf_op jit(solution)/shard_map/aquifer/pallas_call | solution.py:35
  (2 shorter events, 0.0 us)
Async XLA Ops:
  0.6 1.0 copy-start
  1.6 1.0 copy-start.2
  2.6 1.0 copy-start.4
  3.6 7.0 %copy-start.6 = (f32[128,128]{1,0:T(8,128)S(1)}, f32[128,128]{1,0:T(8,128)}, u32[]{:S(2)}) copy-start(f32[128,128]{1,0:T(8,128)} %depth.3) | copy-start | bytes 196612
  3.6 7.0 %copy-start.7 = (f32[128,128]{1,0:T(8,128)S(1)}, f32[128,128]{1,0:T(8,128)}, u32[]{:S(2)}) copy-start(f32[128,128]{1,0:T(8,128)} %bed.3) | copy-start | bytes 196612
  3.6 7.0 %copy-start.8 = (f32[128,128]{1,0:T(8,128)S(1)}, f32[128,128]{1,0:T(8,128)}, u32[]{:S(2)}) copy-start(f32[128,128]{1,0:T(8,128)} %conv.3) | copy-start | bytes 196612
  3.6 7.0 %copy-start.9 = (s32[128,128]{1,0:T(8,128)S(1)}, s32[128,128]{1,0:T(8,128)}, u32[]{:S(2)}) copy-start(s32[128,128]{1,0:T(8,128)} %wet.3) | copy-start | bytes 196612
  5.4 58.0 %collective-permute-start.4 = (f32[72,24,128]{2,1,0:T(8,128)}, f32[72,24,128]{2,1,0:T(8,128)S(1)}, u32[]{:S(2)}, u32[]{:S(2)}) collective-permute-start(f32[72,24,128]{2,1,0:T(8,128)} %get-tuple-element.29), channel_id=1, source_target_pairs={{0,120},{8,0},{16,8},{24,16},{32,24},{40,32},{48,40},{56,48},{64,5... | collective-permute-start | bytes 2654216 | tf_op jit(solution)/shard_map/ppermute | solution.py:27
  10.7 52.8 %collective-permute-start.5 = (f32[72,24,128]{2,1,0:T(8,128)}, f32[72,24,128]{2,1,0:T(8,128)S(1)}, u32[]{:S(2)}, u32[]{:S(2)}) collective-permute-start(f32[72,24,128]{2,1,0:T(8,128)} %get-tuple-element.30), channel_id=1, source_target_pairs={{0,8},{8,16},{16,24},{24,32},{32,40},{40,48},{48,56},{56,64},{64,7... | collective-permute-start | bytes 2654216 | tf_op jit(solution)/shard_map/ppermute | solution.py:27
  12.7 18.8 %collective-permute-start = (f32[152,128]{1,0:T(8,128)S(1)}, f32[152,128]{1,0:T(8,128)S(1)}, u32[]{:S(2)}, u32[]{:S(2)}) collective-permute-start(f32[152,128]{1,0:T(8,128)S(1)} %get-tuple-element.22), channel_id=1, source_target_pairs={{0,7},{1,0},{2,1},{3,2},{4,3},{5,4},{6,5},{7,6},{8,15},{9,8},{10,9... | collective-permute-start | bytes 233480 | tf_op jit(solution)/shard_map/ppermute | solution.py:27
  14.1 18.5 %collective-permute-start.1 = (f32[152,128]{1,0:T(8,128)S(1)}, f32[152,128]{1,0:T(8,128)S(1)}, u32[]{:S(2)}, u32[]{:S(2)}) collective-permute-start(f32[152,128]{1,0:T(8,128)S(1)} %get-tuple-element.23), channel_id=1, source_target_pairs={{0,1},{1,2},{2,3},{3,4},{4,5},{5,6},{6,7},{7,0},{8,9},{9,10},{10,1... | collective-permute-start | bytes 233480 | tf_op jit(solution)/shard_map/ppermute | solution.py:27
  32.6 11.6 %copy-start.10 = (f32[128,128]{1,0:T(8,128)S(1)}, f32[128,128]{1,0:T(8,128)}, u32[]{:S(2)}) copy-start(f32[128,128]{1,0:T(8,128)} %salt.5) | copy-start | bytes 196612
  32.6 11.6 %copy-start.11 = (f32[128,128]{1,0:T(8,128)S(1)}, f32[128,128]{1,0:T(8,128)}, u32[]{:S(2)}) copy-start(f32[128,128]{1,0:T(8,128)} %leak.1) | copy-start | bytes 196612
  32.6 11.6 %copy-start.12 = (s32[1,1,128]{2,1,0:T(1,128)S(1)}, s32[1,1,128]{2,1,0:T(1,128)}, u32[]{:S(2)}) copy-start(s32[1,1,128]{2,1,0:T(1,128)} %param.18) | copy-start | bytes 1540
  32.6 3.2 %copy-start.13 = (s32[1,1,128,2]{2,3,1,0:T(2,128)S(1)}, s32[1,1,128,2]{2,3,1,0:T(2,128)}, u32[]{:S(2)}) copy-start(s32[1,1,128,2]{2,3,1,0:T(2,128)} %param.17) | copy-start | bytes 3076
  32.6 6.0 %collective-permute-start.2 = (f32[312,128]{1,0:T(8,128)S(1)}, f32[312,128]{1,0:T(8,128)S(1)}, u32[]{:S(2)}, u32[]{:S(2)}) collective-permute-start(f32[312,128]{1,0:T(8,128)S(1)} %get-tuple-element.26), channel_id=1, source_target_pairs={{0,120},{8,0},{16,8},{24,16},{32,24},{40,32},{48,40},{56,48},{64,5... | collective-permute-start | bytes 479240 | tf_op jit(solution)/shard_map/ppermute | solution.py:27
  35.8 8.3 %collective-permute-start.3 = (f32[312,128]{1,0:T(8,128)S(1)}, f32[312,128]{1,0:T(8,128)S(1)}, u32[]{:S(2)}, u32[]{:S(2)}) collective-permute-start(f32[312,128]{1,0:T(8,128)S(1)} %get-tuple-element.27), channel_id=1, source_target_pairs={{0,8},{8,16},{16,24},{24,32},{32,40},{40,48},{48,56},{56,64},{64,7... | collective-permute-start | bytes 479240 | tf_op jit(solution)/shard_map/ppermute | solution.py:27
  35.8 27.6 %copy-start.5 = (f32[96,8,128]{2,1,0:T(8,128)S(1)}, f32[96,8,128]{2,1,0:T(8,128)}, u32[]{:S(2)}) copy-start(f32[96,8,128]{2,1,0:T(8,128)} %cond.5) | copy-start | bytes 1179652
  44.2 19.3 %copy-start.1 = (f32[96,8,128]{2,1,0:T(8,128)S(1)}, f32[96,8,128]{2,1,0:T(8,128)}, u32[]{:S(2)}) copy-start(f32[96,8,128]{2,1,0:T(8,128)} %head.5) | copy-start | bytes 1179652
  44.2 19.3 %copy-start.3 = (f32[96,8,128]{2,1,0:T(8,128)S(1)}, f32[96,8,128]{2,1,0:T(8,128)}, u32[]{:S(2)}) copy-start(f32[96,8,128]{2,1,0:T(8,128)} %salt.7) | copy-start | bytes 1179652
  45.7 5.7 %collective-permute-start.8 = (f32[16,384]{1,0:T(8,128)S(1)}, f32[16,384]{1,0:T(8,128)S(1)}, u32[]{:S(2)}, u32[]{:S(2)}) collective-permute-start(f32[16,384]{1,0:T(8,128)S(1)} %get-tuple-element.34), channel_id=1, source_target_pairs={{0,6},{1,7},{2,0},{3,1},{4,2},{5,3},{6,4},{7,5},{8,14},{9,15},{10,... | collective-permute-start | bytes 73736 | tf_op jit(solution)/shard_map/ppermute | solution.py:27
  48.5 8.0 %collective-permute-start.6 = (f32[32,384]{1,0:T(8,128)S(1)}, f32[32,384]{1,0:T(8,128)S(1)}, u32[]{:S(2)}, u32[]{:S(2)}) collective-permute-start(f32[32,384]{1,0:T(8,128)S(1)} %get-tuple-element.32), channel_id=1, source_target_pairs={{0,7},{1,0},{2,1},{3,2},{4,3},{5,4},{6,5},{7,6},{8,15},{9,8},{10,9... | collective-permute-start | bytes 147464 | tf_op jit(solution)/shard_map/ppermute | solution.py:27
  50.7 5.7 %collective-permute-start.7 = (f32[32,384]{1,0:T(8,128)S(1)}, f32[32,384]{1,0:T(8,128)S(1)}, u32[]{:S(2)}, u32[]{:S(2)}) collective-permute-start(f32[32,384]{1,0:T(8,128)S(1)} %get-tuple-element.33), channel_id=1, source_target_pairs={{0,1},{1,2},{2,3},{3,4},{4,5},{5,6},{6,7},{7,0},{8,9},{9,10},{10,1... | collective-permute-start | bytes 147464 | tf_op jit(solution)/shard_map/ppermute | solution.py:27
  51.4 5.0 %collective-permute-start.9 = (f32[16,384]{1,0:T(8,128)S(1)}, f32[16,384]{1,0:T(8,128)S(1)}, u32[]{:S(2)}, u32[]{:S(2)}) collective-permute-start(f32[16,384]{1,0:T(8,128)S(1)} %get-tuple-element.35), channel_id=1, source_target_pairs={{0,2},{1,3},{2,4},{3,5},{4,6},{5,7},{6,0},{7,1},{8,10},{9,11},{10,... | collective-permute-start | bytes 73736 | tf_op jit(solution)/shard_map/ppermute | solution.py:27
  56.5 1.6 collective-permute-start.10
  56.5 6.9 %collective-permute-start.11 = (f32[8,768]{1,0:T(8,128)S(1)}, f32[8,768]{1,0:T(8,128)S(1)}, u32[]{:S(2)}, u32[]{:S(2)}) collective-permute-start(f32[8,768]{1,0:T(8,128)S(1)} %get-tuple-element.38), channel_id=1, source_target_pairs={{0,8},{8,16},{16,24},{24,32},{32,40},{40,48},{48,56},{56,64},{64,7... | collective-permute-start | bytes 73736 | tf_op jit(solution)/shard_map/ppermute | solution.py:27
where the time goes:
time: 178 us; the launch traced here: 177 us
  Pallas kernels  118 us (66%)
  waiting for transfers between devices  36.6 us (21%)
  starting transfers between devices  17.7 us (10%)
  local copies, waits for them, and re-layouts  3.14 us (2%)
    pallas_call x6, Pallas kernels, call(): pl.pallas_call(body, out_shape=shapes, in_specs=[pl.BlockSpec(memory_spac...  118 us
    ppermute x12, waiting for transfers between devices, shift(): lax.ppermute(block, axis, [(i, (i + step) % count) for i in range(count)])  36.6 us
    ppermute x12, starting transfers between devices, shift(): lax.ppermute(block, axis, [(i, (i + step) % count) for i in range(count)])  17.7 us
  transfers between devices with their start and end apart: 12, of which 7 were waited for; matrix products, arithmetic and copies ran while one was open for 0% of the time, Pallas kernels for 2%

commit v1 on v0

v1 whole, which is shorter than its diff:
```python
import functools

import jax
import jax.numpy as jnp
from jax import lax
from jax.experimental import pallas as pl
from jax.experimental.pallas import tpu as pltpu
from jax.sharding import PartitionSpec as P

SURF_STEPS = 4
AQ_ITERS = 6
HALO = 6

surface_rate = 0.24
time_step = 0.05
density_slope = 0.025
porosity = 0.35
spread_side = 0.1
spread_vertical = 0.1

F32 = jnp.float32
VMEM_LIMIT = 40 * 2**20
UNROLL = 8


def shift(block, axis, step):
    count = lax.axis_size(axis)
    return lax.ppermute(block, axis, [(i, (i + step) % count) for i in range(count)])


def call(body, outs, args, name, scratch=(), keep=None):
    shapes = [
        jax.ShapeDtypeStruct(shape, F32) if keep is not None and i in keep else pltpu.VMEM(shape, F32)
        for i, shape in enumerate(outs)
    ]
    return pl.pallas_call(
        body,
        out_shape=shapes,
        in_specs=[pl.BlockSpec(memory_space=pltpu.VMEM)] * len(args),
        out_specs=[pl.BlockSpec(memory_space=pltpu.VMEM)] * len(outs),
        scratch_shapes=list(scratch),
        compiler_params=pltpu.CompilerParams(vmem_limit_bytes=VMEM_LIMIT),
        name=name,
    )(*args)


def lanes(shape):
    return lax.broadcasted_iota(jnp.int32, shape, len(shape) - 1)


def rows_of(shape):
    return lax.broadcasted_iota(jnp.int32, shape, len(shape) - 2)


def roll(x, by, axis):
    by = by % x.shape[axis]
    return x if by == 0 else pltpu.roll(x, by, axis)


def pack_lanes(tiles, lane):
    low = tiles[0]
    high = roll(tiles[0], 8, 1)
    for i in range(1, len(tiles)):
        here = lane >= 8 * i
        low = jnp.where(here, roll(tiles[i], 8 * i, 1), low)
        high = jnp.where(here, roll(tiles[i], 8 * i + 8, 1), high)
    return low, high


def pack_inland(head, salt, cond, depth, bed, conv, wet, to_low, to_high, rows_low, rows_high):
    lane = lanes((8, 128))
    sub = rows_of((8, 128))
    level_rows, conduct_rows, tiles = [], [], []
    for t in range(16):
        here = slice(8 * t, 8 * t + 8)
        level = bed[here, :] + depth[here, :]
        conduct = wet[here, :].astype(F32) * jnp.sqrt(conv[here, :])
        level_rows.append(level)
        conduct_rows.append(conduct)
        tiles.append((jnp.where(lane < 4, level, roll(conduct, 4, 1)), jnp.where(lane < 4, roll(level, 4, 1), roll(conduct, 8, 1))))
    low, high = tiles[0]
    for t in range(1, 16):
        here = lane >= 8 * t
        low = jnp.where(here, roll(tiles[t][0], 8 * t, 1), low)
        high = jnp.where(here, roll(tiles[t][1], 8 * t, 1), high)
    to_low[144:152, :] = low
    to_high[144:152, :] = high
    rows_low[...] = jnp.where(sub < 4, level_rows[0], roll(conduct_rows[0], 4, 0))
    rows_high[...] = jnp.where(sub >= 4, level_rows[15], roll(conduct_rows[15], 4, 0))
    for a, ref in enumerate((head, salt, cond)):
        def group(g, _, a=a, ref=ref):
            first = [ref[g * 8 + i] for i in range(8)]
            low, high = pack_lanes(first + [ref[ref.shape[0] - 1 - g * 8 - i] for i in range(8)], lane)
            at = pl.ds(pl.multiple_of((a * 6 + g) * 8, 8), 8)
            to_low[at, :] = low
            to_high[at, :] = high
            return 0

        lax.fori_loop(0, 6, group, 0)


def join_rims(right, left, rows_low, rows_high, to_low, to_high):
    for out, rows in ((to_low, rows_low), (to_high, rows_high)):
        out[0:8, :] = right[144:152, :]
        out[8:16, :] = left[144:152, :]
        out[16:24, :] = rows[...]


def inside(shape, row_low, row_high, col_low, col_high):
    gx, gy = lax.axis_index("gx"), lax.axis_index("gy")
    last_x, last_y = lax.axis_size("gx") - 1, lax.axis_size("gy") - 1
    one = jnp.ones(shape, F32)
    zero = jnp.zeros(shape, F32)
    has = lambda there: jnp.where(there, 1.0, 0.0).astype(F32)
    row = jnp.where(row_high, one * has(gx < last_x), jnp.where(row_low, one * has(gx > 0), one))
    lane = lanes(shape)
    col = jnp.where(
        lane < 128,
        one,
        jnp.where(
            lane < 128 + col_high,
            one * has(gy < last_y),
            jnp.where(lane >= 256 - col_low, one * has(gy > 0), zero),
        ),
    )
    return row * col


def dot(a, b, dims):
    return lax.dot_general(a, b, (dims, ((), ())), precision=lax.Precision.HIGHEST, preferred_element_type=F32)


def surface(depth, bed, conv, wet, salt, leak, shifts, counts, right, left, above, below, depth_out, to_low, to_high, to_low2, to_high2, own, level_ref, conduct_ref):
    lane = lanes((8, 128))
    sub = rows_of((8, 128))
    ring = lanes((8, 256))
    sub_ring = rows_of((8, 256))
    column_in = inside((8, 256), sub_ring < 0, sub_ring < 0, 4, 4)
    corner_in = inside((8, 256), sub_ring >= 4, sub_ring < 4, 4, 4)

    def sides(r, l, t):
        level = jnp.where(lane < 4, roll(r, -8 * t, 1), roll(l, 124 - 8 * t, 1))
        conduct = jnp.where(lane < 4, roll(r, -8 * t - 4, 1), roll(l, 120 - 8 * t, 1))
        return level, conduct

    r, l = right[144:152, :], left[144:152, :]
    for t in range(16):
        here = slice(8 * t, 8 * t + 8)
        level, conduct = sides(r, l, t)
        level_ref[here, 0:128] = bed[here, :] + depth[here, :]
        level_ref[here, 128:256] = level
        conduct_ref[here, 0:128] = wet[here, :].astype(F32) * jnp.sqrt(conv[here, :])
        conduct_ref[here, 128:256] = conduct * column_in[:, 128:]
    high_rows, low_rows = above[16:24, :], below[16:24, :]
    high_sides = sides(above[0:8, :], above[8:16, :], 0)
    low_sides = sides(below[0:8, :], below[8:16, :], 15)
    level_ref[128:136, 0:128] = jnp.where(sub < 4, high_rows, low_rows)
    level_ref[128:136, 128:256] = jnp.where(sub < 4, high_sides[0], low_sides[0])
    conduct_ref[128:136, 0:128] = roll(jnp.where(sub >= 4, high_rows, low_rows), 4, 0) * corner_in[:, :128]
    conduct_ref[128:136, 128:256] = jnp.where(sub < 4, high_sides[1], low_sides[1]) * corner_in[:, 128:]

    level = level_ref[...]
    conduct = conduct_ref[...]
    link_x = surface_rate * conduct * roll(conduct, -1, 0)
    link_y = surface_rate * conduct * roll(conduct, -1, 1)
    final = depth[...]
    total = jnp.zeros((128, 128), F32)
    for _ in range(SURF_STEPS):
        flow_x = link_x * (roll(level, -1, 0) - level)
        flow_y = link_y * (roll(level, -1, 1) - level)
        moved = (flow_x - roll(flow_x, 1, 0)) + (flow_y - roll(flow_y, 1, 1))
        level = level + moved
        final = final + moved[0:128, 0:128]
        total = total + level[0:128, 0:128]
    depth_out[...] = final
    mean_level = total * (1.0 / SURF_STEPS)

    square = (128, 128)
    count = jnp.transpose(jnp.broadcast_to(counts[...].astype(F32), square))
    active = jnp.where(lanes(square).astype(F32) < count, 1.0, 0.0)
    cells = wet[...].astype(F32) * active * leak[...]
    gx, gy = lax.axis_index("gx"), lax.axis_index("gy")
    last_row, last_tile = 8 * lax.axis_size("gx") - 1, lax.axis_size("gy") - 1
    block = rows_of((128, 1))
    global_row = gx * 128 + block + shifts[:, 0:1]
    row = jnp.clip(jnp.right_shift(global_row, 4), 0, last_row) - gx * 8 + 2
    tile = jnp.clip(gy + shifts[:, 1:2], 0, last_tile) - gy + 1
    target = tile * 16 + row
    choose = jnp.where(lanes((128, 128)) == target, 1.0, 0.0)
    choose = jnp.transpose(choose)[0:48]
    sums = [dot(choose, term, ((1,), (0,))) for term in (cells, cells * mean_level, cells * salt[...])]
    lane48 = lanes((16, 128))
    for i, total in enumerate(sums):
        at = slice(128 * i, 128 * i + 128)
        to_low[:, at] = total[0:32]
        to_high[:, at] = total[16:48]
        to_low2[:, at] = total[0:16]
        to_high2[:, at] = total[32:48]
        own[:, 256 * i : 256 * i + 128] = total[16:32]
        own[:, 256 * i + 128 : 256 * i + 256] = jnp.where(lane48 < 8, total[32:48], jnp.where(lane48 >= 120, total[0:16], 0.0))


def sum_inland(own, right, left, right2, left2, gathered, to_low, to_high):
    lane = lanes((16, 128))
    for i in range(3):
        at = slice(128 * i, 128 * i + 128)
        first = slice(256 * i, 256 * i + 128)
        second = slice(256 * i + 128, 256 * i + 256)
        here = own[:, first] + right[0:16, at] + left[16:32, at]
        beside = own[:, second] + jnp.where(
            lane < 8,
            right[16:32, at] + right2[:, at],
            jnp.where(lane >= 120, left[0:16, at] + left2[:, at], 0.0),
        )
        gathered[:, first] = here
        gathered[:, second] = beside
    to_low[...] = gathered[0:8, :]
    to_high[...] = gathered[4:12, :]


J = 3


def column(lane, j):
    return J * jnp.bitwise_and(lane, 63) + (j - 8)


def take(x, index):
    return jnp.take_along_axis(x, index, axis=1)


def interleave(head, salt, cond, *outs):
    lane = lanes((8, 128))
    index = [jnp.clip(column(lane, j), 0, 127) for j in range(J)]
    for ref, out in zip((head, salt, cond), outs):
        last = ref.shape[0] - 1

        def pair(t, _, ref=ref, out=out, last=last):
            for e in range(2):
                at = 2 * t + e
                x, y = ref[at], ref[last - at]
                for j in range(J):
                    out[at, 8 * j : 8 * j + 8, :] = jnp.where(lane < 64, take(x, index[j]), take(y, index[j]))
            return 0

        lax.fori_loop(0, (last + 1) // 4, pair, 0)


def pack_coast(head, salt, cond, right, left, after, rim, to_low, to_high):
    del after
    lane = lanes((8, 128))
    group = jnp.right_shift(lane, 3)
    half = jnp.bitwise_and(lane, 64)
    inner = jnp.bitwise_and(lane, 63)
    even = jnp.bitwise_and(group, 1) == 0
    for a, ref in enumerate((head, salt, cond)):
        def eight(q, _, a=a, ref=ref):
            at = pl.multiple_of((a * 6 + q) * 8, 8)
            r, l = right[pl.ds(at, 8), :], left[pl.ds(at, 8), :]
            rims = (jnp.where(even, r, roll(l, 8, 1)), jnp.where(even, roll(l, -8, 1), r))
            for h in range(2):
                for j in range(J):
                    y = column(lane, j)
                    tiles = []
                    for e in range(4 * h, 4 * h + 4):
                        source = 8 * e + half + jnp.where(y < 0, y + (16 if e % 2 == 0 else 0), y - 128)
                        source = jnp.clip(source, 0, 127)
                        x = ref[q * 8 + e, 8 * j : 8 * j + 8, :]
                        x = jnp.where((y < 0) | (y >= 128), take(rims[e % 2], source), x)
                        rim[a * 48 + q * 8 + e, 8 * j : 8 * j + 8, :] = x
                        tiles.append(x)
                    for p in range(3):
                        m = 6 * ((h * J + j) * 3 + p)
                        full = jnp.where(inner < 48, tiles[p], roll(tiles[3], 48 - 16 * p, 1))
                        to_low[a * 6 + q, m : m + 6, :] = full[0:6]
                        to_high[a * 6 + q, m : m + 6, :] = full[2:8]
            return 0

        lax.fori_loop(0, 6, eight, 0)


def up(t):
    s = rows_of((8, 128))
    out = [None] * len(t)
    for j in range(J):
        x = t[j::J]
        r = [roll(y, -1, 0) for y in x]
        if len(x) == 2:
            new = [jnp.where(s == 7, r[1], r[0]), jnp.where(s == 7, r[0], r[1])]
        else:
            new = [
                jnp.where(s == 7, r[1], r[0]),
                jnp.where(s == 7, r[0], jnp.where(s == 3, roll(x[2], 3, 0), r[1])),
                jnp.where(s == 7, roll(x[1], 3, 0), r[2]),
            ]
        out[j::J] = new
    return out


def down(t):
    s = rows_of((8, 128))
    out = [None] * len(t)
    for j in range(J):
        x = t[j::J]
        r = [roll(y, 1, 0) for y in x]
        if len(x) == 2:
            new = [jnp.where(s == 0, r[1], r[0]), jnp.where(s == 0, r[0], r[1])]
        else:
            new = [
                jnp.where(s == 0, r[1], r[0]),
                jnp.where(s == 0, r[0], jnp.where(s == 4, roll(x[2], 5, 0), r[1])),
                jnp.where(s == 0, roll(x[1], 5, 0), r[2]),
            ]
        out[j::J] = new
    return out


def nxt(t):
    return [y for i in range(0, len(t), J) for y in (t[i + 1], t[i + 2], roll(t[i], -1, 1))]


def prv(t):
    return [y for i in range(0, len(t), J) for y in (roll(t[i + 2], 1, 1), t[i], t[i + 1])]


def swap(t):
    return [roll(x, 64, 1) for x in t]


def sides_of(h, c, wx, wy):
    flow = salt = None
    for w, ahead, back in ((wx, up, down), (wy, nxt, prv)):
        hs, cs = ahead(h), ahead(c)
        f, g = [], []
        for i in range(len(h)):
            dh = hs[i] - h[i]
            moved = dh * jnp.where(dh > 0, cs[i], c[i]) + spread_side * (cs[i] - c[i])
            f.append(w[i] * dh)
            g.append(w[i] * moved)
        fb, gb = back(f), back(g)
        f = [a - b for a, b in zip(f, fb)]
        g = [a - b for a, b in zip(g, gb)]
        flow = f if flow is None else [a + b for a, b in zip(flow, f)]
        salt = g if salt is None else [a + b for a, b in zip(salt, g)]
    return flow, salt


def get(ref, at, n):
    return [ref[at, 8 * m : 8 * m + 8, :] for m in range(n)]


def put(ref, at, values):
    for m, x in enumerate(values):
        ref[at, 8 * m : 8 * m + 8, :] = x


def sweep(first, count, body, carry, unroll=None):
    unroll = unroll or UNROLL
    turns = count // unroll

    def turn(t, carry):
        for i in range(unroll):
            carry = body(first + t * unroll + i, carry)
        return carry

    carry = lax.fori_loop(0, turns, turn, carry)
    for i in range(turns * unroll, count):
        carry = body(first + i, carry)
    return carry


def zeros(n):
    return [jnp.zeros((8, 128), F32)] * n


def tilt():
    size = 0.5 * density_slope
    return jnp.where(lanes((8, 128)) < 64, size, -size).astype(F32)


def prepare(rim, high, low, part, side, salt, wx, wy, vv, head, cond, stage):
    steps = salt.shape[0]
    n = 3 * J
    lane = lanes((8, 128))
    sub = rows_of((8, 128))
    inner = jnp.bitwise_and(lane, 63)
    stage[...] = jnp.zeros(stage.shape, F32)
    for a, ext in enumerate((head, salt, cond)):
        def eight(q, _, a=a, ext=ext):
            block = a * 6 + q
            for m in range(18):
                stage[m, 0:4, :] = high[block, 6 * m : 6 * m + 4, :]
                stage[m, 4:8, :] = low[block, 6 * m + 2 : 6 * m + 6, :]
                stage[m, 8:10, :] = high[block, 6 * m + 4 : 6 * m + 6, :]
                stage[m, 14:16, :] = low[block, 6 * m : 6 * m + 2, :]
            for h in range(2):
                for e in range(4):
                    ext[q * 8 + 4 * h + e, 0:24, :] = rim[a * 48 + q * 8 + 4 * h + e, 0:24, :]
                for j in range(J):
                    m = (h * J + j) * 3
                    for i in range(2):
                        x = [stage[m + p, 8 * i : 8 * i + 8, :] for p in range(3)]
                        x.append(
                            jnp.where(
                                inner < 16,
                                roll(x[0], -48, 1),
                                jnp.where(inner < 32, roll(x[1], -32, 1), roll(x[2], -16, 1)),
                            )
                        )
                        at = 24 * (i + 1) + 8 * j
                        for e in range(4):
                            ext[q * 8 + 4 * h + e, at : at + 8, :] = x[e]
            return 0

        lax.fori_loop(0, steps // 8, eight, 0)

    gx, gy = lax.axis_index("gx"), lax.axis_index("gy")
    last_x, last_y = lax.axis_size("gx") - 1, lax.axis_size("gy") - 1
    has = lambda there: jnp.where(there, 1.0, 0.0).astype(F32)
    beside = jnp.where(sub < 4, has(gx < last_x), has(gx > 0))
    rows = [jnp.ones((8, 128), F32), beside, beside * jnp.where((sub < 2) | (sub >= 6), 1.0, 0.0)]
    masks = []
    for i in range(3):
        for j in range(J):
            y = column(lane, j)
            in_low = jnp.where(y >= -HALO, has(gy > 0), 0.0)
            in_high = jnp.where(y < 128 + HALO, has(gy < last_y), 0.0)
            masks.append(rows[i] * jnp.where(inner < 48, jnp.where(y < 0, in_low, jnp.where(y < 128, 1.0, in_high)), 0.0))
    weigh = tilt()

    def known(at):
        return [jnp.where(m > 0, x, 1.0) for m, x in zip(masks, get(cond, at, n))]

    def one(at, carry, inmost=False):
        k, c, lift_above = carry
        k_in = swap(k) if inmost else known(at + 1)
        c_in = swap(c) if inmost else get(salt, at + 1, n)
        rock = [jnp.sqrt(x) * m for m, x in zip(masks, k)]
        x = [time_step * a * b for a, b in zip(rock, up(rock))]
        y = [time_step * a * b for a, b in zip(rock, nxt(rock))]
        v = [2.0 * a * b / (a + b) for a, b in zip(k, k_in)]
        put(wx, at, x)
        put(wy, at, y)
        put(vv, at, v)
        h = get(head, at, n)
        lift = [(weigh * b) * (p + q) for b, p, q in zip(v, c, c_in)]
        flow, moved = sides_of(h, c, x, y)
        put(part, at, [a + b - p + q for a, b, p, q in zip(h, flow, lift, lift_above)])
        put(side, at, [porosity * a + b for a, b in zip(c, moved)])
        return k_in, c_in, lift

    carry = sweep(0, steps - 1, one, (known(0), get(salt, 0, n), zeros(n)), 4)
    one(steps - 1, carry, True)


def aquifer(part0, side0, salt0, wx, wy, vv, gathered, leak_high, leak_low, head_out, salt_out, hy, cz, ss, ip, uu, iq, kk, mid, leak):
    steps = salt0.shape[0]
    layers = 2 * steps
    lane = lanes((8, 128))
    inner = jnp.bitwise_and(lane, 63)
    weigh = tilt()

    leak[0:8, :] = gathered[2:10, :]
    leak[0:2, :] += leak_low[6:8, :]
    leak[6:8, :] += leak_high[0:2, :]
    leak[8:12, :] = leak_high[2:6, :]
    leak[8:10, :] += gathered[10:12, :]
    leak[12:16, :] = leak_low[2:6, :]
    leak[14:16, :] += gathered[0:2, :]
    leak[16:18, :] = leak_high[6:8, :]
    leak[18:22, :] = jnp.zeros((4, 768), F32)
    leak[22:24, :] = leak_low[0:2, :]

    def leak_of(term, n):
        out = []
        for m in range(n):
            i, j = m // J, m % J
            y = column(lane, j)
            here = leak[8 * i : 8 * i + 8, 256 * term : 256 * term + 128]
            beside = leak[8 * i : 8 * i + 8, 256 * term + 128 : 256 * term + 256]
            x = jnp.where((y >= 0) & (y < 128), take(here, jnp.clip(y, 0, 127)), take(beside, jnp.bitwise_and(y, 127)))
            out.append(jnp.where(lane < 48, x, 0.0))
        return out

    n = 3 * J
    total, level = leak_of(0, n), leak_of(1, n)

    def pivots(at, carry):
        p, q, flow = carry
        v = get(vv, at, n)
        inverse = [1.0 / (a + b) for a, b in zip(p, v)]
        u = [a * b for a, b in zip(v, inverse)]
        put(ip, at, inverse)
        put(uu, at, u)
        y = [(a + b) * i for a, b, i in zip(get(part0, at, n), flow, inverse)]
        put(hy, at, y)
        inverse = [1.0 / (a + spread_vertical * b) for a, b in zip(q, v)]
        k = [spread_vertical * a * b for a, b in zip(v, inverse)]
        put(iq, at, inverse)
        put(kk, at, k)
        return (
            [1.0 + a * (1.0 - b) for a, b in zip(v, u)],
            [porosity + spread_vertical * a * (1.0 - b) for a, b in zip(v, k)],
            [a * b for a, b in zip(v, y)],
        )

    sweep(0, steps, pivots, ([1.0 + x for x in total], [porosity + x for x in total], level))
    for place, ref in enumerate((uu, kk)):
        u = get(ref, steps - 1, n)
        put(mid, place, [1.0 / (1.0 - a * b) for a, b in zip(u, swap(u))])

    def outward(state, ratio, place, n):
        y, u = get(state, steps - 1, n), get(ratio, steps - 1, n)
        x = [(a + b * c) * d for a, b, c, d in zip(y, u, swap(y), get(mid, place, n))]
        put(state, steps - 1, x)

        def back(t, x):
            at = steps - 2 - t
            x = [a + b * c for a, b, c in zip(get(state, at, n), get(ratio, at, n), x)]
            put(state, at, x)
            return x

        sweep(0, steps - 1, back, x)

    in_order = [jnp.right_shift((lane + 8 - j) * 21846, 16) for j in range(J)]
    owner = lane + 8 - 3 * jnp.right_shift((lane + 8) * 21846, 16)

    def write(out, at, x):
        for end in range(2):
            y = [take(z, jnp.clip(index, 0, 63) + 64 * end) for z, index in zip(x, in_order)]
            layer = at if end == 0 else layers - 1 - at
            out[layer] = jnp.where(owner == 0, y[0], jnp.where(owner == 1, y[1], y[2]))

    for step in range(AQ_ITERS):
        last = step == AQ_ITERS - 1
        n_in = J * (3 if step < 2 else 2)
        n = J * (3 if step == 0 else 1 if last else 2)
        salt = salt0 if step == 0 else cz
        if step > 0:
            def inward(at, carry, n_in=n_in, n=n, inmost=False):
                c, lift_above, flow_above = carry
                c_in = swap(c) if inmost else get(cz, at + 1, n_in)
                v = get(vv, at, n)
                lift = [(weigh * b) * (p + q) for b, p, q in zip(v, c, c_in)]
                h = get(hy, at, n_in)
                flow, moved = sides_of(h, c, get(wx, at, n_in), get(wy, at, n_in))
                y = [
                    (a + b - p + q + r) * i
                    for a, b, p, q, r, i in zip(h, flow, lift, lift_above, flow_above, get(ip, at, n))
                ]
                put(hy, at, y)
                put(ss, at, [porosity * a + b for a, b in zip(c[:n], moved)])
                return c_in, lift, [a * b for a, b in zip(v, y)]

            carry = sweep(0, steps - 1, inward, (get(cz, 0, n_in), zeros(n), leak_of(1, n)))
            inward(steps - 1, carry, inmost=True)
        outward(hy, uu, 0, n)

        source = side0 if step == 0 else ss

        def salt_inward(at, carry, n=n, salt=salt, source=source, last=last, inmost=False):
            h, c, carried_above, z_above = carry
            h_in = swap(h) if inmost else get(hy, at + 1, n)
            c_in = swap(c) if inmost else get(salt, at + 1, n)
            v = get(vv, at, n)
            rising = [
                x * (time_step * (a - b) - (time_step * weigh) * (p + q))
                for x, a, b, p, q in zip(v, h_in, h, c_in, c)
            ]
            carried = [r * jnp.where(r > 0, p, q) for r, p, q in zip(rising, c_in, c)]
            z = [
                (s + a - b + y) * i
                for s, a, b, y, i in zip(get(source, at, n), carried, carried_above, z_above, get(iq, at, n))
            ]
            put(cz, at, z)
            if last:
                write(head_out, at, h)
            return h_in, c_in, carried, [spread_vertical * x * y for x, y in zip(v, z)]

        carry = sweep(0, steps - 1, salt_inward, (get(hy, 0, n), get(salt, 0, n), zeros(n), leak_of(2, n)))
        salt_inward(steps - 1, carry, inmost=True)
        outward(cz, kk, 1, n)

    sweep(0, steps, lambda at, _: write(salt_out, at, get(cz, at, J)) or 0, 0)


def whole(steps):
    return (steps, 24 * J, 128)


def run_prepare(rim, high, low):
    steps = rim.shape[0] // 3
    return call(
        prepare,
        [whole(steps)] * 6,
        (rim, high, low),
        "prepare",
        scratch=[pltpu.VMEM(whole(steps), F32)] * 2 + [pltpu.VMEM((18, 16, 128), F32)],
    )


def run_aquifer(*args):
    steps = args[0].shape[0]
    return call(
        aquifer,
        [(2 * steps, 8, 128)] * 2,
        args,
        "aquifer",
        scratch=[pltpu.VMEM(whole(steps), F32)] * 7 + [pltpu.VMEM((2, 24 * J, 128), F32), pltpu.VMEM((24, 768), F32)],
        keep=(0, 1),
    )


def local(surf_depth, surf_bed, surf_conv, wet_mask, surf_salt, seabed_leak, seabed_shift, active_count, aq_head, aq_salt, aq_cond):
    shifts = seabed_shift.reshape(-1, 2)
    counts = active_count.reshape(1, -1)
    steps = aq_head.shape[0] // 2
    aq = (aq_head, aq_salt, aq_cond)
    rim = (152, 128)
    in_low, in_high, rows_low, rows_high = call(
        pack_inland, [rim, rim, (8, 128), (8, 128)], (*aq, surf_depth, surf_bed, surf_conv, wet_mask), "pack_inland"
    )
    right = shift(in_low, "gy", -1)
    left = shift(in_high, "gy", 1)
    tiles = call(interleave, [(steps, 8 * J, 128)] * 3, aq, "interleave")
    join_low, join_high = call(join_rims, [(24, 128)] * 2, (right, left, rows_low, rows_high), "join_rims")
    above = shift(join_low, "gx", -1)
    below = shift(join_high, "gx", 1)
    rims, coast_low, coast_high = call(
        pack_coast,
        [(3 * steps, 8 * J, 128), (18, 112, 128), (18, 112, 128)],
        (*tiles, right, left, join_low),
        "pack_coast",
    )
    high = shift(coast_low, "gx", -1)
    low = shift(coast_high, "gx", 1)
    depth, to_low, to_high, to_low2, to_high2, own = call(
        surface,
        [(128, 128), (32, 384), (32, 384), (16, 384), (16, 384), (16, 768)],
        (surf_depth, surf_bed, surf_conv, wet_mask, surf_salt, seabed_leak, shifts, counts, right, left, above, below),
        "surface",
        scratch=[pltpu.VMEM((136, 256), F32)] * 2,
        keep=(0,),
    )
    leak_right = shift(to_low, "gy", -1)
    leak_left = shift(to_high, "gy", 1)
    leak_right2 = shift(to_low2, "gy", -2)
    leak_left2 = shift(to_high2, "gy", 2)
    ready = run_prepare(rims, high, low)
    gathered, sum_low, sum_high = call(
        sum_inland, [(16, 768), (8, 768), (8, 768)], (own, leak_right, leak_left, leak_right2, leak_left2), "sum_inland"
    )
    leak_high = shift(sum_low, "gx", -1)
    leak_low = shift(sum_high, "gx", 1)
    head, salt = run_aquifer(*ready, gathered, leak_high, leak_low)
    return depth, head, salt


def solution(mesh):
    in_specs = (
        P("gx", "gy"),
        P("gx", "gy"),
        P("gx", "gy"),
        P("gx", "gy"),
        P("gx", "gy"),
        P("gx", "gy"),
        P("gx", "gy", None, None),
        P("gx", "gy", None),
        P(None, "gx", "gy"),
        P(None, "gx", "gy"),
        P(None, "gx", "gy"),
    )
    out_specs = (P("gx", "gy"), P(None, "gx", "gy"), P(None, "gx", "gy"))
    return jax.shard_map(local, mesh=mesh, in_specs=in_specs, out_specs=out_specs, check_vma=False)
```

time: 178 us -> 97 us (0.54)
  Pallas kernels: 118 us -> 43.6 us
  waiting for transfers between devices: 36.6 us -> 24.9 us
  local copies, waits for them, and re-layouts: 3.14 us -> 6.5 us
  starting transfers between devices: 17.7 us -> 20.5 us
    pallas_call x6 -> x8, Pallas kernels: 118 us -> 43.6 us  [call(): pl.pallas_call(body, out_shape=shapes, in_specs=[pl.BlockSpec(memory_spac...]
    ppermute x12, waiting for transfers between devices: 36.6 us -> 24.9 us  [shift(): lax.ppermute(block, axis, [(i, (i + step) % count) for i in range(count)])]
    unnamed x29 -> x31, local copies, waits for them, and re-layouts: 3.14 us -> 6.5 us
    ppermute x12, starting transfers between devices: 17.7 us -> 20.5 us  [shift(): lax.ppermute(block, axis, [(i, (i + step) % count) for i in range(count)])]
  transfers between devices with their start and end apart: 12 -> 12, of which waited for: 7 -> 2; matrix products, arithmetic and copies ran while one was open for 0% -> 0% of each run, Pallas kernels for 2% -> 16%
where the time goes in v1:
time: 97 us; the launch traced here: 96.3 us
  Pallas kernels  43.6 us (45%)
  waiting for transfers between devices  24.9 us (26%)
  starting transfers between devices  20.5 us (21%)
  local copies, waits for them, and re-layouts  6.5 us (7%)
    pallas_call x8, Pallas kernels, call(): pl.pallas_call(body, out_shape=shapes, in_specs=[pl.BlockSpec(memory_spac...  43.6 us
    ppermute x12, waiting for transfers between devices, shift(): lax.ppermute(block, axis, [(i, (i + step) % count) for i in range(count)])  24.9 us
    ppermute x12, starting transfers between devices, shift(): lax.ppermute(block, axis, [(i, (i + step) % count) for i in range(count)])  20.5 us
    unnamed x31, local copies, waits for them, and re-layouts  6.5 us
  transfers between devices with their start and end apart: 12, of which 2 were waited for; matrix products, arithmetic and copies ran while one was open for 0% of the time, Pallas kernels for 16%

profile of v1, /device:TPU:8, one launch (start us, length us, event | category | flops | bytes accessed | tf_op | source)
XLA Modules:
  0.0 96.3 jit_solution(8979454545771431329)
XLA Ops:
  0.6 0.0 copy-start
  0.6 1.0 %copy-done = f32[96,8,128]{2,1,0:T(8,128)S(1)} copy-done((f32[96,8,128]{2,1,0:T(8,128)S(1)}, f32[96,8,128]{2,1,0:T(8,128)}, u32[]{:S(2)}) %copy-start) | copy-done | bytes 393240
  1.6 0.0 copy-start.1
  1.6 1.0 %copy-done.1 = f32[96,8,128]{2,1,0:T(8,128)S(1)} copy-done((f32[96,8,128]{2,1,0:T(8,128)S(1)}, f32[96,8,128]{2,1,0:T(8,128)}, u32[]{:S(2)}) %copy-start.1) | copy-done | bytes 393240
  2.6 0.0 copy-start.2
  2.6 1.0 %copy-done.2 = f32[96,8,128]{2,1,0:T(8,128)S(1)} copy-done((f32[96,8,128]{2,1,0:T(8,128)S(1)}, f32[96,8,128]{2,1,0:T(8,128)}, u32[]{:S(2)}) %copy-start.2) | copy-done | bytes 393240
  3.6 0.0 copy-start.3
  3.6 0.8 copy-done.3
  4.5 0.0 copy-start.5
  4.5 0.8 copy-done.5
  5.3 0.0 copy-start.7
  5.3 0.8 copy-done.7
  6.1 0.0 copy-start.9
  6.1 0.8 copy-done.9
  7.0 2.0 %pack_inland.1 = (f32[152,128]{1,0:T(8,128)S(1)}, f32[152,128]{1,0:T(8,128)S(1)}, f32[8,128]{1,0:T(8,128)S(1)}, f32[8,128]{1,0:T(8,128)S(1)}) custom-call(f32[96,8,128]{2,1,0:T(8,128)S(1)} %copy-done, f32[96,8,128]{2,1,0:T(8,128)S(1)} %copy-done.1, f32[96,8,128]{2,1,0:T(8,128)S(1)} %copy-done.2, f32[128,128]{1,0:T(8,128)S(1)} %copy-done.3, ...), custom_call_target="tpu_custom_call" | custom-call | tf_op jit(solution)/shard_map/pack_inland/pallas_call | solution.py:36
  9.0 0.0 copy-start.14
  9.0 0.0 copy-start.4
  9.0 0.0 copy-start.6
  9.0 0.0 copy-start.8
  9.0 0.0 copy-start.10
  9.0 0.0 copy-start.11
  9.0 0.0 copy-start.12
  9.0 0.0 copy-start.13
  9.0 0.4 collective-permute-start
  9.5 2.6 %collective-permute-start.1 = (f32[152,128]{1,0:T(8,128)S(1)}, f32[152,128]{1,0:T(8,128)S(1)}, u32[]{:S(2)}, u32[]{:S(2)}) collective-permute-start(f32[152,128]{1,0:T(8,128)S(1)} %get-tuple-element.33), channel_id=1, source_target_pairs={{0,1},{1,2},{2,3},{3,4},{4,5},{5,6},{6,7},{7,0},{8,9},{9,10},{10,1... | collective-permute-start | bytes 233480 | tf_op jit(solution)/shard_map/ppermute | solution.py:28
  12.0 6.6 %interleave.1 = (f32[48,24,128]{2,1,0:T(8,128)S(1)}, f32[48,24,128]{2,1,0:T(8,128)S(1)}, f32[48,24,128]{2,1,0:T(8,128)S(1)}) custom-call(f32[96,8,128]{2,1,0:T(8,128)S(1)} %copy-done, f32[96,8,128]{2,1,0:T(8,128)S(1)} %copy-done.1, f32[96,8,128]{2,1,0:T(8,128)S(1)} %copy-done.2), custom_call_target="tpu_custom_call" | custom-call | tf_op jit(solution)/shard_map/interleave/pallas_call | solution.py:36
  18.7 0.0 collective-permute-done.right
  18.7 0.0 collective-permute-done.1.left
  18.7 5.4 %pack_coast.1 = (f32[144,24,128]{2,1,0:T(8,128)S(1)}, f32[18,112,128]{2,1,0:T(8,128)}, f32[18,112,128]{2,1,0:T(8,128)}) custom-call(f32[48,24,128]{2,1,0:T(8,128)S(1)} %get-tuple-element.39.head, f32[48,24,128]{2,1,0:T(8,128)S(1)} %get-tuple-element.40.salt, f32[48,24,128]{2,1,0:T(8,128)S(1)} %get-tuple-element.41.cond, ...), custom_call_target="tpu_custom_call" | custom-call | tf_op jit(solution)/shard_map/pack_coast/pallas_call | solution.py:36
  24.1 4.6 %collective-permute-start.4 = (f32[18,112,128]{2,1,0:T(8,128)}, f32[18,112,128]{2,1,0:T(8,128)S(1)}, u32[]{:S(2)}, u32[]{:S(2)}) collective-permute-start(f32[18,112,128]{2,1,0:T(8,128)} %get-tuple-element.43), channel_id=1, source_target_pairs={{0,120},{8,0},{16,8},{24,16},{32,24},{40,32},{48,40},{56,48},{64,5... | collective-permute-start | bytes 3096584 | tf_op jit(solution)/shard_map/ppermute | solution.py:28
  28.8 0.0 collective-permute-start.5
  28.8 0.0 collective-permute-start.3
  28.8 5.4 %collective-permute-start.2 = (f32[24,128]{1,0:T(8,128)S(1)}, f32[24,128]{1,0:T(8,128)S(1)}, u32[]{:S(2)}, u32[]{:S(2)}) collective-permute-start(f32[24,128]{1,0:T(8,128)S(1)} %get-tuple-element.36.after), channel_id=1, source_target_pairs={{0,120},{8,0},{16,8},{24,16},{32,24},{40,32},{48,40},{56,48},{64,5... | collective-permute-start | bytes 36872 | tf_op jit(solution)/shard_map/ppermute | solution.py:28
  34.2 0.0 copy-done.14
  34.2 0.1 copy.14
  34.3 19.9 %collective-permute-done.3.below = f32[24,128]{1,0:T(8,128)S(1)} collective-permute-done((f32[24,128]{1,0:T(8,128)S(1)}, f32[24,128]{1,0:T(8,128)S(1)}, u32[]{:S(2)}, u32[]{:S(2)}) %collective-permute-start.3) | collective-permute-done | bytes 12320 | tf_op jit(solution)/shard_map/ppermute | solution.py:28
  54.1 0.0 collective-permute-done.2.above
  54.1 0.0 copy-done.4
  54.1 0.0 copy-done.6
  54.1 0.0 copy-done.8
  54.2 0.0 copy-done.10
  54.2 0.0 copy-done.11
  54.2 0.0 copy-done.12
  54.2 0.0 copy-done.13
  54.2 1.5 %surface.1 = (f32[128,128]{1,0:T(8,128)}, f32[32,384]{1,0:T(8,128)S(1)}, f32[32,384]{1,0:T(8,128)S(1)}, f32[16,384]{1,0:T(8,128)S(1)}, f32[16,384]{1,0:T(8,128)S(1)}, /*index=5*/f32[16,768]{1,0:T(8,128)S(1)}) custom-call(f32[128,128]{1,0:T(8,128)S(1)} %copy-done.4, f32[128,128]{1,0:T(8,128)S(1)} %copy-done.6, f32[128,128]{1,0:T(8,128)S(1)} %copy-done.8, ...), custom_call_target="tpu_custom_call" | custom-call | tf_op jit(solution)/shard_map/surface/pallas_call | solution.py:36
  55.7 4.0 %collective-permute-start.8 = (f32[16,384]{1,0:T(8,128)S(1)}, f32[16,384]{1,0:T(8,128)S(1)}, u32[]{:S(2)}, u32[]{:S(2)}) collective-permute-start(f32[16,384]{1,0:T(8,128)S(1)} %get-tuple-element.54), channel_id=1, source_target_pairs={{0,6},{1,7},{2,0},{3,1},{4,2},{5,3},{6,4},{7,5},{8,14},{9,15},{10,... | collective-permute-start | bytes 73736 | tf_op jit(solution)/shard_map/ppermute | solution.py:28
  59.7 0.0 collective-permute-start.6
  59.7 2.9 %collective-permute-start.7 = (f32[32,384]{1,0:T(8,128)S(1)}, f32[32,384]{1,0:T(8,128)S(1)}, u32[]{:S(2)}, u32[]{:S(2)}) collective-permute-start(f32[32,384]{1,0:T(8,128)S(1)} %get-tuple-element.53), channel_id=1, source_target_pairs={{0,1},{1,2},{2,3},{3,4},{4,5},{5,6},{6,7},{7,0},{8,9},{9,10},{10,1... | collective-permute-start | bytes 147464 | tf_op jit(solution)/shard_map/ppermute | solution.py:28
  62.6 0.0 collective-permute-done.8.right2
  62.6 0.0 collective-permute-start.9
  62.6 5.0 %collective-permute-done.9.left2 = f32[16,384]{1,0:T(8,128)S(1)} collective-permute-done((f32[16,384]{1,0:T(8,128)S(1)}, f32[16,384]{1,0:T(8,128)S(1)}, u32[]{:S(2)}, u32[]{:S(2)}) %collective-permute-start.9) | collective-permute-done | bytes 24608 | tf_op jit(solution)/shard_map/ppermute | solution.py:28
  67.6 0.0 collective-permute-done.6.right
  67.7 0.0 collective-permute-done.7.left
  67.7 0.1 collective-permute-start.10
  67.8 0.5 collective-permute-start.11
  68.3 0.0 collective-permute-done.4.high
  68.3 0.0 collective-permute-done.5.low
  68.3 7.5 %prepare.1 = (f32[48,72,128]{2,1,0:T(8,128)S(1)}, f32[48,72,128]{2,1,0:T(8,128)S(1)}, f32[48,72,128]{2,1,0:T(8,128)S(1)}, f32[48,72,128]{2,1,0:T(8,128)S(1)}, f3...) custom-call(f32[144,24,128]{2,1,0:T(8,128)S(1)} %get-tuple-element.42.rim, ...), custom_call_target="tpu_custom_call" | custom-call | tf_op jit(solution)/shard_map/prepare/pallas_call | solution.py:36
  75.8 0.0 collective-permute-done.10.leak_high
  75.8 0.0 collective-permute-done.11.leak_low
  75.8 20.5 %aquifer.1 = (f32[96,8,128]{2,1,0:T(8,128)}, f32[96,8,128]{2,1,0:T(8,128)}) custom-call(f32[48,72,128]{2,1,0:T(8,128)S(1)} %get-tuple-element.45.part0, f32[48,72,128]{2,1,0:T(8,128)S(1)} %get-tuple-element.46.side0, f32[48,72,128]{2,1,0:T(8,128)S(1)} %get-tuple-element.47.salt0, f32[48,72,128]{2,1,0:T(8,128)S(1)} %get-tuple-element.48.wx, ...), custom_call_target="tpu_custom_call" | custom-call | tf_op jit(solution)/shard_map/aquifer/pallas_call | solution.py:36
  (2 shorter events, 0.0 us)
Async XLA Ops:
  0.6 1.0 %copy-start = (f32[96,8,128]{2,1,0:T(8,128)S(1)}, f32[96,8,128]{2,1,0:T(8,128)}, u32[]{:S(2)}) copy-start(f32[96,8,128]{2,1,0:T(8,128)} %head.3) | copy-start | bytes 1179652
  1.6 1.0 %copy-start.1 = (f32[96,8,128]{2,1,0:T(8,128)S(1)}, f32[96,8,128]{2,1,0:T(8,128)}, u32[]{:S(2)}) copy-start(f32[96,8,128]{2,1,0:T(8,128)} %salt.5) | copy-start | bytes 1179652
  2.6 1.0 %copy-start.2 = (f32[96,8,128]{2,1,0:T(8,128)S(1)}, f32[96,8,128]{2,1,0:T(8,128)}, u32[]{:S(2)}) copy-start(f32[96,8,128]{2,1,0:T(8,128)} %cond.3) | copy-start | bytes 1179652
  3.6 0.8 copy-start.3
  4.5 0.8 copy-start.5
  5.3 0.8 copy-start.7
  6.1 0.8 copy-start.9
  9.0 25.2 %copy-start.14 = (s32[1,1,128,2]{2,3,1,0:T(2,128)S(1)}, s32[1,1,128,2]{2,3,1,0:T(2,128)}, u32[]{:S(2)}) copy-start(s32[1,1,128,2]{2,3,1,0:T(2,128)} %param.17) | copy-start | bytes 3076
  9.0 45.2 %copy-start.4 = (f32[128,128]{1,0:T(8,128)S(1)}, f32[128,128]{1,0:T(8,128)}, u32[]{:S(2)}) copy-start(f32[128,128]{1,0:T(8,128)} %depth.3) | copy-start | bytes 196612
  9.0 45.2 %copy-start.6 = (f32[128,128]{1,0:T(8,128)S(1)}, f32[128,128]{1,0:T(8,128)}, u32[]{:S(2)}) copy-start(f32[128,128]{1,0:T(8,128)} %bed.3) | copy-start | bytes 196612
  9.0 45.2 %copy-start.8 = (f32[128,128]{1,0:T(8,128)S(1)}, f32[128,128]{1,0:T(8,128)}, u32[]{:S(2)}) copy-start(f32[128,128]{1,0:T(8,128)} %conv.3) | copy-start | bytes 196612
  9.0 45.2 %copy-start.10 = (s32[128,128]{1,0:T(8,128)S(1)}, s32[128,128]{1,0:T(8,128)}, u32[]{:S(2)}) copy-start(s32[128,128]{1,0:T(8,128)} %wet.3) | copy-start | bytes 196612
  9.0 45.2 %copy-start.11 = (f32[128,128]{1,0:T(8,128)S(1)}, f32[128,128]{1,0:T(8,128)}, u32[]{:S(2)}) copy-start(f32[128,128]{1,0:T(8,128)} %salt.4) | copy-start | bytes 196612
  9.0 45.2 %copy-start.12 = (f32[128,128]{1,0:T(8,128)S(1)}, f32[128,128]{1,0:T(8,128)}, u32[]{:S(2)}) copy-start(f32[128,128]{1,0:T(8,128)} %leak.1) | copy-start | bytes 196612
  9.0 45.1 %copy-start.13 = (s32[1,1,128]{2,1,0:T(1,128)S(1)}, s32[1,1,128]{2,1,0:T(1,128)}, u32[]{:S(2)}) copy-start(s32[1,1,128]{2,1,0:T(1,128)} %param.18) | copy-start | bytes 1540
  9.0 9.6 %collective-permute-start = (f32[152,128]{1,0:T(8,128)S(1)}, f32[152,128]{1,0:T(8,128)S(1)}, u32[]{:S(2)}, u32[]{:S(2)}) collective-permute-start(f32[152,128]{1,0:T(8,128)S(1)} %get-tuple-element.32), channel_id=1, source_target_pairs={{0,7},{1,0},{2,1},{3,2},{4,3},{5,4},{6,5},{7,6},{8,15},{9,8},{10,9... | collective-permute-start | bytes 233480 | tf_op jit(solution)/shard_map/ppermute | solution.py:28
  9.5 9.2 %collective-permute-start.1 = (f32[152,128]{1,0:T(8,128)S(1)}, f32[152,128]{1,0:T(8,128)S(1)}, u32[]{:S(2)}, u32[]{:S(2)}) collective-permute-start(f32[152,128]{1,0:T(8,128)S(1)} %get-tuple-element.33), channel_id=1, source_target_pairs={{0,1},{1,2},{2,3},{3,4},{4,5},{5,6},{6,7},{7,0},{8,9},{9,10},{10,1... | collective-permute-start | bytes 233480 | tf_op jit(solution)/shard_map/ppermute | solution.py:28
  24.1 44.1 %collective-permute-start.4 = (f32[18,112,128]{2,1,0:T(8,128)}, f32[18,112,128]{2,1,0:T(8,128)S(1)}, u32[]{:S(2)}, u32[]{:S(2)}) collective-permute-start(f32[18,112,128]{2,1,0:T(8,128)} %get-tuple-element.43), channel_id=1, source_target_pairs={{0,120},{8,0},{16,8},{24,16},{32,24},{40,32},{48,40},{56,48},{64,5... | collective-permute-start | bytes 3096584 | tf_op jit(solution)/shard_map/ppermute | solution.py:28
  28.8 39.5 %collective-permute-start.5 = (f32[18,112,128]{2,1,0:T(8,128)}, f32[18,112,128]{2,1,0:T(8,128)}, u32[]{:S(2)}, u32[]{:S(2)}) collective-permute-start(f32[18,112,128]{2,1,0:T(8,128)} %get-tuple-element.44), channel_id=1, source_target_pairs={{0,8},{8,16},{16,24},{24,32},{32,40},{40,48},{48,56},{56,64},{64,7... | collective-permute-start | bytes 3096584 | tf_op jit(solution)/shard_map/ppermute | solution.py:28
  28.8 25.4 %collective-permute-start.3 = (f32[24,128]{1,0:T(8,128)S(1)}, f32[24,128]{1,0:T(8,128)S(1)}, u32[]{:S(2)}, u32[]{:S(2)}) collective-permute-start(f32[24,128]{1,0:T(8,128)S(1)} %get-tuple-element.37), channel_id=1, source_target_pairs={{0,8},{8,16},{16,24},{24,32},{32,40},{40,48},{48,56},{56,64},{64,7... | collective-permute-start | bytes 36872 | tf_op jit(solution)/shard_map/ppermute | solution.py:28
  28.8 25.4 %collective-permute-start.2 = (f32[24,128]{1,0:T(8,128)S(1)}, f32[24,128]{1,0:T(8,128)S(1)}, u32[]{:S(2)}, u32[]{:S(2)}) collective-permute-start(f32[24,128]{1,0:T(8,128)S(1)} %get-tuple-element.36.after), channel_id=1, source_target_pairs={{0,120},{8,0},{16,8},{24,16},{32,24},{40,32},{48,40},{56,48},{64,5... | collective-permute-start | bytes 36872 | tf_op jit(solution)/shard_map/ppermute | solution.py:28
  55.7 6.9 %collective-permute-start.8 = (f32[16,384]{1,0:T(8,128)S(1)}, f32[16,384]{1,0:T(8,128)S(1)}, u32[]{:S(2)}, u32[]{:S(2)}) collective-permute-start(f32[16,384]{1,0:T(8,128)S(1)} %get-tuple-element.54), channel_id=1, source_target_pairs={{0,6},{1,7},{2,0},{3,1},{4,2},{5,3},{6,4},{7,5},{8,14},{9,15},{10,... | collective-permute-start | bytes 73736 | tf_op jit(solution)/shard_map/ppermute | solution.py:28
  59.7 8.0 %collective-permute-start.6 = (f32[32,384]{1,0:T(8,128)S(1)}, f32[32,384]{1,0:T(8,128)S(1)}, u32[]{:S(2)}, u32[]{:S(2)}) collective-permute-start(f32[32,384]{1,0:T(8,128)S(1)} %get-tuple-element.52), channel_id=1, source_target_pairs={{0,7},{1,0},{2,1},{3,2},{4,3},{5,4},{6,5},{7,6},{8,15},{9,8},{10,9... | collective-permute-start | bytes 147464 | tf_op jit(solution)/shard_map/ppermute | solution.py:28
  59.7 8.0 %collective-permute-start.7 = (f32[32,384]{1,0:T(8,128)S(1)}, f32[32,384]{1,0:T(8,128)S(1)}, u32[]{:S(2)}, u32[]{:S(2)}) collective-permute-start(f32[32,384]{1,0:T(8,128)S(1)} %get-tuple-element.53), channel_id=1, source_target_pairs={{0,1},{1,2},{2,3},{3,4},{4,5},{5,6},{6,7},{7,0},{8,9},{9,10},{10,1... | collective-permute-start | bytes 147464 | tf_op jit(solution)/shard_map/ppermute | solution.py:28
  62.6 5.0 %collective-permute-start.9 = (f32[16,384]{1,0:T(8,128)S(1)}, f32[16,384]{1,0:T(8,128)S(1)}, u32[]{:S(2)}, u32[]{:S(2)}) collective-permute-start(f32[16,384]{1,0:T(8,128)S(1)} %get-tuple-element.55), channel_id=1, source_target_pairs={{0,2},{1,3},{2,4},{3,5},{4,6},{5,7},{6,0},{7,1},{8,10},{9,11},{10,... | collective-permute-start | bytes 73736 | tf_op jit(solution)/shard_map/ppermute | solution.py:28
  67.7 8.1 %collective-permute-start.10 = (f32[8,768]{1,0:T(8,128)S(1)}, f32[8,768]{1,0:T(8,128)S(1)}, u32[]{:S(2)}, u32[]{:S(2)}) collective-permute-start(f32[8,768]{1,0:T(8,128)S(1)} %get-tuple-element.57), channel_id=1, source_target_pairs={{0,120},{8,0},{16,8},{24,16},{32,24},{40,32},{48,40},{56,48},{64,5... | collective-permute-start | bytes 73736 | tf_op jit(solution)/shard_map/ppermute | solution.py:28
  67.8 8.1 %collective-permute-start.11 = (f32[8,768]{1,0:T(8,128)S(1)}, f32[8,768]{1,0:T(8,128)S(1)}, u32[]{:S(2)}, u32[]{:S(2)}) collective-permute-start(f32[8,768]{1,0:T(8,128)S(1)} %get-tuple-element.58), channel_id=1, source_target_pairs={{0,8},{8,16},{16,24},{24,32},{32,40},{40,48},{48,56},{56,64},{64,7... | collective-permute-start | bytes 73736 | tf_op jit(solution)/shard_map/ppermute | solution.py:28

commit v2 on v1

--- a/solution.py
+++ b/solution.py
@@ -19,7 +19,7 @@
 spread_vertical = 0.1
 
 F32 = jnp.float32
-VMEM_LIMIT = 40 * 2**20
+VMEM_LIMIT = 20 * 2**20
 UNROLL = 8
 
 
@@ -28,20 +28,37 @@
     return lax.ppermute(block, axis, [(i, (i + step) % count) for i in range(count)])
 
 
-def call(body, outs, args, name, scratch=(), keep=None):
-    shapes = [
-        jax.ShapeDtypeStruct(shape, F32) if keep is not None and i in keep else pltpu.VMEM(shape, F32)
-        for i, shape in enumerate(outs)
-    ]
+def call(body, outs, args, name, scratch=(), keep=(), raw=(), micros=1.0):
+    outs = [x if isinstance(x, jax.core.ShapedArray) else jax.ShapeDtypeStruct(x, F32) for x in outs]
+    shapes = [x if i in keep else pltpu.VMEM(x.shape, x.dtype) for i, x in enumerate(outs)]
+    args = [pltpu.with_memory_space_constraint(x, pltpu.HBM) if i in raw else x for i, x in enumerate(args)]
+    spec = lambda i: pl.BlockSpec(memory_space=pltpu.HBM if i in raw else pltpu.VMEM)
     return pl.pallas_call(
         body,
         out_shape=shapes,
-        in_specs=[pl.BlockSpec(memory_space=pltpu.VMEM)] * len(args),
+        in_specs=[spec(i) for i in range(len(args))],
         out_specs=[pl.BlockSpec(memory_space=pltpu.VMEM)] * len(outs),
         scratch_shapes=list(scratch),
         compiler_params=pltpu.CompilerParams(vmem_limit_bytes=VMEM_LIMIT),
+        cost_estimate=pl.CostEstimate(flops=0, bytes_accessed=int(micros * 3.5e6), transcendentals=0),
         name=name,
     )(*args)
+
+
+def behind(arrays, *first):
+    def body(*refs):
+        del refs
+
+    count = len(arrays)
+    return pl.pallas_call(
+        body,
+        out_shape=[pltpu.VMEM(x.shape, x.dtype) for x in arrays],
+        in_specs=[pl.BlockSpec(memory_space=pltpu.VMEM)] * (count + len(first)),
+        out_specs=[pl.BlockSpec(memory_space=pltpu.VMEM)] * count,
+        input_output_aliases={i: i for i in range(count)},
+        compiler_params=pltpu.CompilerParams(vmem_limit_bytes=VMEM_LIMIT),
+        name="behind",
+    )(*arrays, *first)
 
 
 def lanes(shape):
@@ -57,49 +74,57 @@
     return x if by == 0 else pltpu.roll(x, by, axis)
 
 
-def pack_lanes(tiles, lane):
-    low = tiles[0]
-    high = roll(tiles[0], 8, 1)
-    for i in range(1, len(tiles)):
-        here = lane >= 8 * i
-        low = jnp.where(here, roll(tiles[i], 8 * i, 1), low)
-        high = jnp.where(here, roll(tiles[i], 8 * i + 8, 1), high)
-    return low, high
-
-
-def pack_inland(head, salt, cond, depth, bed, conv, wet, to_low, to_high, rows_low, rows_high):
+def pack_inland(*refs):
+    args, (to_low, to_high, rows_low, rows_high), here, sems = refs[:11], refs[11:15], refs[15:26], refs[26]
+    copies = [pltpu.make_async_copy(x, y, sems.at[i]) for i, (x, y) in enumerate(zip(args, here))]
+    surf_copies, late_copies, aq_copies = copies[:4], copies[4:8], copies[8:]
+    for copy in (*surf_copies, *aq_copies, *late_copies):
+        copy.start()
+    for copy in surf_copies:
+        copy.wait()
+    depth, bed, conv, wet = here[:4]
     lane = lanes((8, 128))
     sub = rows_of((8, 128))
     level_rows, conduct_rows, tiles = [], [], []
     for t in range(16):
-        here = slice(8 * t, 8 * t + 8)
-        level = bed[here, :] + depth[here, :]
-        conduct = wet[here, :].astype(F32) * jnp.sqrt(conv[here, :])
+        at = slice(8 * t, 8 * t + 8)
+        level = bed[at, :] + depth[at, :]
+        conduct = wet[at, :].astype(F32) * jnp.sqrt(conv[at, :])
         level_rows.append(level)
         conduct_rows.append(conduct)
         tiles.append((jnp.where(lane < 4, level, roll(conduct, 4, 1)), jnp.where(lane < 4, roll(level, 4, 1), roll(conduct, 8, 1))))
     low, high = tiles[0]
     for t in range(1, 16):
-        here = lane >= 8 * t
-        low = jnp.where(here, roll(tiles[t][0], 8 * t, 1), low)
-        high = jnp.where(here, roll(tiles[t][1], 8 * t, 1), high)
+        at = lane >= 8 * t
+        low = jnp.where(at, roll(tiles[t][0], 8 * t, 1), low)
+        high = jnp.where(at, roll(tiles[t][1], 8 * t, 1), high)
     to_low[144:152, :] = low
     to_high[144:152, :] = high
     rows_low[...] = jnp.where(sub < 4, level_rows[0], roll(conduct_rows[0], 4, 0))
     rows_high[...] = jnp.where(sub >= 4, level_rows[15], roll(conduct_rows[15], 4, 0))
-    for a, ref in enumerate((head, salt, cond)):
-        def group(g, _, a=a, ref=ref):
-            first = [ref[g * 8 + i] for i in range(8)]
-            low, high = pack_lanes(first + [ref[ref.shape[0] - 1 - g * 8 - i] for i in range(8)], lane)
-            at = pl.ds(pl.multiple_of((a * 6 + g) * 8, 8), 8)
-            to_low[at, :] = low
-            to_high[at, :] = high
-            return 0
-
-        lax.fori_loop(0, 6, group, 0)
-
-
-def join_rims(right, left, rows_low, rows_high, to_low, to_high):
+    first = jnp.bitwise_and(lane, 8) == 0
+    for a in range(3):
+        aq_copies[a].wait()
+        ref = here[8 + a]
+        last = ref.shape[0] - 1
+        for q in range(6):
+            ends = []
+            for h in range(2):
+                t = 8 * q + 4 * h
+                layers = [t + e for e in range(4)] + [last - t - e for e in range(4)]
+                x = roll(ref[layers[0]], 8, 1)
+                for k in range(1, 8):
+                    x = jnp.where(lane >= 16 * k, roll(ref[layers[k]], 16 * k + 8, 1), x)
+                ends.append(x)
+            at = slice((a * 6 + q) * 8, (a * 6 + q) * 8 + 8)
+            to_low[at, :] = jnp.where(first, roll(ends[1], -8, 1), ends[0])
+            to_high[at, :] = jnp.where(first, ends[0], roll(ends[1], 8, 1))
+    for copy in late_copies:
+        copy.wait()
+
+
+def join_rims(right, left, rows_low, rows_high, after, to_low, to_high):
+    del after
     for out, rows in ((to_low, rows_low), (to_high, rows_high)):
         out[0:8, :] = right[144:152, :]
         out[8:16, :] = left[144:152, :]
@@ -181,13 +206,12 @@
     cells = wet[...].astype(F32) * active * leak[...]
     gx, gy = lax.axis_index("gx"), lax.axis_index("gy")
     last_row, last_tile = 8 * lax.axis_size("gx") - 1, lax.axis_size("gy") - 1
-    block = rows_of((128, 1))
-    global_row = gx * 128 + block + shifts[:, 0:1]
+    block = lanes((1, 128))
+    global_row = gx * 128 + block + shifts[0:1, :]
     row = jnp.clip(jnp.right_shift(global_row, 4), 0, last_row) - gx * 8 + 2
-    tile = jnp.clip(gy + shifts[:, 1:2], 0, last_tile) - gy + 1
+    tile = jnp.clip(gy + shifts[1:2, :], 0, last_tile) - gy + 1
     target = tile * 16 + row
-    choose = jnp.where(lanes((128, 128)) == target, 1.0, 0.0)
-    choose = jnp.transpose(choose)[0:48]
+    choose = jnp.where(rows_of((48, 128)) == target, 1.0, 0.0)
     sums = [dot(choose, term, ((1,), (0,))) for term in (cells, cells * mean_level, cells * salt[...])]
     lane48 = lanes((16, 128))
     for i, total in enumerate(sums):
@@ -231,52 +255,76 @@
 
 def interleave(head, salt, cond, *outs):
     lane = lanes((8, 128))
+    inner = jnp.bitwise_and(lane, 63)
     index = [jnp.clip(column(lane, j), 0, 127) for j in range(J)]
     for ref, out in zip((head, salt, cond), outs):
         last = ref.shape[0] - 1
 
-        def pair(t, _, ref=ref, out=out, last=last):
-            for e in range(2):
-                at = 2 * t + e
-                x, y = ref[at], ref[last - at]
+        def eight(q, _, ref=ref, out=out, last=last):
+            for h in range(2):
                 for j in range(J):
-                    out[at, 8 * j : 8 * j + 8, :] = jnp.where(lane < 64, take(x, index[j]), take(y, index[j]))
+                    x = []
+                    for e in range(4):
+                        at = q * 8 + 4 * h + e
+                        x.append(jnp.where(lane < 64, take(ref[at], index[j]), take(ref[last - at], index[j])))
+                    m = (h * J + j) * 3
+                    for p in range(3):
+                        out[q, m + p] = jnp.where(inner < 48, x[p], roll(x[3], 48 - 16 * p, 1))
             return 0
 
-        lax.fori_loop(0, (last + 1) // 4, pair, 0)
-
-
-def pack_coast(head, salt, cond, right, left, after, rim, to_low, to_high):
-    del after
+        lax.fori_loop(0, (last + 1) // 16, eight, 0)
+
+
+def pack_coast(head, salt, cond, right, left, full, first_low, first_high, then_low, then_high):
     lane = lanes((8, 128))
-    group = jnp.right_shift(lane, 3)
     half = jnp.bitwise_and(lane, 64)
     inner = jnp.bitwise_and(lane, 63)
-    even = jnp.bitwise_and(group, 1) == 0
-    for a, ref in enumerate((head, salt, cond)):
-        def eight(q, _, a=a, ref=ref):
+    odd = jnp.bitwise_and(lane, 8) != 0
+    picks = []
+    for h in range(2):
+        for j in range(J):
+            for p in range(3):
+                mine = inner < 48
+                y = J * jnp.where(mine, inner, inner - 48 + 16 * p) + (j - 8)
+                e = jnp.where(mine, p, 3)
+                right_at, left_at = (8, 0) if h == 0 else (0, 8)
+                source = 16 * e + half + jnp.where(y < 0, left_at + 8 + y, right_at + y - 128)
+                picks.append(((y < 0) | (y >= 128), jnp.clip(source, 0, 127)))
+    ways = ((first_low, first_high, 6), (then_low, then_high, 0), (first_low, first_high, 0))
+    for a, (ref, (to_low, to_high, start)) in enumerate(zip((head, salt, cond), ways)):
+        def eight(q, _, a=a, ref=ref, to_low=to_low, to_high=to_high, start=start):
             at = pl.multiple_of((a * 6 + q) * 8, 8)
             r, l = right[pl.ds(at, 8), :], left[pl.ds(at, 8), :]
-            rims = (jnp.where(even, r, roll(l, 8, 1)), jnp.where(even, roll(l, -8, 1), r))
-            for h in range(2):
-                for j in range(J):
-                    y = column(lane, j)
-                    tiles = []
-                    for e in range(4 * h, 4 * h + 4):
-                        source = 8 * e + half + jnp.where(y < 0, y + (16 if e % 2 == 0 else 0), y - 128)
-                        source = jnp.clip(source, 0, 127)
-                        x = ref[q * 8 + e, 8 * j : 8 * j + 8, :]
-                        x = jnp.where((y < 0) | (y >= 128), take(rims[e % 2], source), x)
-                        rim[a * 48 + q * 8 + e, 8 * j : 8 * j + 8, :] = x
-                        tiles.append(x)
-                    for p in range(3):
-                        m = 6 * ((h * J + j) * 3 + p)
-                        full = jnp.where(inner < 48, tiles[p], roll(tiles[3], 48 - 16 * p, 1))
-                        to_low[a * 6 + q, m : m + 6, :] = full[0:6]
-                        to_high[a * 6 + q, m : m + 6, :] = full[2:8]
+            rims = (jnp.where(odd, r, l), jnp.where(odd, l, r))
+            for m in range(18):
+                there, source = picks[m]
+                x = jnp.where(there, take(rims[m // 9], source), ref[q, m])
+                full[a * 6 + q, m] = x
+                to_low[start + q, 6 * m : 6 * m + 6, :] = x[0:6]
+                to_high[start + q, 6 * m : 6 * m + 6, :] = x[2:8]
             return 0
 
         lax.fori_loop(0, 6, eight, 0)
+
+
+def fourth(x, inner):
+    return jnp.where(inner < 16, roll(x[0], -48, 1), jnp.where(inner < 32, roll(x[1], -32, 1), roll(x[2], -16, 1)))
+
+
+def open_tile(full, rim):
+    inner = jnp.bitwise_and(lanes((8, 128)), 63)
+
+    def eight(b, _):
+        for h in range(2):
+            for j in range(J):
+                m = (h * J + j) * 3
+                x = [full[b, m + p] for p in range(3)]
+                x.append(fourth(x, inner))
+                for e in range(4):
+                    rim[b * 8 + 4 * h + e, 8 * j : 8 * j + 8, :] = x[e]
+        return 0
+
+    lax.fori_loop(0, 18, eight, 0)
 
 
 def up(t):
@@ -378,42 +426,41 @@
     return jnp.where(lanes((8, 128)) < 64, size, -size).astype(F32)
 
 
-def prepare(rim, high, low, part, side, salt, wx, wy, vv, head, cond, stage):
-    steps = salt.shape[0]
+def unfold(a, rim, high, low, start, ext, stage):
+    inner = jnp.bitwise_and(lanes((8, 128)), 63)
+
+    def eight(q, _):
+        block = start + q
+        for m in range(18):
+            stage[m, 0:4, :] = high[block, 6 * m : 6 * m + 4, :]
+            stage[m, 4:8, :] = low[block, 6 * m + 2 : 6 * m + 6, :]
+            stage[m, 8:10, :] = high[block, 6 * m + 4 : 6 * m + 6, :]
+            stage[m, 14:16, :] = low[block, 6 * m : 6 * m + 2, :]
+        for h in range(2):
+            for e in range(4):
+                ext[q * 8 + 4 * h + e, 0:24, :] = rim[a * 48 + q * 8 + 4 * h + e, 0:24, :]
+            for j in range(J):
+                m = (h * J + j) * 3
+                for i in range(2):
+                    x = [stage[m + p, 8 * i : 8 * i + 8, :] for p in range(3)]
+                    x.append(fourth(x, inner))
+                    at = 24 * (i + 1) + 8 * j
+                    for e in range(4):
+                        ext[q * 8 + 4 * h + e, at : at + 8, :] = x[e]
+        return 0
+
+    stage[...] = jnp.zeros(stage.shape, F32)
+    lax.fori_loop(0, ext.shape[0] // 8, eight, 0)
+
+
+def weights(rim, high, low, head, wx, wy, vv, cond, stage):
+    unfold(2, rim, high, low, 0, cond, stage)
+    unfold(0, rim, high, low, 6, head, stage)
+    steps = head.shape[0]
     n = 3 * J
     lane = lanes((8, 128))
     sub = rows_of((8, 128))
     inner = jnp.bitwise_and(lane, 63)
-    stage[...] = jnp.zeros(stage.shape, F32)
-    for a, ext in enumerate((head, salt, cond)):
-        def eight(q, _, a=a, ext=ext):
-            block = a * 6 + q
-            for m in range(18):
-                stage[m, 0:4, :] = high[block, 6 * m : 6 * m + 4, :]
-                stage[m, 4:8, :] = low[block, 6 * m + 2 : 6 * m + 6, :]
-                stage[m, 8:10, :] = high[block, 6 * m + 4 : 6 * m + 6, :]
-                stage[m, 14:16, :] = low[block, 6 * m : 6 * m + 2, :]
-            for h in range(2):
-                for e in range(4):
-                    ext[q * 8 + 4 * h + e, 0:24, :] = rim[a * 48 + q * 8 + 4 * h + e, 0:24, :]
-                for j in range(J):
-                    m = (h * J + j) * 3
-                    for i in range(2):
-                        x = [stage[m + p, 8 * i : 8 * i + 8, :] for p in range(3)]
-                        x.append(
-                            jnp.where(
-                                inner < 16,
-                                roll(x[0], -48, 1),
-                                jnp.where(inner < 32, roll(x[1], -32, 1), roll(x[2], -16, 1)),
-                            )
-                        )
-                        at = 24 * (i + 1) + 8 * j
-                        for e in range(4):
-                            ext[q * 8 + 4 * h + e, at : at + 8, :] = x[e]
-            return 0
-
-        lax.fori_loop(0, steps // 8, eight, 0)
-
     gx, gy = lax.axis_index("gx"), lax.axis_index("gy")
     last_x, last_y = lax.axis_size("gx") - 1, lax.axis_size("gy") - 1
     has = lambda there: jnp.where(there, 1.0, 0.0).astype(F32)
@@ -426,31 +473,38 @@
             in_low = jnp.where(y >= -HALO, has(gy > 0), 0.0)
             in_high = jnp.where(y < 128 + HALO, has(gy < last_y), 0.0)
             masks.append(rows[i] * jnp.where(inner < 48, jnp.where(y < 0, in_low, jnp.where(y < 128, 1.0, in_high)), 0.0))
-    weigh = tilt()
 
     def known(at):
         return [jnp.where(m > 0, x, 1.0) for m, x in zip(masks, get(cond, at, n))]
 
+    def one(at, k, inmost=False):
+        k_in = swap(k) if inmost else known(at + 1)
+        rock = [jnp.sqrt(x) * m for m, x in zip(masks, k)]
+        put(wx, at, [time_step * a * b for a, b in zip(rock, up(rock))])
+        put(wy, at, [time_step * a * b for a, b in zip(rock, nxt(rock))])
+        put(vv, at, [2.0 * a * b / (a + b) for a, b in zip(k, k_in)])
+        return k_in
+
+    one(steps - 1, sweep(0, steps - 1, one, known(0), 4), True)
+
+
+def prepare(rim, high, low, head, wx, wy, vv, part, side, salt, stage):
+    unfold(1, rim, high, low, 0, salt, stage)
+    steps = salt.shape[0]
+    n = 3 * J
+    weigh = tilt()
+
     def one(at, carry, inmost=False):
-        k, c, lift_above = carry
-        k_in = swap(k) if inmost else known(at + 1)
+        c, lift_above = carry
         c_in = swap(c) if inmost else get(salt, at + 1, n)
-        rock = [jnp.sqrt(x) * m for m, x in zip(masks, k)]
-        x = [time_step * a * b for a, b in zip(rock, up(rock))]
-        y = [time_step * a * b for a, b in zip(rock, nxt(rock))]
-        v = [2.0 * a * b / (a + b) for a, b in zip(k, k_in)]
-        put(wx, at, x)
-        put(wy, at, y)
-        put(vv, at, v)
         h = get(head, at, n)
-        lift = [(weigh * b) * (p + q) for b, p, q in zip(v, c, c_in)]
-        flow, moved = sides_of(h, c, x, y)
+        lift = [(weigh * b) * (p + q) for b, p, q in zip(get(vv, at, n), c, c_in)]
+        flow, moved = sides_of(h, c, get(wx, at, n), get(wy, at, n))
         put(part, at, [a + b - p + q for a, b, p, q in zip(h, flow, lift, lift_above)])
         put(side, at, [porosity * a + b for a, b in zip(c, moved)])
-        return k_in, c_in, lift
-
-    carry = sweep(0, steps - 1, one, (known(0), get(salt, 0, n), zeros(n)), 4)
-    one(steps - 1, carry, True)
+        return c_in, lift
+
+    one(steps - 1, sweep(0, steps - 1, one, (get(salt, 0, n), zeros(n)), 4), True)
 
 
 def aquifer(part0, side0, salt0, wx, wy, vv, gathered, leak_high, leak_low, head_out, salt_out, hy, cz, ss, ip, uu, iq, kk, mid, leak):
@@ -588,14 +642,27 @@
     return (steps, 24 * J, 128)
 
 
-def run_prepare(rim, high, low):
+def run_weights(rim, high, low):
+    steps = rim.shape[0] // 3
+    return call(
+        weights,
+        [whole(steps)] * 4,
+        (rim, high, low),
+        "weights",
+        scratch=[pltpu.VMEM(whole(steps), F32), pltpu.VMEM((18, 16, 128), F32)],
+        micros=4.0,
+    )
+
+
+def run_prepare(rim, high, low, *ready):
     steps = rim.shape[0] // 3
     return call(
         prepare,
-        [whole(steps)] * 6,
-        (rim, high, low),
+        [whole(steps)] * 3,
+        (rim, high, low, *ready),
         "prepare",
-        scratch=[pltpu.VMEM(whole(steps), F32)] * 2 + [pltpu.VMEM((18, 16, 128), F32)],
+        scratch=[pltpu.VMEM((18, 16, 128), F32)],
+        micros=4.0,
     )
 
 
@@ -608,51 +675,66 @@
         "aquifer",
         scratch=[pltpu.VMEM(whole(steps), F32)] * 7 + [pltpu.VMEM((2, 24 * J, 128), F32), pltpu.VMEM((24, 768), F32)],
         keep=(0, 1),
+        micros=20.0,
     )
 
 
 def local(surf_depth, surf_bed, surf_conv, wet_mask, surf_salt, seabed_leak, seabed_shift, active_count, aq_head, aq_salt, aq_cond):
-    shifts = seabed_shift.reshape(-1, 2)
+    shifts = seabed_shift.reshape(-1, 2).T
     counts = active_count.reshape(1, -1)
     steps = aq_head.shape[0] // 2
-    aq = (aq_head, aq_salt, aq_cond)
+    args = (surf_depth, surf_bed, surf_conv, wet_mask, surf_salt, seabed_leak, shifts, counts, aq_head, aq_salt, aq_cond)
     rim = (152, 128)
-    in_low, in_high, rows_low, rows_high = call(
-        pack_inland, [rim, rim, (8, 128), (8, 128)], (*aq, surf_depth, surf_bed, surf_conv, wet_mask), "pack_inland"
-    )
+    in_low, in_high, rows_low, rows_high, *args = call(
+        pack_inland,
+        [rim, rim, (8, 128), (8, 128), *(jax.typeof(x) for x in args)],
+        args,
+        "pack_inland",
+        scratch=[pltpu.SemaphoreType.DMA((11,))],
+        raw=range(11),
+        micros=3.0,
+    )
+    aq = args[8:]
     right = shift(in_low, "gy", -1)
     left = shift(in_high, "gy", 1)
-    tiles = call(interleave, [(steps, 8 * J, 128)] * 3, aq, "interleave")
-    join_low, join_high = call(join_rims, [(24, 128)] * 2, (right, left, rows_low, rows_high), "join_rims")
+    tiles = call(interleave, [(steps // 8, 18, 8, 128)] * 3, aq, "interleave", micros=4.0)
+    join_low, join_high = call(join_rims, [(24, 128)] * 2, (right, left, rows_low, rows_high, tiles[0]), "join_rims")
     above = shift(join_low, "gx", -1)
     below = shift(join_high, "gx", 1)
-    rims, coast_low, coast_high = call(
+    blocks = 3 * steps // 8
+    full, *coast = call(
         pack_coast,
-        [(3 * steps, 8 * J, 128), (18, 112, 128), (18, 112, 128)],
-        (*tiles, right, left, join_low),
+        [(blocks, 18, 8, 128)] + [(blocks // 3 * 2, 112, 128)] * 2 + [(blocks // 3, 112, 128)] * 2,
+        (*tiles, right, left),
         "pack_coast",
-    )
-    high = shift(coast_low, "gx", -1)
-    low = shift(coast_high, "gx", 1)
+        micros=3.0,
+    )
+    rims = call(open_tile, [(3 * steps, 8 * J, 128)], (full,), "open_tile", micros=3.0)[0]
+    first_low, first_high = behind(coast[:2], above, below)
+    first = shift(first_low, "gx", -1), shift(first_high, "gx", 1)
     depth, to_low, to_high, to_low2, to_high2, own = call(
         surface,
         [(128, 128), (32, 384), (32, 384), (16, 384), (16, 384), (16, 768)],
-        (surf_depth, surf_bed, surf_conv, wet_mask, surf_salt, seabed_leak, shifts, counts, right, left, above, below),
+        (*args[:8], right, left, above, below),
         "surface",
         scratch=[pltpu.VMEM((136, 256), F32)] * 2,
         keep=(0,),
+        micros=1.5,
     )
     leak_right = shift(to_low, "gy", -1)
     leak_left = shift(to_high, "gy", 1)
     leak_right2 = shift(to_low2, "gy", -2)
     leak_left2 = shift(to_high2, "gy", 2)
-    ready = run_prepare(rims, high, low)
+    then_low, then_high = behind(coast[2:], leak_right, leak_left, leak_right2, leak_left2)
+    then = shift(then_low, "gx", -1), shift(then_high, "gx", 1)
+    head, *links = run_weights(rims, *first)
+    ready = run_prepare(rims, *then, head, *links)
     gathered, sum_low, sum_high = call(
         sum_inland, [(16, 768), (8, 768), (8, 768)], (own, leak_right, leak_left, leak_right2, leak_left2), "sum_inland"
     )
     leak_high = shift(sum_low, "gx", -1)
     leak_low = shift(sum_high, "gx", 1)
-    head, salt = run_aquifer(*ready, gathered, leak_high, leak_low)
+    head, salt = run_aquifer(*ready, *links, gathered, leak_high, leak_low)
     return depth, head, salt
 
 

time: 97 us -> 78.7 us (0.81)
  local copies, waits for them, and re-layouts: 6.5 us -> 0 us
  Pallas kernels: 43.6 us -> 37.5 us
  waiting for transfers between devices: 24.9 us -> 20.1 us
    unnamed x31 -> x0, local copies, waits for them, and re-layouts: 6.5 us -> none
    pallas_call x8 -> x12, Pallas kernels: 43.6 us -> 37.5 us  [the longest x10 37.5 us: call(): pl.pallas_call(body, out_shape=shapes, in_specs=[spec(i) for i in range(l...]
    ppermute x12 -> x14, waiting for transfers between devices: 24.9 us -> 20.1 us  [shift(): lax.ppermute(block, axis, [(i, (i + step) % count) for i in range(count)])]
    ppermute x12 -> x14, starting transfers between devices: 20.5 us -> 20.2 us  [shift(): lax.ppermute(block, axis, [(i, (i + step) % count) for i in range(count)])]
  transfers between devices with their start and end apart: 12 -> 14, of which waited for: 2 -> 6; matrix products, arithmetic and copies ran while one was open for 0% -> 0% of each run, Pallas kernels for 16% -> 19%
where the time goes in v2:
time: 78.7 us; the launch traced here: 78.5 us
  Pallas kernels  37.5 us (48%)
  starting transfers between devices  20.2 us (26%)
  waiting for transfers between devices  20.1 us (26%)
    pallas_call x10, Pallas kernels, call(): pl.pallas_call(body, out_shape=shapes, in_specs=[spec(i) for i in range(l...  37.5 us
    ppermute x14, starting transfers between devices, shift(): lax.ppermute(block, axis, [(i, (i + step) % count) for i in range(count)])  20.2 us
    ppermute x14, waiting for transfers between devices, shift(): lax.ppermute(block, axis, [(i, (i + step) % count) for i in range(count)])  20.1 us
  transfers between devices with their start and end apart: 14, of which 6 were waited for; matrix products, arithmetic and copies ran while one was open for 0% of the time, Pallas kernels for 19%

profile of v2, /device:TPU:8, one launch (start us, length us, event | category | flops | bytes accessed | tf_op | source)
XLA Modules:
  0.0 78.5 jit_solution(9234610317358261723)
XLA Ops:
  0.6 1.9 %pack_inland.1 = (f32[152,128]{1,0:T(8,128)S(1)}, f32[152,128]{1,0:T(8,128)S(1)}, f32[8,128]{1,0:T(8,128)S(1)}, f32[8,128]{1,0:T(8,128)S(1)}, f32[128,128]{1,0:T...) custom-call(f32[128,128]{1,0:T(8,128)} %refs_0_.1, ...), custom_call_target="tpu_custom_call" | custom-call | bytes 10500000 | tf_op jit(solution)/shard_map/pack_inland/pallas_call | solution.py:36
  2.5 0.4 collective-permute-start
  3.0 2.6 %collective-permute-start.1 = (f32[152,128]{1,0:T(8,128)S(1)}, f32[152,128]{1,0:T(8,128)S(1)}, u32[]{:S(2)}, u32[]{:S(2)}) collective-permute-start(f32[152,128]{1,0:T(8,128)S(1)} %get-tuple-element.59), channel_id=1, source_target_pairs={{0,1},{1,2},{2,3},{3,4},{4,5},{5,6},{6,7},{7,0},{8,9},{9,10},{10,1... | collective-permute-start | bytes 233480 | tf_op jit(solution)/shard_map/ppermute | solution.py:28
  5.5 3.4 %interleave.1 = (f32[6,18,8,128]{3,2,1,0:T(8,128)S(1)}, f32[6,18,8,128]{3,2,1,0:T(8,128)S(1)}, f32[6,18,8,128]{3,2,1,0:T(8,128)S(1)}) custom-call(f32[96,8,128]{2,1,0:T(8,128)S(1)} %get-tuple-element.62.head, f32[96,8,128]{2,1,0:T(8,128)S(1)} %get-tuple-element.63.salt, f32[96,8,128]{2,1,0:T(8,128)S(1)} %get-tuple-element.64.cond), custom_call_target="tpu_custom_call" | custom-call | bytes 14000000 | tf_op jit(solution)/shard_map/interleave/pallas_call | solution.py:36
  8.9 0.0 collective-permute-done.right
  8.9 0.6 collective-permute-done.1.left
  9.6 5.0 %collective-permute-start.2 = (f32[24,128]{1,0:T(8,128)S(1)}, f32[24,128]{1,0:T(8,128)S(1)}, u32[]{:S(2)}, u32[]{:S(2)}) collective-permute-start(f32[24,128]{1,0:T(8,128)S(1)} %get-tuple-element.66), channel_id=1, source_target_pairs={{0,120},{8,0},{16,8},{24,16},{32,24},{40,32},{48,40},{56,48},{64,5... | collective-permute-start | bytes 36872 | tf_op jit(solution)/shard_map/ppermute | solution.py:28
  14.6 0.0 collective-permute-start.3
  14.6 2.1 %pack_coast.1 = (f32[18,18,8,128]{3,2,1,0:T(8,128)S(1)}, f32[12,112,128]{2,1,0:T(8,128)S(1)}, f32[12,112,128]{2,1,0:T(8,128)S(1)}, f32[6,112,128]{2,1,0:T(8,128)S(1)}, f32[6,112,128]{2,1,0:T(8,128)S(1)}) custom-call(f32[6,18,8,128]{3,2,1,0:T(8,128)S(1)} %get-tuple-element.65.after.head, f32[6,18,8,128]{3,2,1,0:T(8,128)S(1)} %get-tuple-element.69.salt, ...), custom_call_target="tpu_custom_call" | custom-call | bytes 10500000 | tf_op jit(solution)/shard_map/pack_coast/pallas_call | solution.py:36
  16.6 0.0 collective-permute-done.2.above.refs_2_
  16.7 4.6 %collective-permute-done.3.below.refs_3_ = f32[24,128]{1,0:T(8,128)S(1)} collective-permute-done((f32[24,128]{1,0:T(8,128)S(1)}, f32[24,128]{1,0:T(8,128)S(1)}, u32[]{:S(2)}, u32[]{:S(2)}) %collective-permute-start.3) | collective-permute-done | bytes 12320 | tf_op jit(solution)/shard_map/ppermute | solution.py:28
  21.3 0.8 %collective-permute-start.10 = (f32[12,112,128]{2,1,0:T(8,128)S(1)}, f32[12,112,128]{2,1,0:T(8,128)S(1)}, u32[]{:S(2)}, u32[]{:S(2)}) collective-permute-start(f32[12,112,128]{2,1,0:T(8,128)S(1)} %get-tuple-element.82), channel_id=1, source_target_pairs={{0,120},{8,0},{16,8},{24,16},{32,24},{40,32},{48,40},{56,48},{64,5... | collective-permute-start | bytes 2064392 | tf_op jit(solution)/shard_map/ppermute | solution.py:28
  22.1 0.0 collective-permute-start.11
  22.1 1.4 %surface.1 = (f32[128,128]{1,0:T(8,128)}, f32[32,384]{1,0:T(8,128)S(1)}, f32[32,384]{1,0:T(8,128)S(1)}, f32[16,384]{1,0:T(8,128)S(1)}, f32[16,384]{1,0:T(8,128)S(1)}, /*index=5*/f32[16,768]{1,0:T(8,128)S(1)}) custom-call(f32[128,128]{1,0:T(8,128)S(1)} %get-tuple-element.50.depth, f32[128,128]{1,0:T(8,128)S(1)} %get-tuple-element.51.bed, ...), custom_call_target="tpu_custom_call" | custom-call | bytes 5250000 | tf_op jit(solution)/shard_map/surface/pallas_call | solution.py:36
  23.5 3.1 %collective-permute-start.6 = (f32[16,384]{1,0:T(8,128)S(1)}, f32[16,384]{1,0:T(8,128)S(1)}, u32[]{:S(2)}, u32[]{:S(2)}) collective-permute-start(f32[16,384]{1,0:T(8,128)S(1)} %get-tuple-element.76), channel_id=1, source_target_pairs={{0,6},{1,7},{2,0},{3,1},{4,2},{5,3},{6,4},{7,5},{8,14},{9,15},{10,... | collective-permute-start | bytes 73736 | tf_op jit(solution)/shard_map/ppermute | solution.py:28
  26.6 0.1 collective-permute-start.4
  26.7 2.8 %collective-permute-start.5 = (f32[32,384]{1,0:T(8,128)S(1)}, f32[32,384]{1,0:T(8,128)S(1)}, u32[]{:S(2)}, u32[]{:S(2)}) collective-permute-start(f32[32,384]{1,0:T(8,128)S(1)} %get-tuple-element.75), channel_id=1, source_target_pairs={{0,1},{1,2},{2,3},{3,4},{4,5},{5,6},{6,7},{7,0},{8,9},{9,10},{10,1... | collective-permute-start | bytes 147464 | tf_op jit(solution)/shard_map/ppermute | solution.py:28
  29.5 0.0 collective-permute-done.6.refs_4_.right2
  29.5 0.0 collective-permute-start.7
  29.5 5.0 %collective-permute-done.7.refs_5_.left2 = f32[16,384]{1,0:T(8,128)S(1)} collective-permute-done((f32[16,384]{1,0:T(8,128)S(1)}, f32[16,384]{1,0:T(8,128)S(1)}, u32[]{:S(2)}, u32[]{:S(2)}) %collective-permute-start.7) | collective-permute-done | bytes 24608 | tf_op jit(solution)/shard_map/ppermute | solution.py:28
  34.6 4.5 %collective-permute-done.4.refs_2_.right = f32[32,384]{1,0:T(8,128)S(1)} collective-permute-done((f32[32,384]{1,0:T(8,128)S(1)}, f32[32,384]{1,0:T(8,128)S(1)}, u32[]{:S(2)}, u32[]{:S(2)}) %collective-permute-start.4) | collective-permute-done | bytes 49184 | tf_op jit(solution)/shard_map/ppermute | solution.py:28
  39.1 3.6 %collective-permute-done.5.refs_3_.left = f32[32,384]{1,0:T(8,128)S(1)} collective-permute-done((f32[32,384]{1,0:T(8,128)S(1)}, f32[32,384]{1,0:T(8,128)S(1)}, u32[]{:S(2)}, u32[]{:S(2)}) %collective-permute-start.5) | collective-permute-done | bytes 49184 | tf_op jit(solution)/shard_map/ppermute | solution.py:28
  42.7 0.0 collective-permute-start.8
  42.7 0.5 collective-permute-start.9
  43.2 4.9 %collective-permute-start.12 = (f32[8,768]{1,0:T(8,128)S(1)}, f32[8,768]{1,0:T(8,128)S(1)}, u32[]{:S(2)}, u32[]{:S(2)}) collective-permute-start(f32[8,768]{1,0:T(8,128)S(1)} %get-tuple-element.93), channel_id=1, source_target_pairs={{0,120},{8,0},{16,8},{24,16},{32,24},{40,32},{48,40},{56,48},{64,5... | collective-permute-start | bytes 73736 | tf_op jit(solution)/shard_map/ppermute | solution.py:28
  48.1 0.0 collective-permute-done.10.high
  48.1 0.0 collective-permute-start.13
  48.1 1.6 %open_tile.1.rim = f32[144,24,128]{2,1,0:T(8,128)S(1)} custom-call(f32[18,18,8,128]{3,2,1,0:T(8,128)S(1)} %get-tuple-element.71.full), custom_call_target="tpu_custom_call" | custom-call | bytes 10500000 | tf_op jit(solution)/shard_map/open_tile/pallas_call | solution.py:36
  49.7 0.0 collective-permute-done.11.low
  49.7 3.0 %weights.1 = (f32[48,72,128]{2,1,0:T(8,128)S(1)}, f32[48,72,128]{2,1,0:T(8,128)S(1)}, f32[48,72,128]{2,1,0:T(8,128)S(1)}, f32[48,72,128]{2,1,0:T(8,128)S(1)}) custom-call(f32[144,24,128]{2,1,0:T(8,128)S(1)} %open_tile.1.rim, f32[12,112,128]{2,1,0:T(8,128)S(1)} %collective-permute-done.10.high, f32[12,112,128]{2,1,0:T(8,128)S(1)} %collective-permute-done.11.low), custom_call_target="tpu_custom_call" | custom-call | bytes 14000000 | tf_op jit(solution)/shard_map/weights/pallas_call | solution.py:36
  52.8 0.0 collective-permute-done.8.high
  52.8 1.6 %collective-permute-done.9.low = f32[6,112,128]{2,1,0:T(8,128)S(1)} collective-permute-done((f32[6,112,128]{2,1,0:T(8,128)S(1)}, f32[6,112,128]{2,1,0:T(8,128)S(1)}, u32[]{:S(2)}, u32[]{:S(2)}) %collective-permute-start.9) | collective-permute-done | bytes 344096 | tf_op jit(solution)/shard_map/ppermute | solution.py:28
  54.4 3.6 %prepare.1 = (f32[48,72,128]{2,1,0:T(8,128)S(1)}, f32[48,72,128]{2,1,0:T(8,128)S(1)}, f32[48,72,128]{2,1,0:T(8,128)S(1)}) custom-call(f32[144,24,128]{2,1,0:T(8,128)S(1)} %open_tile.1.rim, f32[6,112,128]{2,1,0:T(8,128)S(1)} %collective-permute-done.8.high, f32[6,112,128]{2,1,0:T(8,128)S(1)} %collective-permute-done.9.low, ...), custom_call_target="tpu_custom_call" | custom-call | bytes 14000000 | tf_op jit(solution)/shard_map/prepare/pallas_call | solution.py:36
  58.0 0.0 collective-permute-done.12.leak_high
  58.0 0.0 collective-permute-done.13.leak_low
  58.0 20.5 %aquifer.1 = (f32[96,8,128]{2,1,0:T(8,128)}, f32[96,8,128]{2,1,0:T(8,128)}) custom-call(f32[48,72,128]{2,1,0:T(8,128)S(1)} %get-tuple-element.88.part0, f32[48,72,128]{2,1,0:T(8,128)S(1)} %get-tuple-element.89.side0, f32[48,72,128]{2,1,0:T(8,128)S(1)} %get-tuple-element.90.salt0, f32[48,72,128]{2,1,0:T(8,128)S(1)} %get-tuple-element.85.wx, ...), custom_call_target="tpu_custom_call" | custom-call | bytes 70000000 | tf_op jit(solution)/shard_map/aquifer/pallas_call | solution.py:36
  (4 shorter events, 0.0 us)
Async XLA Ops:
  2.5 6.4 %collective-permute-start = (f32[152,128]{1,0:T(8,128)S(1)}, f32[152,128]{1,0:T(8,128)S(1)}, u32[]{:S(2)}, u32[]{:S(2)}) collective-permute-start(f32[152,128]{1,0:T(8,128)S(1)} %get-tuple-element.58), channel_id=1, source_target_pairs={{0,7},{1,0},{2,1},{3,2},{4,3},{5,4},{6,5},{7,6},{8,15},{9,8},{10,9... | collective-permute-start | bytes 233480 | tf_op jit(solution)/shard_map/ppermute | solution.py:28
  3.0 6.6 %collective-permute-start.1 = (f32[152,128]{1,0:T(8,128)S(1)}, f32[152,128]{1,0:T(8,128)S(1)}, u32[]{:S(2)}, u32[]{:S(2)}) collective-permute-start(f32[152,128]{1,0:T(8,128)S(1)} %get-tuple-element.59), channel_id=1, source_target_pairs={{0,1},{1,2},{2,3},{3,4},{4,5},{5,6},{6,7},{7,0},{8,9},{9,10},{10,1... | collective-permute-start | bytes 233480 | tf_op jit(solution)/shard_map/ppermute | solution.py:28
  9.6 7.1 %collective-permute-start.2 = (f32[24,128]{1,0:T(8,128)S(1)}, f32[24,128]{1,0:T(8,128)S(1)}, u32[]{:S(2)}, u32[]{:S(2)}) collective-permute-start(f32[24,128]{1,0:T(8,128)S(1)} %get-tuple-element.66), channel_id=1, source_target_pairs={{0,120},{8,0},{16,8},{24,16},{32,24},{40,32},{48,40},{56,48},{64,5... | collective-permute-start | bytes 36872 | tf_op jit(solution)/shard_map/ppermute | solution.py:28
  14.6 6.7 %collective-permute-start.3 = (f32[24,128]{1,0:T(8,128)S(1)}, f32[24,128]{1,0:T(8,128)S(1)}, u32[]{:S(2)}, u32[]{:S(2)}) collective-permute-start(f32[24,128]{1,0:T(8,128)S(1)} %get-tuple-element.67), channel_id=1, source_target_pairs={{0,8},{8,16},{16,24},{24,32},{32,40},{40,48},{48,56},{56,64},{64,7... | collective-permute-start | bytes 36872 | tf_op jit(solution)/shard_map/ppermute | solution.py:28
  21.3 26.8 %collective-permute-start.10 = (f32[12,112,128]{2,1,0:T(8,128)S(1)}, f32[12,112,128]{2,1,0:T(8,128)S(1)}, u32[]{:S(2)}, u32[]{:S(2)}) collective-permute-start(f32[12,112,128]{2,1,0:T(8,128)S(1)} %get-tuple-element.82), channel_id=1, source_target_pairs={{0,120},{8,0},{16,8},{24,16},{32,24},{40,32},{48,40},{56,48},{64,5... | collective-permute-start | bytes 2064392 | tf_op jit(solution)/shard_map/ppermute | solution.py:28
  22.1 27.6 %collective-permute-start.11 = (f32[12,112,128]{2,1,0:T(8,128)S(1)}, f32[12,112,128]{2,1,0:T(8,128)S(1)}, u32[]{:S(2)}, u32[]{:S(2)}) collective-permute-start(f32[12,112,128]{2,1,0:T(8,128)S(1)} %get-tuple-element.83), channel_id=1, source_target_pairs={{0,8},{8,16},{16,24},{24,32},{32,40},{40,48},{48,56},{56,64},{64,7... | collective-permute-start | bytes 2064392 | tf_op jit(solution)/shard_map/ppermute | solution.py:28
  23.5 6.0 %collective-permute-start.6 = (f32[16,384]{1,0:T(8,128)S(1)}, f32[16,384]{1,0:T(8,128)S(1)}, u32[]{:S(2)}, u32[]{:S(2)}) collective-permute-start(f32[16,384]{1,0:T(8,128)S(1)} %get-tuple-element.76), channel_id=1, source_target_pairs={{0,6},{1,7},{2,0},{3,1},{4,2},{5,3},{6,4},{7,5},{8,14},{9,15},{10,... | collective-permute-start | bytes 73736 | tf_op jit(solution)/shard_map/ppermute | solution.py:28
  26.6 12.5 %collective-permute-start.4 = (f32[32,384]{1,0:T(8,128)S(1)}, f32[32,384]{1,0:T(8,128)S(1)}, u32[]{:S(2)}, u32[]{:S(2)}) collective-permute-start(f32[32,384]{1,0:T(8,128)S(1)} %get-tuple-element.74), channel_id=1, source_target_pairs={{0,7},{1,0},{2,1},{3,2},{4,3},{5,4},{6,5},{7,6},{8,15},{9,8},{10,9... | collective-permute-start | bytes 147464 | tf_op jit(solution)/shard_map/ppermute | solution.py:28
  26.7 16.0 %collective-permute-start.5 = (f32[32,384]{1,0:T(8,128)S(1)}, f32[32,384]{1,0:T(8,128)S(1)}, u32[]{:S(2)}, u32[]{:S(2)}) collective-permute-start(f32[32,384]{1,0:T(8,128)S(1)} %get-tuple-element.75), channel_id=1, source_target_pairs={{0,1},{1,2},{2,3},{3,4},{4,5},{5,6},{6,7},{7,0},{8,9},{9,10},{10,1... | collective-permute-start | bytes 147464 | tf_op jit(solution)/shard_map/ppermute | solution.py:28
  29.5 5.0 %collective-permute-start.7 = (f32[16,384]{1,0:T(8,128)S(1)}, f32[16,384]{1,0:T(8,128)S(1)}, u32[]{:S(2)}, u32[]{:S(2)}) collective-permute-start(f32[16,384]{1,0:T(8,128)S(1)} %get-tuple-element.77), channel_id=1, source_target_pairs={{0,2},{1,3},{2,4},{3,5},{4,6},{5,7},{6,0},{7,1},{8,10},{9,11},{10,... | collective-permute-start | bytes 73736 | tf_op jit(solution)/shard_map/ppermute | solution.py:28
  42.7 10.1 %collective-permute-start.8 = (f32[6,112,128]{2,1,0:T(8,128)S(1)}, f32[6,112,128]{2,1,0:T(8,128)S(1)}, u32[]{:S(2)}, u32[]{:S(2)}) collective-permute-start(f32[6,112,128]{2,1,0:T(8,128)S(1)} %get-tuple-element.78), channel_id=1, source_target_pairs={{0,120},{8,0},{16,8},{24,16},{32,24},{40,32},{48,40},{56,48},{64,5... | collective-permute-start | bytes 1032200 | tf_op jit(solution)/shard_map/ppermute | solution.py:28
  42.7 11.7 %collective-permute-start.9 = (f32[6,112,128]{2,1,0:T(8,128)S(1)}, f32[6,112,128]{2,1,0:T(8,128)S(1)}, u32[]{:S(2)}, u32[]{:S(2)}) collective-permute-start(f32[6,112,128]{2,1,0:T(8,128)S(1)} %get-tuple-element.79), channel_id=1, source_target_pairs={{0,8},{8,16},{16,24},{24,32},{32,40},{40,48},{48,56},{56,64},{64,7... | collective-permute-start | bytes 1032200 | tf_op jit(solution)/shard_map/ppermute | solution.py:28
  43.2 14.8 %collective-permute-start.12 = (f32[8,768]{1,0:T(8,128)S(1)}, f32[8,768]{1,0:T(8,128)S(1)}, u32[]{:S(2)}, u32[]{:S(2)}) collective-permute-start(f32[8,768]{1,0:T(8,128)S(1)} %get-tuple-element.93), channel_id=1, source_target_pairs={{0,120},{8,0},{16,8},{24,16},{32,24},{40,32},{48,40},{56,48},{64,5... | collective-permute-start | bytes 73736 | tf_op jit(solution)/shard_map/ppermute | solution.py:28
  48.1 9.9 %collective-permute-start.13 = (f32[8,768]{1,0:T(8,128)S(1)}, f32[8,768]{1,0:T(8,128)S(1)}, u32[]{:S(2)}, u32[]{:S(2)}) collective-permute-start(f32[8,768]{1,0:T(8,128)S(1)} %get-tuple-element.94), channel_id=1, source_target_pairs={{0,8},{8,16},{16,24},{24,32},{32,40},{40,48},{48,56},{56,64},{64,7... | collective-permute-start | bytes 73736 | tf_op jit(solution)/shard_map/ppermute | solution.py:28

commit v3 on v2

--- a/solution.py
+++ b/solution.py
@@ -21,6 +21,7 @@
 F32 = jnp.float32
 VMEM_LIMIT = 20 * 2**20
 UNROLL = 8
+HEAD_SCALE = 10.0
 
 
 def shift(block, axis, step):
@@ -28,7 +29,7 @@
     return lax.ppermute(block, axis, [(i, (i + step) % count) for i in range(count)])
 
 
-def call(body, outs, args, name, scratch=(), keep=(), raw=(), micros=1.0):
+def call(body, outs, args, name, scratch=(), keep=(), raw=(), away=(), micros=1.0):
     outs = [x if isinstance(x, jax.core.ShapedArray) else jax.ShapeDtypeStruct(x, F32) for x in outs]
     shapes = [x if i in keep else pltpu.VMEM(x.shape, x.dtype) for i, x in enumerate(outs)]
     args = [pltpu.with_memory_space_constraint(x, pltpu.HBM) if i in raw else x for i, x in enumerate(args)]
@@ -37,7 +38,7 @@
         body,
         out_shape=shapes,
         in_specs=[spec(i) for i in range(len(args))],
-        out_specs=[pl.BlockSpec(memory_space=pltpu.VMEM)] * len(outs),
+        out_specs=[pl.BlockSpec(memory_space=pltpu.HBM if i in away else pltpu.VMEM) for i in range(len(outs))],
         scratch_shapes=list(scratch),
         compiler_params=pltpu.CompilerParams(vmem_limit_bytes=VMEM_LIMIT),
         cost_estimate=pl.CostEstimate(flops=0, bytes_accessed=int(micros * 3.5e6), transcendentals=0),
@@ -290,21 +291,24 @@
                 right_at, left_at = (8, 0) if h == 0 else (0, 8)
                 source = 16 * e + half + jnp.where(y < 0, left_at + 8 + y, right_at + y - 128)
                 picks.append(((y < 0) | (y >= 128), jnp.clip(source, 0, 127)))
-    ways = ((first_low, first_high, 6), (then_low, then_high, 0), (first_low, first_high, 0))
+    ways = ((first_low, first_high, 3), (then_low, then_high, 0), (first_low, first_high, 0))
     for a, (ref, (to_low, to_high, start)) in enumerate(zip((head, salt, cond), ways)):
-        def eight(q, _, a=a, ref=ref, to_low=to_low, to_high=to_high, start=start):
-            at = pl.multiple_of((a * 6 + q) * 8, 8)
-            r, l = right[pl.ds(at, 8), :], left[pl.ds(at, 8), :]
-            rims = (jnp.where(odd, r, l), jnp.where(odd, l, r))
-            for m in range(18):
-                there, source = picks[m]
-                x = jnp.where(there, take(rims[m // 9], source), ref[q, m])
-                full[a * 6 + q, m] = x
-                to_low[start + q, 6 * m : 6 * m + 6, :] = x[0:6]
-                to_high[start + q, 6 * m : 6 * m + 6, :] = x[2:8]
+        def sixteen(pair, _, a=a, ref=ref, to_low=to_low, to_high=to_high, start=start):
+            for part in range(2):
+                q = 2 * pair + part
+                at = pl.multiple_of((a * 6 + q) * 8, 8)
+                r, l = right[pl.ds(at, 8), :], left[pl.ds(at, 8), :]
+                rims = (jnp.where(odd, r, l), jnp.where(odd, l, r))
+                for m in range(18):
+                    there, source = picks[m]
+                    x = jnp.where(there, take(rims[m // 9], source), ref[q, m])
+                    full[a * 6 + q, m] = x
+                    row = 108 * part + 6 * m
+                    to_low[start + pair, row : row + 6, :] = x[0:6]
+                    to_high[start + pair, row : row + 6, :] = x[2:8]
             return 0
 
-        lax.fori_loop(0, 6, eight, 0)
+        lax.fori_loop(0, 3, sixteen, 0)
 
 
 def fourth(x, inner):
@@ -382,7 +386,7 @@
         f, g = [], []
         for i in range(len(h)):
             dh = hs[i] - h[i]
-            moved = dh * jnp.where(dh > 0, cs[i], c[i]) + spread_side * (cs[i] - c[i])
+            moved = dh * jnp.where(dh > 0, cs[i], c[i]) + (cs[i] - c[i])
             f.append(w[i] * dh)
             g.append(w[i] * moved)
         fb, gb = back(f), back(g)
@@ -421,21 +425,26 @@
     return [jnp.zeros((8, 128), F32)] * n
 
 
+def scaled(t):
+    return [HEAD_SCALE * x for x in t]
+
+
 def tilt():
-    size = 0.5 * density_slope
+    size = 0.5 * HEAD_SCALE * density_slope
     return jnp.where(lanes((8, 128)) < 64, size, -size).astype(F32)
 
 
 def unfold(a, rim, high, low, start, ext, stage):
     inner = jnp.bitwise_and(lanes((8, 128)), 63)
 
-    def eight(q, _):
-        block = start + q
+    def eight(q, pair, part):
+        block = start + pair
+        first = 108 * part
         for m in range(18):
-            stage[m, 0:4, :] = high[block, 6 * m : 6 * m + 4, :]
-            stage[m, 4:8, :] = low[block, 6 * m + 2 : 6 * m + 6, :]
-            stage[m, 8:10, :] = high[block, 6 * m + 4 : 6 * m + 6, :]
-            stage[m, 14:16, :] = low[block, 6 * m : 6 * m + 2, :]
+            stage[m, 0:4, :] = high[block, first + 6 * m : first + 6 * m + 4, :]
+            stage[m, 4:8, :] = low[block, first + 6 * m + 2 : first + 6 * m + 6, :]
+            stage[m, 8:10, :] = high[block, first + 6 * m + 4 : first + 6 * m + 6, :]
+            stage[m, 14:16, :] = low[block, first + 6 * m : first + 6 * m + 2, :]
         for h in range(2):
             for e in range(4):
                 ext[q * 8 + 4 * h + e, 0:24, :] = rim[a * 48 + q * 8 + 4 * h + e, 0:24, :]
@@ -447,15 +456,19 @@
                     at = 24 * (i + 1) + 8 * j
                     for e in range(4):
                         ext[q * 8 + 4 * h + e, at : at + 8, :] = x[e]
+
+    def sixteen(pair, _):
+        for part in range(2):
+            eight(2 * pair + part, pair, part)
         return 0
 
     stage[...] = jnp.zeros(stage.shape, F32)
-    lax.fori_loop(0, ext.shape[0] // 8, eight, 0)
+    lax.fori_loop(0, ext.shape[0] // 16, sixteen, 0)
 
 
 def weights(rim, high, low, head, wx, wy, vv, cond, stage):
     unfold(2, rim, high, low, 0, cond, stage)
-    unfold(0, rim, high, low, 6, head, stage)
+    unfold(0, rim, high, low, 3, head, stage)
     steps = head.shape[0]
     n = 3 * J
     lane = lanes((8, 128))
@@ -497,17 +510,17 @@
     def one(at, carry, inmost=False):
         c, lift_above = carry
         c_in = swap(c) if inmost else get(salt, at + 1, n)
-        h = get(head, at, n)
+        h = scaled(get(head, at, n))
         lift = [(weigh * b) * (p + q) for b, p, q in zip(get(vv, at, n), c, c_in)]
         flow, moved = sides_of(h, c, get(wx, at, n), get(wy, at, n))
         put(part, at, [a + b - p + q for a, b, p, q in zip(h, flow, lift, lift_above)])
-        put(side, at, [porosity * a + b for a, b in zip(c, moved)])
+        put(side, at, [HEAD_SCALE * porosity * a + b for a, b in zip(c, moved)])
         return c_in, lift
 
     one(steps - 1, sweep(0, steps - 1, one, (get(salt, 0, n), zeros(n)), 4), True)
 
 
-def aquifer(part0, side0, salt0, wx, wy, vv, gathered, leak_high, leak_low, head_out, salt_out, hy, cz, ss, ip, uu, iq, kk, mid, leak):
+def aquifer(part0, side0, salt0, wx, wy, vv, gathered, leak_high, leak_low, head_to, salt_to, hy, cz, ss, ip, uu, iq, kk, mid, leak, head_out, salt_out, sems):
     steps = salt0.shape[0]
     layers = 2 * steps
     lane = lanes((8, 128))
@@ -537,7 +550,7 @@
         return out
 
     n = 3 * J
-    total, level = leak_of(0, n), leak_of(1, n)
+    total, level = leak_of(0, n), scaled(leak_of(1, n))
 
     def pivots(at, carry):
         p, q, flow = carry
@@ -548,33 +561,20 @@
         put(uu, at, u)
         y = [(a + b) * i for a, b, i in zip(get(part0, at, n), flow, inverse)]
         put(hy, at, y)
-        inverse = [1.0 / (a + spread_vertical * b) for a, b in zip(q, v)]
-        k = [spread_vertical * a * b for a, b in zip(v, inverse)]
+        inverse = [1.0 / (a + b) for a, b in zip(q, v)]
+        k = [a * b for a, b in zip(v, inverse)]
         put(iq, at, inverse)
         put(kk, at, k)
         return (
             [1.0 + a * (1.0 - b) for a, b in zip(v, u)],
-            [porosity + spread_vertical * a * (1.0 - b) for a, b in zip(v, k)],
+            [HEAD_SCALE * porosity + a * (1.0 - b) for a, b in zip(v, k)],
             [a * b for a, b in zip(v, y)],
         )
 
-    sweep(0, steps, pivots, ([1.0 + x for x in total], [porosity + x for x in total], level))
+    sweep(0, steps, pivots, ([1.0 + x for x in total], [HEAD_SCALE * porosity + HEAD_SCALE * x for x in total], level))
     for place, ref in enumerate((uu, kk)):
         u = get(ref, steps - 1, n)
         put(mid, place, [1.0 / (1.0 - a * b) for a, b in zip(u, swap(u))])
-
-    def outward(state, ratio, place, n):
-        y, u = get(state, steps - 1, n), get(ratio, steps - 1, n)
-        x = [(a + b * c) * d for a, b, c, d in zip(y, u, swap(y), get(mid, place, n))]
-        put(state, steps - 1, x)
-
-        def back(t, x):
-            at = steps - 2 - t
-            x = [a + b * c for a, b, c in zip(get(state, at, n), get(ratio, at, n), x)]
-            put(state, at, x)
-            return x
-
-        sweep(0, steps - 1, back, x)
 
     in_order = [jnp.right_shift((lane + 8 - j) * 21846, 16) for j in range(J)]
     owner = lane + 8 - 3 * jnp.right_shift((lane + 8) * 21846, 16)
@@ -584,6 +584,24 @@
             y = [take(z, jnp.clip(index, 0, 63) + 64 * end) for z, index in zip(x, in_order)]
             layer = at if end == 0 else layers - 1 - at
             out[layer] = jnp.where(owner == 0, y[0], jnp.where(owner == 1, y[1], y[2]))
+
+    def outward(state, ratio, place, n, out=None):
+        y, u = get(state, steps - 1, n), get(ratio, steps - 1, n)
+        x = [(a + b * c) * d for a, b, c, d in zip(y, u, swap(y), get(mid, place, n))]
+        put(state, steps - 1, x)
+        if out is not None:
+            write(out, steps - 1, x)
+
+        def back(t, x):
+            at = steps - 2 - t
+            x = [a + b * c for a, b, c in zip(get(state, at, n), get(ratio, at, n), x)]
+            if out is None:
+                put(state, at, x)
+            else:
+                write(out, at, x)
+            return x
+
+        sweep(0, steps - 1, back, x, steps - 1)
 
     for step in range(AQ_ITERS):
         last = step == AQ_ITERS - 1
@@ -603,10 +621,10 @@
                     for a, b, p, q, r, i in zip(h, flow, lift, lift_above, flow_above, get(ip, at, n))
                 ]
                 put(hy, at, y)
-                put(ss, at, [porosity * a + b for a, b in zip(c[:n], moved)])
+                put(ss, at, [HEAD_SCALE * porosity * a + b for a, b in zip(c[:n], moved)])
                 return c_in, lift, [a * b for a, b in zip(v, y)]
 
-            carry = sweep(0, steps - 1, inward, (get(cz, 0, n_in), zeros(n), leak_of(1, n)))
+            carry = sweep(0, steps - 1, inward, (get(cz, 0, n_in), zeros(n), scaled(leak_of(1, n))))
             inward(steps - 1, carry, inmost=True)
         outward(hy, uu, 0, n)
 
@@ -628,14 +646,19 @@
             ]
             put(cz, at, z)
             if last:
-                write(head_out, at, h)
-            return h_in, c_in, carried, [spread_vertical * x * y for x, y in zip(v, z)]
-
-        carry = sweep(0, steps - 1, salt_inward, (get(hy, 0, n), get(salt, 0, n), zeros(n), leak_of(2, n)))
+                write(head_out, at, [spread_side * x for x in h])
+            return h_in, c_in, carried, [x * y for x, y in zip(v, z)]
+
+        carry = sweep(0, steps - 1, salt_inward, (get(hy, 0, n), get(salt, 0, n), zeros(n), scaled(leak_of(2, n))), 16)
         salt_inward(steps - 1, carry, inmost=True)
-        outward(cz, kk, 1, n)
-
-    sweep(0, steps, lambda at, _: write(salt_out, at, get(cz, at, J)) or 0, 0)
+        if last:
+            head_copy = pltpu.make_async_copy(head_out, head_to, sems.at[0])
+            head_copy.start()
+        outward(cz, kk, 1, n, salt_out if last else None)
+    salt_copy = pltpu.make_async_copy(salt_out, salt_to, sems.at[1])
+    salt_copy.start()
+    head_copy.wait()
+    salt_copy.wait()
 
 
 def whole(steps):
@@ -673,8 +696,11 @@
         [(2 * steps, 8, 128)] * 2,
         args,
         "aquifer",
-        scratch=[pltpu.VMEM(whole(steps), F32)] * 7 + [pltpu.VMEM((2, 24 * J, 128), F32), pltpu.VMEM((24, 768), F32)],
+        scratch=[pltpu.VMEM(whole(steps), F32)] * 7 + [pltpu.VMEM((2, 24 * J, 128), F32), pltpu.VMEM((24, 768), F32)]
+        + [pltpu.VMEM((2 * steps, 8, 128), F32)] * 2
+        + [pltpu.SemaphoreType.DMA((2,))],
         keep=(0, 1),
+        away=(0, 1),
         micros=20.0,
     )
 
@@ -704,7 +730,7 @@
     blocks = 3 * steps // 8
     full, *coast = call(
         pack_coast,
-        [(blocks, 18, 8, 128)] + [(blocks // 3 * 2, 112, 128)] * 2 + [(blocks // 3, 112, 128)] * 2,
+        [(blocks, 18, 8, 128)] + [(blocks // 3, 216, 128)] * 2 + [(blocks // 6, 216, 128)] * 2,
         (*tiles, right, left),
         "pack_coast",
         micros=3.0,
@@ -725,7 +751,7 @@
     leak_left = shift(to_high, "gy", 1)
     leak_right2 = shift(to_low2, "gy", -2)
     leak_left2 = shift(to_high2, "gy", 2)
-    then_low, then_high = behind(coast[2:], leak_right, leak_left, leak_right2, leak_left2)
+    then_low, then_high = behind(coast[2:], leak_right, leak_left, leak_right2, leak_left2, rims)
     then = shift(then_low, "gx", -1), shift(then_high, "gx", 1)
     head, *links = run_weights(rims, *first)
     ready = run_prepare(rims, *then, head, *links)

time: 78.7 us -> 75.5 us (0.959)
  Pallas kernels: 37.5 us -> 34.6 us
    pallas_call x10, Pallas kernels: 37.5 us -> 34.6 us  [call(): pl.pallas_call(body, out_shape=shapes, in_specs=[spec(i) for i in range(l...]
where the time goes in v3:
time: 75.5 us; the launch traced here: 75.4 us
  Pallas kernels  34.6 us (46%)
  waiting for transfers between devices  20 us (26%)
  starting transfers between devices  19.9 us (26%)
  between operations  0.88 us (1%)
    pallas_call x10, Pallas kernels, call(): pl.pallas_call(body, out_shape=shapes, in_specs=[spec(i) for i in range(l...  34.6 us
    ppermute x14, waiting for transfers between devices, shift(): lax.ppermute(block, axis, [(i, (i + step) % count) for i in range(count)])  20 us
    ppermute x14, starting transfers between devices, shift(): lax.ppermute(block, axis, [(i, (i + step) % count) for i in range(count)])  19.9 us
  transfers between devices with their start and end apart: 14, of which 6 were waited for; matrix products, arithmetic and copies ran while one was open for 0% of the time, Pallas kernels for 19%

profile of v3, /device:TPU:8, one launch (start us, length us, event | category | flops | bytes accessed | tf_op | source)
XLA Modules:
  0.0 75.4 jit_solution(8649620341886287357)
XLA Ops:
  0.6 1.9 %pack_inland.1 = (f32[152,128]{1,0:T(8,128)S(1)}, f32[152,128]{1,0:T(8,128)S(1)}, f32[8,128]{1,0:T(8,128)S(1)}, f32[8,128]{1,0:T(8,128)S(1)}, f32[128,128]{1,0:T...) custom-call(f32[128,128]{1,0:T(8,128)} %refs_0_.1, ...), custom_call_target="tpu_custom_call" | custom-call | bytes 10500000 | tf_op jit(solution)/shard_map/pack_inland/pallas_call | solution.py:37
  2.5 0.4 collective-permute-start
  3.0 2.6 %collective-permute-start.1 = (f32[152,128]{1,0:T(8,128)S(1)}, f32[152,128]{1,0:T(8,128)S(1)}, u32[]{:S(2)}, u32[]{:S(2)}) collective-permute-start(f32[152,128]{1,0:T(8,128)S(1)} %get-tuple-element.59), channel_id=1, source_target_pairs={{0,1},{1,2},{2,3},{3,4},{4,5},{5,6},{6,7},{7,0},{8,9},{9,10},{10,1... | collective-permute-start | bytes 233480 | tf_op jit(solution)/shard_map/ppermute | solution.py:29
  5.5 3.4 %interleave.1 = (f32[6,18,8,128]{3,2,1,0:T(8,128)S(1)}, f32[6,18,8,128]{3,2,1,0:T(8,128)S(1)}, f32[6,18,8,128]{3,2,1,0:T(8,128)S(1)}) custom-call(f32[96,8,128]{2,1,0:T(8,128)S(1)} %get-tuple-element.62.head, f32[96,8,128]{2,1,0:T(8,128)S(1)} %get-tuple-element.63.salt, f32[96,8,128]{2,1,0:T(8,128)S(1)} %get-tuple-element.64.cond), custom_call_target="tpu_custom_call" | custom-call | bytes 14000000 | tf_op jit(solution)/shard_map/interleave/pallas_call | solution.py:37
  8.9 0.0 collective-permute-done.right
  8.9 0.6 collective-permute-done.1.left
  9.6 5.0 %collective-permute-start.2 = (f32[24,128]{1,0:T(8,128)S(1)}, f32[24,128]{1,0:T(8,128)S(1)}, u32[]{:S(2)}, u32[]{:S(2)}) collective-permute-start(f32[24,128]{1,0:T(8,128)S(1)} %get-tuple-element.66), channel_id=1, source_target_pairs={{0,120},{8,0},{16,8},{24,16},{32,24},{40,32},{48,40},{56,48},{64,5... | collective-permute-start | bytes 36872 | tf_op jit(solution)/shard_map/ppermute | solution.py:29
  14.6 0.0 collective-permute-start.3
  14.6 1.5 %pack_coast.1 = (f32[18,18,8,128]{3,2,1,0:T(8,128)S(1)}, f32[6,216,128]{2,1,0:T(8,128)S(1)}, f32[6,216,128]{2,1,0:T(8,128)S(1)}, f32[3,216,128]{2,1,0:T(8,128)S(1)}, f32[3,216,128]{2,1,0:T(8,128)S(1)}) custom-call(f32[6,18,8,128]{3,2,1,0:T(8,128)S(1)} %get-tuple-element.65.after.head, f32[6,18,8,128]{3,2,1,0:T(8,128)S(1)} %get-tuple-element.69.salt, ...), custom_call_target="tpu_custom_call" | custom-call | bytes 10500000 | tf_op jit(solution)/shard_map/pack_coast/pallas_call | solution.py:37
  16.1 0.0 collective-permute-done.2.above.refs_2_
  16.1 5.2 %collective-permute-done.3.below.refs_3_ = f32[24,128]{1,0:T(8,128)S(1)} collective-permute-done((f32[24,128]{1,0:T(8,128)S(1)}, f32[24,128]{1,0:T(8,128)S(1)}, u32[]{:S(2)}, u32[]{:S(2)}) %collective-permute-start.3) | collective-permute-done | bytes 12320 | tf_op jit(solution)/shard_map/ppermute | solution.py:29
  21.3 0.2 collective-permute-start.10
  21.5 0.3 collective-permute-start.11
  21.8 1.4 %surface.1 = (f32[128,128]{1,0:T(8,128)}, f32[32,384]{1,0:T(8,128)S(1)}, f32[32,384]{1,0:T(8,128)S(1)}, f32[16,384]{1,0:T(8,128)S(1)}, f32[16,384]{1,0:T(8,128)S(1)}, /*index=5*/f32[16,768]{1,0:T(8,128)S(1)}) custom-call(f32[128,128]{1,0:T(8,128)S(1)} %get-tuple-element.50.depth, f32[128,128]{1,0:T(8,128)S(1)} %get-tuple-element.51.bed, ...), custom_call_target="tpu_custom_call" | custom-call | bytes 5250000 | tf_op jit(solution)/shard_map/surface/pallas_call | solution.py:37
  23.2 3.1 %collective-permute-start.6 = (f32[16,384]{1,0:T(8,128)S(1)}, f32[16,384]{1,0:T(8,128)S(1)}, u32[]{:S(2)}, u32[]{:S(2)}) collective-permute-start(f32[16,384]{1,0:T(8,128)S(1)} %get-tuple-element.76), channel_id=1, source_target_pairs={{0,6},{1,7},{2,0},{3,1},{4,2},{5,3},{6,4},{7,5},{8,14},{9,15},{10,... | collective-permute-start | bytes 73736 | tf_op jit(solution)/shard_map/ppermute | solution.py:29
  26.3 0.1 collective-permute-start.4
  26.4 2.8 %collective-permute-start.5 = (f32[32,384]{1,0:T(8,128)S(1)}, f32[32,384]{1,0:T(8,128)S(1)}, u32[]{:S(2)}, u32[]{:S(2)}) collective-permute-start(f32[32,384]{1,0:T(8,128)S(1)} %get-tuple-element.75), channel_id=1, source_target_pairs={{0,1},{1,2},{2,3},{3,4},{4,5},{5,6},{6,7},{7,0},{8,9},{9,10},{10,1... | collective-permute-start | bytes 147464 | tf_op jit(solution)/shard_map/ppermute | solution.py:29
  29.2 0.0 collective-permute-done.6.refs_4_.right2
  29.2 0.0 collective-permute-start.7
  29.2 1.6 %open_tile.1.refs_6_.rim = f32[144,24,128]{2,1,0:T(8,128)S(1)} custom-call(f32[18,18,8,128]{3,2,1,0:T(8,128)S(1)} %get-tuple-element.71.full), custom_call_target="tpu_custom_call" | custom-call | bytes 10500000 | tf_op jit(solution)/shard_map/open_tile/pallas_call | solution.py:37
  30.8 3.5 %collective-permute-done.7.refs_5_.left2 = f32[16,384]{1,0:T(8,128)S(1)} collective-permute-done((f32[16,384]{1,0:T(8,128)S(1)}, f32[16,384]{1,0:T(8,128)S(1)}, u32[]{:S(2)}, u32[]{:S(2)}) %collective-permute-start.7) | collective-permute-done | bytes 24608 | tf_op jit(solution)/shard_map/ppermute | solution.py:29
  34.3 4.3 %collective-permute-done.4.refs_2_.right = f32[32,384]{1,0:T(8,128)S(1)} collective-permute-done((f32[32,384]{1,0:T(8,128)S(1)}, f32[32,384]{1,0:T(8,128)S(1)}, u32[]{:S(2)}, u32[]{:S(2)}) %collective-permute-start.4) | collective-permute-done | bytes 49184 | tf_op jit(solution)/shard_map/ppermute | solution.py:29
  38.5 3.6 %collective-permute-done.5.refs_3_.left = f32[32,384]{1,0:T(8,128)S(1)} collective-permute-done((f32[32,384]{1,0:T(8,128)S(1)}, f32[32,384]{1,0:T(8,128)S(1)}, u32[]{:S(2)}, u32[]{:S(2)}) %collective-permute-start.5) | collective-permute-done | bytes 49184 | tf_op jit(solution)/shard_map/ppermute | solution.py:29
  42.1 0.0 collective-permute-start.8
  42.1 0.5 collective-permute-start.9
  42.7 4.9 %collective-permute-start.12 = (f32[8,768]{1,0:T(8,128)S(1)}, f32[8,768]{1,0:T(8,128)S(1)}, u32[]{:S(2)}, u32[]{:S(2)}) collective-permute-start(f32[8,768]{1,0:T(8,128)S(1)} %get-tuple-element.93), channel_id=1, source_target_pairs={{0,120},{8,0},{16,8},{24,16},{32,24},{40,32},{48,40},{56,48},{64,5... | collective-permute-start | bytes 73736 | tf_op jit(solution)/shard_map/ppermute | solution.py:29
  47.6 0.0 collective-permute-done.10.high
  47.6 0.0 collective-permute-start.13
  47.6 0.0 collective-permute-done.11.low
  47.6 2.7 %weights.1 = (f32[48,72,128]{2,1,0:T(8,128)S(1)}, f32[48,72,128]{2,1,0:T(8,128)S(1)}, f32[48,72,128]{2,1,0:T(8,128)S(1)}, f32[48,72,128]{2,1,0:T(8,128)S(1)}) custom-call(f32[144,24,128]{2,1,0:T(8,128)S(1)} %open_tile.1.refs_6_.rim, f32[6,216,128]{2,1,0:T(8,128)S(1)} %collective-permute-done.10.high, f32[6,216,128]{2,1,0:T(8,128)S(1)} %collective-permute-done.11.low), custom_call_target="tpu_custom_call" | custom-call | bytes 14000000 | tf_op jit(solution)/shard_map/weights/pallas_call | solution.py:37
  50.3 0.0 collective-permute-done.8.high
  50.3 2.8 %collective-permute-done.9.low = f32[3,216,128]{2,1,0:T(8,128)S(1)} collective-permute-done((f32[3,216,128]{2,1,0:T(8,128)S(1)}, f32[3,216,128]{2,1,0:T(8,128)S(1)}, u32[]{:S(2)}, u32[]{:S(2)}) %collective-permute-start.9) | collective-permute-done | bytes 331808 | tf_op jit(solution)/shard_map/ppermute | solution.py:29
  53.0 3.5 %prepare.1 = (f32[48,72,128]{2,1,0:T(8,128)S(1)}, f32[48,72,128]{2,1,0:T(8,128)S(1)}, f32[48,72,128]{2,1,0:T(8,128)S(1)}) custom-call(f32[144,24,128]{2,1,0:T(8,128)S(1)} %open_tile.1.refs_6_.rim, f32[3,216,128]{2,1,0:T(8,128)S(1)} %collective-permute-done.8.high, f32[3,216,128]{2,1,0:T(8,128)S(1)} %collective-permute-done.9.low, ...), custom_call_target="tpu_custom_call" | custom-call | bytes 14000000 | tf_op jit(solution)/shard_map/prepare/pallas_call | solution.py:37
  56.6 0.0 collective-permute-done.12.leak_high
  56.6 0.0 collective-permute-done.13.leak_low
  56.6 18.6 %aquifer.1 = (f32[96,8,128]{2,1,0:T(8,128)}, f32[96,8,128]{2,1,0:T(8,128)}) custom-call(f32[48,72,128]{2,1,0:T(8,128)S(1)} %get-tuple-element.88.part0, f32[48,72,128]{2,1,0:T(8,128)S(1)} %get-tuple-element.89.side0, f32[48,72,128]{2,1,0:T(8,128)S(1)} %get-tuple-element.90.salt0, f32[48,72,128]{2,1,0:T(8,128)S(1)} %get-tuple-element.85.wx, ...), custom_call_target="tpu_custom_call" | custom-call | bytes 70000000 | tf_op jit(solution)/shard_map/aquifer/pallas_call | solution.py:37
  (4 shorter events, 0.0 us)
Async XLA Ops:
  2.5 6.4 %collective-permute-start = (f32[152,128]{1,0:T(8,128)S(1)}, f32[152,128]{1,0:T(8,128)S(1)}, u32[]{:S(2)}, u32[]{:S(2)}) collective-permute-start(f32[152,128]{1,0:T(8,128)S(1)} %get-tuple-element.58), channel_id=1, source_target_pairs={{0,7},{1,0},{2,1},{3,2},{4,3},{5,4},{6,5},{7,6},{8,15},{9,8},{10,9... | collective-permute-start | bytes 233480 | tf_op jit(solution)/shard_map/ppermute | solution.py:29
  3.0 6.6 %collective-permute-start.1 = (f32[152,128]{1,0:T(8,128)S(1)}, f32[152,128]{1,0:T(8,128)S(1)}, u32[]{:S(2)}, u32[]{:S(2)}) collective-permute-start(f32[152,128]{1,0:T(8,128)S(1)} %get-tuple-element.59), channel_id=1, source_target_pairs={{0,1},{1,2},{2,3},{3,4},{4,5},{5,6},{6,7},{7,0},{8,9},{9,10},{10,1... | collective-permute-start | bytes 233480 | tf_op jit(solution)/shard_map/ppermute | solution.py:29
  9.6 6.5 %collective-permute-start.2 = (f32[24,128]{1,0:T(8,128)S(1)}, f32[24,128]{1,0:T(8,128)S(1)}, u32[]{:S(2)}, u32[]{:S(2)}) collective-permute-start(f32[24,128]{1,0:T(8,128)S(1)} %get-tuple-element.66), channel_id=1, source_target_pairs={{0,120},{8,0},{16,8},{24,16},{32,24},{40,32},{48,40},{56,48},{64,5... | collective-permute-start | bytes 36872 | tf_op jit(solution)/shard_map/ppermute | solution.py:29
  14.6 6.7 %collective-permute-start.3 = (f32[24,128]{1,0:T(8,128)S(1)}, f32[24,128]{1,0:T(8,128)S(1)}, u32[]{:S(2)}, u32[]{:S(2)}) collective-permute-start(f32[24,128]{1,0:T(8,128)S(1)} %get-tuple-element.67), channel_id=1, source_target_pairs={{0,8},{8,16},{16,24},{24,32},{32,40},{40,48},{48,56},{56,64},{64,7... | collective-permute-start | bytes 36872 | tf_op jit(solution)/shard_map/ppermute | solution.py:29
  21.3 26.3 %collective-permute-start.10 = (f32[6,216,128]{2,1,0:T(8,128)S(1)}, f32[6,216,128]{2,1,0:T(8,128)S(1)}, u32[]{:S(2)}, u32[]{:S(2)}) collective-permute-start(f32[6,216,128]{2,1,0:T(8,128)S(1)} %get-tuple-element.82), channel_id=1, source_target_pairs={{0,120},{8,0},{16,8},{24,16},{32,24},{40,32},{48,40},{56,48},{64,5... | collective-permute-start | bytes 1990664 | tf_op jit(solution)/shard_map/ppermute | solution.py:29
  21.5 26.1 %collective-permute-start.11 = (f32[6,216,128]{2,1,0:T(8,128)S(1)}, f32[6,216,128]{2,1,0:T(8,128)S(1)}, u32[]{:S(2)}, u32[]{:S(2)}) collective-permute-start(f32[6,216,128]{2,1,0:T(8,128)S(1)} %get-tuple-element.83), channel_id=1, source_target_pairs={{0,8},{8,16},{16,24},{24,32},{32,40},{40,48},{48,56},{56,64},{64,7... | collective-permute-start | bytes 1990664 | tf_op jit(solution)/shard_map/ppermute | solution.py:29
  23.2 6.0 %collective-permute-start.6 = (f32[16,384]{1,0:T(8,128)S(1)}, f32[16,384]{1,0:T(8,128)S(1)}, u32[]{:S(2)}, u32[]{:S(2)}) collective-permute-start(f32[16,384]{1,0:T(8,128)S(1)} %get-tuple-element.76), channel_id=1, source_target_pairs={{0,6},{1,7},{2,0},{3,1},{4,2},{5,3},{6,4},{7,5},{8,14},{9,15},{10,... | collective-permute-start | bytes 73736 | tf_op jit(solution)/shard_map/ppermute | solution.py:29
  26.3 12.2 %collective-permute-start.4 = (f32[32,384]{1,0:T(8,128)S(1)}, f32[32,384]{1,0:T(8,128)S(1)}, u32[]{:S(2)}, u32[]{:S(2)}) collective-permute-start(f32[32,384]{1,0:T(8,128)S(1)} %get-tuple-element.74), channel_id=1, source_target_pairs={{0,7},{1,0},{2,1},{3,2},{4,3},{5,4},{6,5},{7,6},{8,15},{9,8},{10,9... | collective-permute-start | bytes 147464 | tf_op jit(solution)/shard_map/ppermute | solution.py:29
  26.4 15.8 %collective-permute-start.5 = (f32[32,384]{1,0:T(8,128)S(1)}, f32[32,384]{1,0:T(8,128)S(1)}, u32[]{:S(2)}, u32[]{:S(2)}) collective-permute-start(f32[32,384]{1,0:T(8,128)S(1)} %get-tuple-element.75), channel_id=1, source_target_pairs={{0,1},{1,2},{2,3},{3,4},{4,5},{5,6},{6,7},{7,0},{8,9},{9,10},{10,1... | collective-permute-start | bytes 147464 | tf_op jit(solution)/shard_map/ppermute | solution.py:29
  29.2 5.0 %collective-permute-start.7 = (f32[16,384]{1,0:T(8,128)S(1)}, f32[16,384]{1,0:T(8,128)S(1)}, u32[]{:S(2)}, u32[]{:S(2)}) collective-permute-start(f32[16,384]{1,0:T(8,128)S(1)} %get-tuple-element.77), channel_id=1, source_target_pairs={{0,2},{1,3},{2,4},{3,5},{4,6},{5,7},{6,0},{7,1},{8,10},{9,11},{10,... | collective-permute-start | bytes 73736 | tf_op jit(solution)/shard_map/ppermute | solution.py:29
  42.1 8.2 %collective-permute-start.8 = (f32[3,216,128]{2,1,0:T(8,128)S(1)}, f32[3,216,128]{2,1,0:T(8,128)S(1)}, u32[]{:S(2)}, u32[]{:S(2)}) collective-permute-start(f32[3,216,128]{2,1,0:T(8,128)S(1)} %get-tuple-element.78), channel_id=1, source_target_pairs={{0,120},{8,0},{16,8},{24,16},{32,24},{40,32},{48,40},{56,48},{64,5... | collective-permute-start | bytes 995336 | tf_op jit(solution)/shard_map/ppermute | solution.py:29
  42.1 10.9 %collective-permute-start.9 = (f32[3,216,128]{2,1,0:T(8,128)S(1)}, f32[3,216,128]{2,1,0:T(8,128)S(1)}, u32[]{:S(2)}, u32[]{:S(2)}) collective-permute-start(f32[3,216,128]{2,1,0:T(8,128)S(1)} %get-tuple-element.79), channel_id=1, source_target_pairs={{0,8},{8,16},{16,24},{24,32},{32,40},{40,48},{48,56},{56,64},{64,7... | collective-permute-start | bytes 995336 | tf_op jit(solution)/shard_map/ppermute | solution.py:29
  42.7 13.9 %collective-permute-start.12 = (f32[8,768]{1,0:T(8,128)S(1)}, f32[8,768]{1,0:T(8,128)S(1)}, u32[]{:S(2)}, u32[]{:S(2)}) collective-permute-start(f32[8,768]{1,0:T(8,128)S(1)} %get-tuple-element.93), channel_id=1, source_target_pairs={{0,120},{8,0},{16,8},{24,16},{32,24},{40,32},{48,40},{56,48},{64,5... | collective-permute-start | bytes 73736 | tf_op jit(solution)/shard_map/ppermute | solution.py:29
  47.6 9.0 %collective-permute-start.13 = (f32[8,768]{1,0:T(8,128)S(1)}, f32[8,768]{1,0:T(8,128)S(1)}, u32[]{:S(2)}, u32[]{:S(2)}) collective-permute-start(f32[8,768]{1,0:T(8,128)S(1)} %get-tuple-element.94), channel_id=1, source_target_pairs={{0,8},{8,16},{16,24},{24,32},{32,40},{40,48},{48,56},{56,64},{64,7... | collective-permute-start | bytes 73736 | tf_op jit(solution)/shard_map/ppermute | solution.py:29

commit v4 on v3

--- a/solution.py
+++ b/solution.py
@@ -466,7 +466,7 @@
     lax.fori_loop(0, ext.shape[0] // 16, sixteen, 0)
 
 
-def weights(rim, high, low, head, wx, wy, vv, cond, stage):
+def weights(rim, high, low, wx, wy, vv, fx, fy, base, head, cond, stage):
     unfold(2, rim, high, low, 0, cond, stage)
     unfold(0, rim, high, low, 3, head, stage)
     steps = head.shape[0]
@@ -493,28 +493,40 @@
     def one(at, k, inmost=False):
         k_in = swap(k) if inmost else known(at + 1)
         rock = [jnp.sqrt(x) * m for m, x in zip(masks, k)]
-        put(wx, at, [time_step * a * b for a, b in zip(rock, up(rock))])
-        put(wy, at, [time_step * a * b for a, b in zip(rock, nxt(rock))])
+        x = [time_step * a * b for a, b in zip(rock, up(rock))]
+        y = [time_step * a * b for a, b in zip(rock, nxt(rock))]
+        put(wx, at, x)
+        put(wy, at, y)
         put(vv, at, [2.0 * a * b / (a + b) for a, b in zip(k, k_in)])
+        h = scaled(get(head, at, n))
+        x = [w * (a - b) for w, a, b in zip(x, up(h), h)]
+        y = [w * (a - b) for w, a, b in zip(y, nxt(h), h)]
+        put(fx, at, x)
+        put(fy, at, y)
+        put(base, at, [a + (b - p) + (c - q) for a, b, p, c, q in zip(h, x, down(x), y, prv(y))])
         return k_in
 
     one(steps - 1, sweep(0, steps - 1, one, known(0), 4), True)
 
 
-def prepare(rim, high, low, head, wx, wy, vv, part, side, salt, stage):
+def prepare(rim, high, low, wx, wy, vv, fx, fy, base, part, side, salt, stage):
     unfold(1, rim, high, low, 0, salt, stage)
     steps = salt.shape[0]
     n = 3 * J
     weigh = tilt()
 
+    def carried(w, f, c, ahead, back):
+        g = [p * jnp.where(p > 0, a, b) + q * (a - b) for p, q, a, b in zip(f, w, ahead(c), c)]
+        return [a - b for a, b in zip(g, back(g))]
+
     def one(at, carry, inmost=False):
         c, lift_above = carry
         c_in = swap(c) if inmost else get(salt, at + 1, n)
-        h = scaled(get(head, at, n))
         lift = [(weigh * b) * (p + q) for b, p, q in zip(get(vv, at, n), c, c_in)]
-        flow, moved = sides_of(h, c, get(wx, at, n), get(wy, at, n))
-        put(part, at, [a + b - p + q for a, b, p, q in zip(h, flow, lift, lift_above)])
-        put(side, at, [HEAD_SCALE * porosity * a + b for a, b in zip(c, moved)])
+        x = carried(get(wx, at, n), get(fx, at, n), c, up, down)
+        y = carried(get(wy, at, n), get(fy, at, n), c, nxt, prv)
+        put(part, at, [a - p + q for a, p, q in zip(get(base, at, n), lift, lift_above)])
+        put(side, at, [HEAD_SCALE * porosity * a + (b + d) for a, b, d in zip(c, x, y)])
         return c_in, lift
 
     one(steps - 1, sweep(0, steps - 1, one, (get(salt, 0, n), zeros(n)), 4), True)
@@ -669,10 +681,10 @@
     steps = rim.shape[0] // 3
     return call(
         weights,
-        [whole(steps)] * 4,
+        [whole(steps)] * 6,
         (rim, high, low),
         "weights",
-        scratch=[pltpu.VMEM(whole(steps), F32), pltpu.VMEM((18, 16, 128), F32)],
+        scratch=[pltpu.VMEM(whole(steps), F32)] * 2 + [pltpu.VMEM((18, 16, 128), F32)],
         micros=4.0,
     )
 
@@ -753,8 +765,8 @@
     leak_left2 = shift(to_high2, "gy", 2)
     then_low, then_high = behind(coast[2:], leak_right, leak_left, leak_right2, leak_left2, rims)
     then = shift(then_low, "gx", -1), shift(then_high, "gx", 1)
-    head, *links = run_weights(rims, *first)
-    ready = run_prepare(rims, *then, head, *links)
+    *links, fx, fy, base = run_weights(rims, *first)
+    ready = run_prepare(rims, *then, *links, fx, fy, base)
     gathered, sum_low, sum_high = call(
         sum_inland, [(16, 768), (8, 768), (8, 768)], (own, leak_right, leak_left, leak_right2, leak_left2), "sum_inland"
     )

time: 75.5 us -> 74.6 us (0.988)
  waiting for transfers between devices: 20 us -> 19.1 us
    ppermute x14, waiting for transfers between devices: 20 us -> 19.1 us  [shift(): lax.ppermute(block, axis, [(i, (i + step) % count) for i in range(count)])]
where the time goes in v4:
time: 74.6 us; the launch traced here: 74.4 us
  Pallas kernels  34.5 us (46%)
  starting transfers between devices  19.9 us (27%)
  waiting for transfers between devices  19.1 us (26%)
  between operations  0.89 us (1%)
    pallas_call x10, Pallas kernels, call(): pl.pallas_call(body, out_shape=shapes, in_specs=[spec(i) for i in range(l...  34.5 us
    ppermute x14, starting transfers between devices, shift(): lax.ppermute(block, axis, [(i, (i + step) % count) for i in range(count)])  19.9 us
    ppermute x14, waiting for transfers between devices, shift(): lax.ppermute(block, axis, [(i, (i + step) % count) for i in range(count)])  19.1 us
  transfers between devices with their start and end apart: 14, of which 6 were waited for; matrix products, arithmetic and copies ran while one was open for 0% of the time, Pallas kernels for 19%

profile of v4, /device:TPU:8, one launch (start us, length us, event | category | flops | bytes accessed | tf_op | source)
XLA Modules:
  0.0 74.4 jit_solution(697274487653075275)
XLA Ops:
  0.6 1.9 %pack_inland.1 = (f32[152,128]{1,0:T(8,128)S(1)}, f32[152,128]{1,0:T(8,128)S(1)}, f32[8,128]{1,0:T(8,128)S(1)}, f32[8,128]{1,0:T(8,128)S(1)}, f32[128,128]{1,0:T...) custom-call(f32[128,128]{1,0:T(8,128)} %refs_0_.1, ...), custom_call_target="tpu_custom_call" | custom-call | bytes 10500000 | tf_op jit(solution)/shard_map/pack_inland/pallas_call | solution.py:37
  2.5 0.4 collective-permute-start
  3.0 2.6 %collective-permute-start.1 = (f32[152,128]{1,0:T(8,128)S(1)}, f32[152,128]{1,0:T(8,128)S(1)}, u32[]{:S(2)}, u32[]{:S(2)}) collective-permute-start(f32[152,128]{1,0:T(8,128)S(1)} %get-tuple-element.61), channel_id=1, source_target_pairs={{0,1},{1,2},{2,3},{3,4},{4,5},{5,6},{6,7},{7,0},{8,9},{9,10},{10,1... | collective-permute-start | bytes 233480 | tf_op jit(solution)/shard_map/ppermute | solution.py:29
  5.5 3.4 %interleave.1 = (f32[6,18,8,128]{3,2,1,0:T(8,128)S(1)}, f32[6,18,8,128]{3,2,1,0:T(8,128)S(1)}, f32[6,18,8,128]{3,2,1,0:T(8,128)S(1)}) custom-call(f32[96,8,128]{2,1,0:T(8,128)S(1)} %get-tuple-element.64.head, f32[96,8,128]{2,1,0:T(8,128)S(1)} %get-tuple-element.65.salt, f32[96,8,128]{2,1,0:T(8,128)S(1)} %get-tuple-element.66.cond), custom_call_target="tpu_custom_call" | custom-call | bytes 14000000 | tf_op jit(solution)/shard_map/interleave/pallas_call | solution.py:37
  8.9 0.0 collective-permute-done.right
  8.9 0.6 collective-permute-done.1.left
  9.6 5.0 %collective-permute-start.2 = (f32[24,128]{1,0:T(8,128)S(1)}, f32[24,128]{1,0:T(8,128)S(1)}, u32[]{:S(2)}, u32[]{:S(2)}) collective-permute-start(f32[24,128]{1,0:T(8,128)S(1)} %get-tuple-element.68), channel_id=1, source_target_pairs={{0,120},{8,0},{16,8},{24,16},{32,24},{40,32},{48,40},{56,48},{64,5... | collective-permute-start | bytes 36872 | tf_op jit(solution)/shard_map/ppermute | solution.py:29
  14.6 0.0 collective-permute-start.3
  14.6 1.5 %pack_coast.1 = (f32[18,18,8,128]{3,2,1,0:T(8,128)S(1)}, f32[6,216,128]{2,1,0:T(8,128)S(1)}, f32[6,216,128]{2,1,0:T(8,128)S(1)}, f32[3,216,128]{2,1,0:T(8,128)S(1)}, f32[3,216,128]{2,1,0:T(8,128)S(1)}) custom-call(f32[6,18,8,128]{3,2,1,0:T(8,128)S(1)} %get-tuple-element.67.after.head, f32[6,18,8,128]{3,2,1,0:T(8,128)S(1)} %get-tuple-element.71.salt, ...), custom_call_target="tpu_custom_call" | custom-call | bytes 10500000 | tf_op jit(solution)/shard_map/pack_coast/pallas_call | solution.py:37
  16.1 0.0 collective-permute-done.2.above.refs_2_
  16.1 5.2 %collective-permute-done.3.below.refs_3_ = f32[24,128]{1,0:T(8,128)S(1)} collective-permute-done((f32[24,128]{1,0:T(8,128)S(1)}, f32[24,128]{1,0:T(8,128)S(1)}, u32[]{:S(2)}, u32[]{:S(2)}) %collective-permute-start.3) | collective-permute-done | bytes 12320 | tf_op jit(solution)/shard_map/ppermute | solution.py:29
  21.3 0.2 collective-permute-start.10
  21.5 0.3 collective-permute-start.11
  21.8 1.4 %surface.1 = (f32[128,128]{1,0:T(8,128)}, f32[32,384]{1,0:T(8,128)S(1)}, f32[32,384]{1,0:T(8,128)S(1)}, f32[16,384]{1,0:T(8,128)S(1)}, f32[16,384]{1,0:T(8,128)S(1)}, /*index=5*/f32[16,768]{1,0:T(8,128)S(1)}) custom-call(f32[128,128]{1,0:T(8,128)S(1)} %get-tuple-element.52.depth, f32[128,128]{1,0:T(8,128)S(1)} %get-tuple-element.53.bed, ...), custom_call_target="tpu_custom_call" | custom-call | bytes 5250000 | tf_op jit(solution)/shard_map/surface/pallas_call | solution.py:37
  23.2 3.1 %collective-permute-start.6 = (f32[16,384]{1,0:T(8,128)S(1)}, f32[16,384]{1,0:T(8,128)S(1)}, u32[]{:S(2)}, u32[]{:S(2)}) collective-permute-start(f32[16,384]{1,0:T(8,128)S(1)} %get-tuple-element.78), channel_id=1, source_target_pairs={{0,6},{1,7},{2,0},{3,1},{4,2},{5,3},{6,4},{7,5},{8,14},{9,15},{10,... | collective-permute-start | bytes 73736 | tf_op jit(solution)/shard_map/ppermute | solution.py:29
  26.3 0.1 collective-permute-start.4
  26.4 2.8 %collective-permute-start.5 = (f32[32,384]{1,0:T(8,128)S(1)}, f32[32,384]{1,0:T(8,128)S(1)}, u32[]{:S(2)}, u32[]{:S(2)}) collective-permute-start(f32[32,384]{1,0:T(8,128)S(1)} %get-tuple-element.77), channel_id=1, source_target_pairs={{0,1},{1,2},{2,3},{3,4},{4,5},{5,6},{6,7},{7,0},{8,9},{9,10},{10,1... | collective-permute-start | bytes 147464 | tf_op jit(solution)/shard_map/ppermute | solution.py:29
  29.2 0.0 collective-permute-done.6.refs_4_.right2
  29.2 0.0 collective-permute-start.7
  29.2 1.6 %open_tile.1.refs_6_.rim = f32[144,24,128]{2,1,0:T(8,128)S(1)} custom-call(f32[18,18,8,128]{3,2,1,0:T(8,128)S(1)} %get-tuple-element.73.full), custom_call_target="tpu_custom_call" | custom-call | bytes 10500000 | tf_op jit(solution)/shard_map/open_tile/pallas_call | solution.py:37
  30.8 3.5 %collective-permute-done.7.refs_5_.left2 = f32[16,384]{1,0:T(8,128)S(1)} collective-permute-done((f32[16,384]{1,0:T(8,128)S(1)}, f32[16,384]{1,0:T(8,128)S(1)}, u32[]{:S(2)}, u32[]{:S(2)}) %collective-permute-start.7) | collective-permute-done | bytes 24608 | tf_op jit(solution)/shard_map/ppermute | solution.py:29
  34.3 4.3 %collective-permute-done.4.refs_2_.right = f32[32,384]{1,0:T(8,128)S(1)} collective-permute-done((f32[32,384]{1,0:T(8,128)S(1)}, f32[32,384]{1,0:T(8,128)S(1)}, u32[]{:S(2)}, u32[]{:S(2)}) %collective-permute-start.4) | collective-permute-done | bytes 49184 | tf_op jit(solution)/shard_map/ppermute | solution.py:29
  38.5 3.6 %collective-permute-done.5.refs_3_.left = f32[32,384]{1,0:T(8,128)S(1)} collective-permute-done((f32[32,384]{1,0:T(8,128)S(1)}, f32[32,384]{1,0:T(8,128)S(1)}, u32[]{:S(2)}, u32[]{:S(2)}) %collective-permute-start.5) | collective-permute-done | bytes 49184 | tf_op jit(solution)/shard_map/ppermute | solution.py:29
  42.1 0.0 collective-permute-start.8
  42.1 0.5 collective-permute-start.9
  42.7 4.9 %collective-permute-start.12 = (f32[8,768]{1,0:T(8,128)S(1)}, f32[8,768]{1,0:T(8,128)S(1)}, u32[]{:S(2)}, u32[]{:S(2)}) collective-permute-start(f32[8,768]{1,0:T(8,128)S(1)} %get-tuple-element.97), channel_id=1, source_target_pairs={{0,120},{8,0},{16,8},{24,16},{32,24},{40,32},{48,40},{56,48},{64,5... | collective-permute-start | bytes 73736 | tf_op jit(solution)/shard_map/ppermute | solution.py:29
  47.6 0.0 collective-permute-done.10.high
  47.6 0.0 collective-permute-start.13
  47.6 0.0 collective-permute-done.11.low
  47.6 3.5 %weights.1 = (f32[48,72,128]{2,1,0:T(8,128)S(1)}, f32[48,72,128]{2,1,0:T(8,128)S(1)}, f32[48,72,128]{2,1,0:T(8,128)S(1)}, f32[48,72,128]{2,1,0:T(8,128)S(1)}, f3...) custom-call(f32[144,24,128]{2,1,0:T(8,128)S(1)} %open_tile.1.refs_6_.rim, ...), custom_call_target="tpu_custom_call" | custom-call | bytes 14000000 | tf_op jit(solution)/shard_map/weights/pallas_call | solution.py:37
  51.1 0.0 collective-permute-done.8.high
  51.2 1.9 %collective-permute-done.9.low = f32[3,216,128]{2,1,0:T(8,128)S(1)} collective-permute-done((f32[3,216,128]{2,1,0:T(8,128)S(1)}, f32[3,216,128]{2,1,0:T(8,128)S(1)}, u32[]{:S(2)}, u32[]{:S(2)}) %collective-permute-start.9) | collective-permute-done | bytes 331808 | tf_op jit(solution)/shard_map/ppermute | solution.py:29
  53.0 2.5 %prepare.1 = (f32[48,72,128]{2,1,0:T(8,128)S(1)}, f32[48,72,128]{2,1,0:T(8,128)S(1)}, f32[48,72,128]{2,1,0:T(8,128)S(1)}) custom-call(f32[144,24,128]{2,1,0:T(8,128)S(1)} %open_tile.1.refs_6_.rim, f32[3,216,128]{2,1,0:T(8,128)S(1)} %collective-permute-done.8.high, f32[3,216,128]{2,1,0:T(8,128)S(1)} %collective-permute-done.9.low, ...), custom_call_target="tpu_custom_call" | custom-call | bytes 14000000 | tf_op jit(solution)/shard_map/prepare/pallas_call | solution.py:37
  55.6 0.0 collective-permute-done.12.leak_high
  55.6 0.0 collective-permute-done.13.leak_low
  55.6 18.7 %aquifer.1 = (f32[96,8,128]{2,1,0:T(8,128)}, f32[96,8,128]{2,1,0:T(8,128)}) custom-call(f32[48,72,128]{2,1,0:T(8,128)S(1)} %get-tuple-element.92.part0, f32[48,72,128]{2,1,0:T(8,128)S(1)} %get-tuple-element.93.side0, f32[48,72,128]{2,1,0:T(8,128)S(1)} %get-tuple-element.94.salt0, f32[48,72,128]{2,1,0:T(8,128)S(1)} %get-tuple-element.86.wx, ...), custom_call_target="tpu_custom_call" | custom-call | bytes 70000000 | tf_op jit(solution)/shard_map/aquifer/pallas_call | solution.py:37
  (4 shorter events, 0.0 us)
Async XLA Ops:
  2.5 6.4 %collective-permute-start = (f32[152,128]{1,0:T(8,128)S(1)}, f32[152,128]{1,0:T(8,128)S(1)}, u32[]{:S(2)}, u32[]{:S(2)}) collective-permute-start(f32[152,128]{1,0:T(8,128)S(1)} %get-tuple-element.60), channel_id=1, source_target_pairs={{0,7},{1,0},{2,1},{3,2},{4,3},{5,4},{6,5},{7,6},{8,15},{9,8},{10,9... | collective-permute-start | bytes 233480 | tf_op jit(solution)/shard_map/ppermute | solution.py:29
  3.0 6.6 %collective-permute-start.1 = (f32[152,128]{1,0:T(8,128)S(1)}, f32[152,128]{1,0:T(8,128)S(1)}, u32[]{:S(2)}, u32[]{:S(2)}) collective-permute-start(f32[152,128]{1,0:T(8,128)S(1)} %get-tuple-element.61), channel_id=1, source_target_pairs={{0,1},{1,2},{2,3},{3,4},{4,5},{5,6},{6,7},{7,0},{8,9},{9,10},{10,1... | collective-permute-start | bytes 233480 | tf_op jit(solution)/shard_map/ppermute | solution.py:29
  9.6 6.5 %collective-permute-start.2 = (f32[24,128]{1,0:T(8,128)S(1)}, f32[24,128]{1,0:T(8,128)S(1)}, u32[]{:S(2)}, u32[]{:S(2)}) collective-permute-start(f32[24,128]{1,0:T(8,128)S(1)} %get-tuple-element.68), channel_id=1, source_target_pairs={{0,120},{8,0},{16,8},{24,16},{32,24},{40,32},{48,40},{56,48},{64,5... | collective-permute-start | bytes 36872 | tf_op jit(solution)/shard_map/ppermute | solution.py:29
  14.6 6.7 %collective-permute-start.3 = (f32[24,128]{1,0:T(8,128)S(1)}, f32[24,128]{1,0:T(8,128)S(1)}, u32[]{:S(2)}, u32[]{:S(2)}) collective-permute-start(f32[24,128]{1,0:T(8,128)S(1)} %get-tuple-element.69), channel_id=1, source_target_pairs={{0,8},{8,16},{16,24},{24,32},{32,40},{40,48},{48,56},{56,64},{64,7... | collective-permute-start | bytes 36872 | tf_op jit(solution)/shard_map/ppermute | solution.py:29
  21.3 26.3 %collective-permute-start.10 = (f32[6,216,128]{2,1,0:T(8,128)S(1)}, f32[6,216,128]{2,1,0:T(8,128)S(1)}, u32[]{:S(2)}, u32[]{:S(2)}) collective-permute-start(f32[6,216,128]{2,1,0:T(8,128)S(1)} %get-tuple-element.84), channel_id=1, source_target_pairs={{0,120},{8,0},{16,8},{24,16},{32,24},{40,32},{48,40},{56,48},{64,5... | collective-permute-start | bytes 1990664 | tf_op jit(solution)/shard_map/ppermute | solution.py:29
  21.5 26.1 %collective-permute-start.11 = (f32[6,216,128]{2,1,0:T(8,128)S(1)}, f32[6,216,128]{2,1,0:T(8,128)S(1)}, u32[]{:S(2)}, u32[]{:S(2)}) collective-permute-start(f32[6,216,128]{2,1,0:T(8,128)S(1)} %get-tuple-element.85), channel_id=1, source_target_pairs={{0,8},{8,16},{16,24},{24,32},{32,40},{40,48},{48,56},{56,64},{64,7... | collective-permute-start | bytes 1990664 | tf_op jit(solution)/shard_map/ppermute | solution.py:29
  23.2 6.0 %collective-permute-start.6 = (f32[16,384]{1,0:T(8,128)S(1)}, f32[16,384]{1,0:T(8,128)S(1)}, u32[]{:S(2)}, u32[]{:S(2)}) collective-permute-start(f32[16,384]{1,0:T(8,128)S(1)} %get-tuple-element.78), channel_id=1, source_target_pairs={{0,6},{1,7},{2,0},{3,1},{4,2},{5,3},{6,4},{7,5},{8,14},{9,15},{10,... | collective-permute-start | bytes 73736 | tf_op jit(solution)/shard_map/ppermute | solution.py:29
  26.3 12.2 %collective-permute-start.4 = (f32[32,384]{1,0:T(8,128)S(1)}, f32[32,384]{1,0:T(8,128)S(1)}, u32[]{:S(2)}, u32[]{:S(2)}) collective-permute-start(f32[32,384]{1,0:T(8,128)S(1)} %get-tuple-element.76), channel_id=1, source_target_pairs={{0,7},{1,0},{2,1},{3,2},{4,3},{5,4},{6,5},{7,6},{8,15},{9,8},{10,9... | collective-permute-start | bytes 147464 | tf_op jit(solution)/shard_map/ppermute | solution.py:29
  26.4 15.8 %collective-permute-start.5 = (f32[32,384]{1,0:T(8,128)S(1)}, f32[32,384]{1,0:T(8,128)S(1)}, u32[]{:S(2)}, u32[]{:S(2)}) collective-permute-start(f32[32,384]{1,0:T(8,128)S(1)} %get-tuple-element.77), channel_id=1, source_target_pairs={{0,1},{1,2},{2,3},{3,4},{4,5},{5,6},{6,7},{7,0},{8,9},{9,10},{10,1... | collective-permute-start | bytes 147464 | tf_op jit(solution)/shard_map/ppermute | solution.py:29
  29.2 5.0 %collective-permute-start.7 = (f32[16,384]{1,0:T(8,128)S(1)}, f32[16,384]{1,0:T(8,128)S(1)}, u32[]{:S(2)}, u32[]{:S(2)}) collective-permute-start(f32[16,384]{1,0:T(8,128)S(1)} %get-tuple-element.79), channel_id=1, source_target_pairs={{0,2},{1,3},{2,4},{3,5},{4,6},{5,7},{6,0},{7,1},{8,10},{9,11},{10,... | collective-permute-start | bytes 73736 | tf_op jit(solution)/shard_map/ppermute | solution.py:29
  42.1 9.0 %collective-permute-start.8 = (f32[3,216,128]{2,1,0:T(8,128)S(1)}, f32[3,216,128]{2,1,0:T(8,128)S(1)}, u32[]{:S(2)}, u32[]{:S(2)}) collective-permute-start(f32[3,216,128]{2,1,0:T(8,128)S(1)} %get-tuple-element.80), channel_id=1, source_target_pairs={{0,120},{8,0},{16,8},{24,16},{32,24},{40,32},{48,40},{56,48},{64,5... | collective-permute-start | bytes 995336 | tf_op jit(solution)/shard_map/ppermute | solution.py:29
  42.1 10.9 %collective-permute-start.9 = (f32[3,216,128]{2,1,0:T(8,128)S(1)}, f32[3,216,128]{2,1,0:T(8,128)S(1)}, u32[]{:S(2)}, u32[]{:S(2)}) collective-permute-start(f32[3,216,128]{2,1,0:T(8,128)S(1)} %get-tuple-element.81), channel_id=1, source_target_pairs={{0,8},{8,16},{16,24},{24,32},{32,40},{40,48},{48,56},{56,64},{64,7... | collective-permute-start | bytes 995336 | tf_op jit(solution)/shard_map/ppermute | solution.py:29
  42.7 12.9 %collective-permute-start.12 = (f32[8,768]{1,0:T(8,128)S(1)}, f32[8,768]{1,0:T(8,128)S(1)}, u32[]{:S(2)}, u32[]{:S(2)}) collective-permute-start(f32[8,768]{1,0:T(8,128)S(1)} %get-tuple-element.97), channel_id=1, source_target_pairs={{0,120},{8,0},{16,8},{24,16},{32,24},{40,32},{48,40},{56,48},{64,5... | collective-permute-start | bytes 73736 | tf_op jit(solution)/shard_map/ppermute | solution.py:29
  47.6 8.0 %collective-permute-start.13 = (f32[8,768]{1,0:T(8,128)S(1)}, f32[8,768]{1,0:T(8,128)S(1)}, u32[]{:S(2)}, u32[]{:S(2)}) collective-permute-start(f32[8,768]{1,0:T(8,128)S(1)} %get-tuple-element.98), channel_id=1, source_target_pairs={{0,8},{8,16},{16,24},{24,32},{32,40},{40,48},{48,56},{56,64},{64,7... | collective-permute-start | bytes 73736 | tf_op jit(solution)/shard_map/ppermute | solution.py:29
